TPU v7x, 512 devices: a whole 4x4x16 slice. The times are simulated.
512 devices in a mesh: blk: 8 (over y, x_lo), rep: 64 (over z, x_hi, core).
Axes of the slice: x: 4 (x_hi: 2, x_lo: 2; x = x_hi * 2 + x_lo), y: 4, z: 16, core: 2. Of those that a mesh axis runs over, the one named last changes fastest.
Arguments:
- rows: float32 [64, 2048, 128], P('rep', 'blk'), may hold values from -6 to 6
- state: float32 [64, 2048], P('rep', 'blk'), may hold values from 1e-09 to 0.001
- bag_ids: int32 [64, 2048, 16], P('rep', 'blk'), may hold values from 0 to 255
- bag_counts: int32 [64, 2048], P('rep', 'blk'), may hold values from 1 to 16
- item_feats: bfloat16 [64, 2048, 128], P('rep', 'blk'), may hold values from -6 to 6
- positives: int32 [64, 2048], P('rep', 'blk'), may hold values from 0 to 2047
- q_w1: bfloat16 [128, 1024], replicated, may hold values from -0.5 to 0.5
- q_w2: bfloat16 [1024, 128], replicated, may hold values from -0.1875 to 0.1875
- i_w1: bfloat16 [128, 1024], replicated, may hold values from -0.5 to 0.5
- i_w2: bfloat16 [1024, 128], replicated, may hold values from -0.1875 to 0.1875
Outputs:
- new_rows: float32 [64, 2048, 128], P('rep', 'blk')
- grad_q1: float32 [128, 1024], replicated
- grad_q2: float32 [1024, 128], replicated
- grad_i1: float32 [128, 1024], replicated
- grad_i2: float32 [1024, 128], replicated
All inputs are finite; a program needn't handle non-finite values.
Results may differ from a plain program's by a relative error of at most 0.003.
Values may be sent and summed in bfloat16 or wider, within the bound.
No kernel may reach another device: no remote copies, remote signals or barrier semaphores. Data moves between devices by JAX's collectives and lax.ppermute only.
A program may use at most 64 MiB of HBM per device.

v0:
```python
import math

import jax
import jax.numpy as jnp
from jax import lax
from jax.sharding import PartitionSpec as P

LOGIT_SCALE = 20.0
LEARNING_RATE = 0.5
NORM_EPS = 1e-06


def contract_lead(left, right, precision=None):
    return lax.dot_general(
        left,
        right,
        (((0,), (0,)), ((), ())),
        precision=precision,
        preferred_element_type=jnp.float32,
    )


def contract_last(left, right):
    return lax.dot_general(
        left, right, (((1,), (1,)), ((), ())), preferred_element_type=jnp.float32
    )


def pooling_matrix(member_ids, member_counts, table_rows):
    columns = lax.broadcasted_iota(jnp.int32, (1, table_rows), 1)
    tally = jnp.zeros((member_ids.shape[0], table_rows), jnp.float32)
    for member in range(member_ids.shape[1]):
        live = (member < member_counts)[:, None]
        tally = tally + jnp.where((member_ids[:, member : member + 1] == columns) & live, 1.0, 0.0)
    return tally / member_counts[:, None].astype(jnp.float32)


def tower(inputs_b, first, second):
    pre = jnp.dot(inputs_b, first, preferred_element_type=jnp.float32)
    hidden = jax.nn.silu(pre).astype(jnp.bfloat16)
    outer = jnp.dot(hidden, second, preferred_element_type=jnp.float32)
    radius = jnp.sqrt(jnp.sum(outer * outer, axis=1, keepdims=True) + NORM_EPS)
    return (pre, hidden, radius, outer / radius)


def tower_back(inputs_b, first, second, pre, hidden, radius, unit, d_unit, with_inputs):
    d_outer = ((d_unit - unit * jnp.sum(unit * d_unit, axis=1, keepdims=True)) / radius).astype(
        jnp.bfloat16
    )
    grad_second = contract_lead(hidden, d_outer)
    d_hidden = contract_last(d_outer, second)
    sigma = jax.nn.sigmoid(pre)
    d_pre = (d_hidden * sigma * (1.0 + pre * (1.0 - sigma))).astype(jnp.bfloat16)
    grad_first = contract_lead(inputs_b, d_pre)
    if with_inputs:
        return (grad_first, grad_second, contract_last(d_pre, first))
    return (grad_first, grad_second, None)


def grad_block(query_part, log_part, target_part, key_part, first_item, norm_c):
    scores = LOGIT_SCALE * contract_last(query_part, key_part)
    columns = first_item + lax.broadcasted_iota(jnp.int32, (1, key_part.shape[0]), 1)
    hits = jnp.where(target_part[:, None] == columns, 1.0, 0.0)
    return ((jnp.exp(scores - log_part[:, None]) - hits) * norm_c).astype(jnp.bfloat16)


def per_device(rows, state, bag_ids, bag_counts, item_feats, positives, q_w1, q_w2, i_w1, i_w2):
    ranks = lax.axis_size("blk")
    table = rows[0]
    q_rows = bag_ids.shape[1]
    norm_c = 1.0 / (q_rows * ranks)
    targets = positives[0]
    pools = pooling_matrix(bag_ids[0], bag_counts[0], table.shape[0])
    pooled_b = jnp.dot(
        pools, table, precision=lax.Precision.HIGHEST, preferred_element_type=jnp.float32
    ).astype(jnp.bfloat16)
    feats = item_feats[0]
    q_pre, q_hidden, q_radius, q_unit = tower(pooled_b, q_w1, q_w2)
    k_pre, k_hidden, k_radius, k_unit = tower(feats, i_w1, i_w2)
    queries = q_unit.astype(jnp.bfloat16)
    keys = k_unit.astype(jnp.bfloat16)
    all_keys = lax.all_gather(keys, "blk", axis=0, tiled=True)
    total_items = all_keys.shape[0]
    width = math.gcd(total_items, 512)
    block_count = total_items // width

    def add_block(block_index, totals):
        key_block = lax.dynamic_slice_in_dim(all_keys, block_index * width, width, 0)
        return totals + jnp.sum(jnp.exp(LOGIT_SCALE * contract_last(queries, key_block)), axis=1)

    totals = lax.fori_loop(0, block_count, add_block, jnp.zeros((q_rows,), jnp.float32))
    log_total = jnp.log(totals)
    width_e = keys.shape[1]

    def back_block(block_index, carry):
        d_queries, key_terms = carry
        first_item = block_index * width
        key_block = lax.dynamic_slice_in_dim(all_keys, first_item, width, 0)
        weights_b = grad_block(queries, log_total, targets, key_block, first_item, norm_c)
        d_queries = d_queries + LOGIT_SCALE * jnp.dot(
            weights_b, key_block, preferred_element_type=jnp.float32
        )
        key_terms = lax.dynamic_update_slice_in_dim(
            key_terms, LOGIT_SCALE * contract_lead(weights_b, queries), first_item, 0
        )
        return (d_queries, key_terms)

    start = (
        jnp.zeros((q_rows, width_e), jnp.float32),
        jnp.zeros((total_items, width_e), jnp.float32),
    )
    d_queries, key_terms = lax.fori_loop(0, block_count, back_block, start)
    d_keys = lax.psum_scatter(key_terms, "blk", scatter_dimension=0, tiled=True)
    gi1, gi2, unused = tower_back(
        feats, i_w1, i_w2, k_pre, k_hidden, k_radius, k_unit, d_keys, False
    )
    gq1, gq2, d_pooled = tower_back(
        pooled_b, q_w1, q_w2, q_pre, q_hidden, q_radius, q_unit, d_queries, True
    )
    sums = lax.psum((gq1, gq2, gi1, gi2), ("blk", "rep"))
    row_grads = contract_lead(pools, d_pooled, lax.Precision.HIGHEST)
    accum = state[0] + jnp.mean(row_grads * row_grads, axis=1)
    updated = table - LEARNING_RATE * row_grads / jnp.sqrt(accum)[:, None]
    return (updated[None], sums[0], sums[1], sums[2], sums[3])


def solution(mesh):
    in_specs = (
        P("rep", "blk", None),
        P("rep", "blk"),
        P("rep", "blk", None),
        P("rep", "blk"),
        P("rep", "blk", None),
        P("rep", "blk"),
        P(),
        P(),
        P(),
        P(),
    )
    out_specs = (P("rep", "blk", None), P(), P(), P(), P())
    return jax.shard_map(
        per_device, mesh=mesh, in_specs=in_specs, out_specs=out_specs, check_vma=False
    )
```

profile of v0, /device:TPU:1, one launch (start us, length us, event | category | flops | bytes accessed | tf_op | source)
XLA Modules:
  0.0 606.0 jit_solution(17159424517446509847)
XLA Ops:
  7.3 0.7 convert_element_type.45
  8.0 0.7 compare_reduce_fusion.15
  9.6 2.5 convolution_convert_fusion
  12.2 1.3 multiply_convert_fusion
  13.5 0.3 multiply_reduce_fusion.3
  13.9 0.4 copy-done.2
  14.4 0.4 copy-done.77
  14.8 0.4 copy-done.78
  15.1 1.4 multiply_convert_fusion.1
  16.5 0.3 multiply_reduce_fusion.4
  16.9 24.6 %all_gather.3 = bf16[2048,128]{0,1:T(8,128)(2,1)S(1)} all-gather(bf16[256,128]{0,1:T(8,128)(2,1)S(1)} %fusion.47), channel_id=1, replica_groups=mesh['blk'=8,'rep'=64] {'blk'}, dimensions={0}, use_global_device_ids=true | all-gather | bytes 589824 | tf_op jit(solution)/shard_map/all_gather | solution.py:82
  41.5 0.3 copy.18
  41.8 1.3 while.30
  41.8 0.3 fusion.89
  42.1 0.3 fusion.89
  42.4 0.3 fusion.89
  42.8 0.3 fusion.89
  43.1 0.6 log.3
  43.7 7.0 %while.31 = (s32[]{:T(128)}, f32[256,128]{1,0:T(8,128)S(1)}, f32[2048,128]{0,1:T(8,128)S(1)}, bf16[2048,128]{1,0:T(8,128)(2,1)S(1)}, bf16[256,128]{1,0:T(8,128)(...) while((s32[]{:T(128)}, f32[256,128]{1,0:T(8,128)S(1)}, ...), condition=%wide.region_6.7_spmd.clone, body=%wide.region_5.6_spmd.clone.sunk | while | flops 101745152 | bytes 2758845 | solution.py:112
  43.8 1.0 fusion.96
  44.8 0.3 fusion.97
  45.5 1.0 fusion.96
  46.5 0.3 fusion.97
  47.3 1.0 fusion.96
  48.3 0.3 fusion.97
  49.0 1.0 fusion.96
  50.0 0.3 fusion.97
  50.3 0.2 convolution_multiply_fusion.7
  50.7 1.0 copy-done.1
  52.0 0.8 copy-done.8
  52.7 1.8 fusion.17
  54.5 1.0 fusion.54
  55.6 1.2 fusion.51
  56.7 49.6 %reduce-scatter.2.cloned.1.call-done = f32[256,128]{0,1:T(8,128)} async-done(((f32[2048,128]{0,1:T(8,128)}), f32[256,128]{0,1:T(8,128)}) %reduce-scatter.2.cloned.1.call-update) | async-done | bytes 131088 | tf_op jit(solution)/shard_map/reduce_scatter | solution.py:113
  106.3 1.0 multiply_reduce_fusion
  107.4 1.1 fusion.52
  108.5 1.6 fusion.20
  110.5 0.3 fusion.53
  111.2 1.7 multiply_reduce_fusion.1
  112.9 0.7 copy-done.14
  113.6 0.8 copy.23
  114.3 479.4 %all-reduce.3.cloned.1.call-done = (f32[128,1024]{1,0:T(8,128)}, f32[1024,128]{1,0:T(8,128)}, f32[128,1024]{0,1:T(8,128)}, f32[1024,128]{1,0:T(8,128)}) async-done(((f32[128,1024]{1,0:T(8,128)}, f32[1024,128]{1,0:T(8,128)}, f32[128,1024]{0,1:T(8,128)}, f32[1024,128]{1,0:T(8,128)}), (f32[128,1024]{1,0:T(8,128)}, f32[1024,128]{1,0:T(8,128)}, f32[128,1024]{0,1:T(8,128)}, ...) | async-done | bytes 2097168 | tf_op jit(solution)/shard_map/psum | solution.py:120
  593.8 2.1 copy.24
  595.9 0.8 copy.54
  596.7 0.4 copy-done.5
  597.1 0.8 copy.55
  597.9 0.4 copy-done.4
  598.3 0.8 copy.56
  (191 shorter events, 3.0 us)
Async XLA Ops:
  7.2 5.0 copy-start
  7.2 1.7 copy-start.13
  7.2 2.4 copy-start.11
  7.2 99.1 %reduce-scatter.2.cloned.1.call-start = ((), (), s32[]{:S(2)}) async-start(), calls=%async_computation.1 | async-start | bytes 1179648 | tf_op jit(solution)/shard_map/reduce_scatter | solution.py:113
  8.0 1.1 copy-start.43
  12.2 1.3 copy-start.7
  13.5 0.8 copy-start.2
  13.8 1.0 copy-start.77
  14.3 0.9 copy-start.78
  15.1 1.4 copy-start.9
  50.7 1.0 copy-start.1
  51.7 542.0 %all-reduce.3.cloned.1.call-start = ((), (), s32[]{:S(2)}) async-start(), calls=%async_computation.2 | async-start | bytes 4194304 | tf_op jit(solution)/shard_map/psum | solution.py:120
  51.8 1.0 copy-start.8
  54.5 1.1 copy-start.3
  106.3 1.0 copy-start.12
  106.3 2.2 copy-start.80
  107.4 1.2 copy-start.10
  107.4 1.2 copy-start.79
  110.2 0.7 copy-start.16
  110.2 0.7 copy-start.18
  110.3 0.7 copy-start.20
  110.3 0.7 copy-start.22
  110.3 0.7 copy-start.24
  110.3 0.7 copy-start.28
  110.3 0.7 copy-start.30
  110.3 0.7 copy-start.32
  110.3 0.7 copy-start.34
  110.3 0.7 copy-start.36
  110.3 0.7 copy-start.38
  110.4 0.7 copy-start.40
  110.4 0.7 copy-start.42
  110.4 0.7 copy-start.44
  110.4 0.7 copy-start.52
  110.4 0.7 copy-start.54
  110.4 0.7 copy-start.56
  110.4 0.7 copy-start.58
  110.5 0.7 copy-start.60
  110.5 0.7 copy-start.62
  110.5 0.7 copy-start.64
  110.5 0.7 copy-start.66
  110.5 0.7 copy-start.68
  110.5 0.7 copy-start.70
  110.5 0.7 copy-start.72
  110.5 0.7 copy-start.74
  112.9 0.7 copy-start.14
  593.8 2.1 copy-start.6
  595.9 1.2 copy-start.5
  597.1 1.2 copy-start.4
  (35 other events, 20.5 us)
Sparse Core Ops, SparseCore 0:
  51.9 54.3 reduce-scatter.1
  112.7 481.0 all-reduce.2
where the time goes:
time: 607 us; the launch traced here: 606 us
  waiting for transfers between devices  529 us (87%)
  blocking collectives  24.6 us (4%)
  matrix products  21.7 us (4%)
  between operations  14.9 us (2%)
  local copies, waits for them, and re-layouts  12.6 us (2%)
    psum x1, waiting for transfers between devices, per_device(): sums = lax.psum((gq1, gq2, gi1, gi2), ('blk', 'rep'))  479 us
    reduce_scatter x1, waiting for transfers between devices, per_device(): d_keys = lax.psum_scatter(key_terms, 'blk', scatter_dimension=0, tiled=True)  49.6 us
    all_gather x1, blocking collectives, per_device(): all_keys = lax.all_gather(keys, 'blk', axis=0, tiled=True)  24.6 us
  transfers between devices with their start and end apart: 2, of which 2 were waited for; matrix products, arithmetic and copies ran while one was open for 1% of the time, Pallas kernels for 0%

commit v1 on v0

v1 whole, which is shorter than its diff:
```python
import functools

import jax
import jax.numpy as jnp
from jax import lax
from jax.experimental import pallas as pl
from jax.experimental.pallas import tpu as pltpu
from jax.sharding import Mesh, PartitionSpec as P

LOGIT_SCALE = 20.0
LEARNING_RATE = 0.5
NORM_EPS = 1e-06

BF16 = jnp.bfloat16
F32 = jnp.float32

CODE_ROWS = 16
LANES = 128


def contract_lead(left, right):
    return lax.dot_general(left, right, (((0,), (0,)), ((), ())), preferred_element_type=F32)


def contract_last(left, right):
    return lax.dot_general(left, right, (((1,), (1,)), ((), ())), preferred_element_type=F32)


def column_of(row):
    return jnp.transpose(jnp.broadcast_to(row, (LANES, row.shape[1])))


def three_pieces(values):
    high = values.astype(BF16)
    rest = values - high.astype(F32)
    middle = rest.astype(BF16)
    low = (rest - middle.astype(F32)).astype(BF16)
    return jnp.concatenate([high, middle, low], axis=1)


def add_pieces(product):
    return (product[:, 2 * LANES :] + product[:, LANES : 2 * LANES]) + product[:, :LANES]


def front_kernel(
    ids_ref, counts_ref, pos_ref, table_ref, feats_ref, qw1_ref, qw2_ref, iw1_ref, iw2_ref,
    payload_ref, pooled_ref, tally_ref, units_ref, radii_ref,
):
    q_rows, members = ids_ref.shape
    table_rows = table_ref.shape[0]
    counts = column_of(counts_ref[...].astype(F32))
    member = lax.broadcasted_iota(jnp.int32, (q_rows, members), 1).astype(F32)
    ids = jnp.where(member < counts[:, :members], ids_ref[...], -1)
    columns = lax.broadcasted_iota(jnp.int32, (q_rows, table_rows), 1)
    tally = jnp.zeros((q_rows, table_rows), F32)
    for m in range(members):
        tally = tally + jnp.where(ids[:, m : m + 1] == columns, 1.0, 0.0)
    tally = tally.astype(BF16)
    tally_ref[...] = tally
    product = jnp.dot(tally, three_pieces(table_ref[...]), preferred_element_type=F32)
    pooled = (add_pieces(product) / counts).astype(BF16)
    pooled_ref[...] = pooled

    def tower(inputs, first_ref, second_ref, slot):
        pre = jnp.dot(inputs, first_ref[...], preferred_element_type=F32)
        hidden = (pre * jax.nn.sigmoid(pre)).astype(BF16)
        outer = jnp.dot(hidden, second_ref[...], preferred_element_type=F32)
        radius = jnp.sqrt(jnp.sum(outer * outer, axis=1, keepdims=True) + NORM_EPS)
        unit = outer / radius
        units_ref[slot] = unit
        radii_ref[slot] = jnp.broadcast_to(radius, unit.shape)
        return unit.astype(BF16)

    keys = tower(feats_ref[...], iw1_ref, iw2_ref, 1)
    queries = tower(pooled, qw1_ref, qw2_ref, 0)
    pos = pos_ref[...]
    digits = jnp.concatenate([pos // LANES, pos % LANES], axis=0).astype(F32)
    spread = jnp.concatenate(
        [digits[:, i * LANES : (i + 1) * LANES] for i in range(q_rows // LANES)]
        + [jnp.zeros((CODE_ROWS - 2 * (q_rows // LANES), LANES), F32)],
        axis=0,
    ).astype(BF16)
    for copy in range(payload_ref.shape[0]):
        payload_ref[copy, :q_rows] = queries
        payload_ref[copy, q_rows : 2 * q_rows] = keys
        payload_ref[copy, 2 * q_rows :] = spread


def middle_kernel(
    where_ref, all_ref, pos_ref, pooled_ref, feats_ref, units_ref, radii_ref,
    qw1_ref, qw2_ref, iw1_ref, iw2_ref,
    keep_ref, send_ref, d_x_ref,
    totals_ref, codes_ref, d_units_ref, grads_ref,
):
    ranks = all_ref.shape[0]
    q_rows = pooled_ref.shape[0]
    i_rows = feats_ref.shape[0]
    blk = where_ref[0]
    core = where_ref[1]
    norm_c = 1.0 / (q_rows * ranks)

    def add_group(s, carry):
        queries = all_ref[s, :q_rows]
        partial = jnp.zeros((8, q_rows), F32)
        for t in range(ranks):
            scores = LOGIT_SCALE * contract_last(all_ref[t, q_rows : q_rows + i_rows], queries)
            partial = partial + jnp.sum(jnp.exp(scores).reshape(i_rows // 8, 8, q_rows), axis=0)
        totals_ref[s] = jnp.broadcast_to(jnp.sum(partial, axis=0, keepdims=True), (8, q_rows))
        digits = all_ref[s, q_rows + i_rows :].astype(F32)
        chunks = q_rows // LANES
        code = jnp.concatenate(
            [digits[2 * i : 2 * i + 1] * LANES + digits[2 * i + 1 : 2 * i + 2] for i in range(chunks)],
            axis=1,
        )
        codes_ref[s] = jnp.broadcast_to(code.astype(jnp.int32), (8, q_rows))
        return carry

    lax.fori_loop(0, ranks, add_group, 0)

    own_keys = all_ref[blk, q_rows : q_rows + i_rows]
    item = blk * i_rows + lax.broadcasted_iota(jnp.int32, (i_rows, q_rows), 0)
    d_keys = jnp.zeros((i_rows, LANES), F32)
    for s in range(ranks):
        queries = all_ref[s, :q_rows]
        shares = jnp.exp(LOGIT_SCALE * contract_last(own_keys, queries)) * (1.0 / totals_ref[s, :1])
        hits = jnp.where(codes_ref[s, :1] == item, 1.0, 0.0)
        weights = ((shares - hits) * norm_c).astype(BF16)
        d_keys = d_keys + jnp.dot(weights, queries, preferred_element_type=F32)
    d_units_ref[1] = LOGIT_SCALE * d_keys

    own_queries = all_ref[blk, :q_rows]
    total = column_of(totals_ref[blk, :1])
    inverse = jnp.concatenate([1.0 / total] * (i_rows // LANES), axis=1)
    target = jnp.concatenate([column_of(pos_ref[...])] * (i_rows // LANES), axis=1)
    place = lax.broadcasted_iota(jnp.int32, (q_rows, i_rows), 1)
    d_queries = jnp.zeros((q_rows, LANES), F32)
    for t in range(ranks):
        keys = all_ref[t, q_rows : q_rows + i_rows]
        shares = jnp.exp(LOGIT_SCALE * contract_last(own_queries, keys)) * inverse
        hits = jnp.where(target == place + t * i_rows, 1.0, 0.0)
        weights = ((shares - hits) * norm_c).astype(BF16)
        d_queries = d_queries + jnp.dot(weights, keys, preferred_element_type=F32)
    d_units_ref[0] = LOGIT_SCALE * d_queries

    def tower_back(inputs, first_ref, second_ref, slot):
        unit = units_ref[slot]
        d_unit = d_units_ref[slot]
        along = jnp.sum(unit * d_unit, axis=1, keepdims=True)
        d_outer = ((d_unit - unit * along) / radii_ref[slot]).astype(BF16)
        pre = jnp.dot(inputs, first_ref[...], preferred_element_type=F32)
        sigma = jax.nn.sigmoid(pre)
        hidden = (pre * sigma).astype(BF16)
        h = hidden.shape[1]
        grads_ref[slot, h:] = contract_lead(hidden, d_outer)
        d_hidden = contract_last(d_outer, second_ref[...])
        d_pre = (d_hidden * sigma * (1.0 + pre * (1.0 - sigma))).astype(BF16)
        first_grad = contract_lead(inputs, d_pre)
        for i in range(h // LANES):
            grads_ref[slot, i * LANES : (i + 1) * LANES] = first_grad[:, i * LANES : (i + 1) * LANES]
        return d_pre

    tower_back(feats_ref[...], iw1_ref, iw2_ref, 1)
    d_pre = tower_back(pooled_ref[...], qw1_ref, qw2_ref, 0)
    d_x_ref[...] = contract_last(d_pre, qw1_ref[...])
    keep_ref[...] = grads_ref[core]
    send_ref[...] = grads_ref[1 - core].astype(BF16)


def rows_kernel(tally_ref, counts_ref, d_x_ref, table_ref, state_ref, new_ref):
    counts = column_of(counts_ref[...].astype(F32))
    pieces = three_pieces(d_x_ref[...] / counts)
    row_grads = add_pieces(contract_lead(tally_ref[...], pieces))
    mean = jnp.mean(row_grads * row_grads, axis=1, keepdims=True)
    acc = column_of(state_ref[...]) + mean
    new_ref[...] = table_ref[...] - LEARNING_RATE * row_grads / jnp.sqrt(acc)


def finish_kernel(where_ref, mine_ref, other_ref, q1_ref, q2_ref, i1_ref, i2_ref):
    core = where_ref[1]
    h = q2_ref.shape[0]

    def write(source_ref, first_ref, second_ref):
        for i in range(h // LANES):
            first_ref[:, i * LANES : (i + 1) * LANES] = source_ref[i * LANES : (i + 1) * LANES].astype(F32)
        second_ref[...] = source_ref[h:].astype(F32)

    @pl.when(core == 0)
    def _():
        write(mine_ref, q1_ref, q2_ref)
        write(other_ref, i1_ref, i2_ref)

    @pl.when(core != 0)
    def _():
        write(other_ref, q1_ref, q2_ref)
        write(mine_ref, i1_ref, i2_ref)


VMEM = pl.BlockSpec(memory_space=pltpu.VMEM)
SMEM = pl.BlockSpec(memory_space=pltpu.SMEM)


def call(kernel, out_shape, operands, scalars=0, scratch=(), flops=0, limit=32):
    return pl.pallas_call(
        kernel,
        out_shape=out_shape,
        in_specs=[SMEM] * scalars + [VMEM] * (len(operands) - scalars),
        out_specs=jax.tree.map(lambda _: VMEM, out_shape),
        scratch_shapes=list(scratch),
        compiler_params=pltpu.CompilerParams(vmem_limit_bytes=limit * 2**20),
        cost_estimate=pl.CostEstimate(flops=flops, bytes_accessed=4 * 2**20, transcendentals=0),
    )(*operands)


def exchange(values, axes):
    return lax.all_to_all(values, axes, 0, 0, tiled=True)


def gather_sum(values, axis):
    copies = jnp.broadcast_to(values, (lax.axis_size(axis),) + values.shape)
    return jnp.sum(exchange(copies, axis), axis=0)


def per_device(rows, state, bag_ids, bag_counts, item_feats, positives, q_w1, q_w2, i_w1, i_w2):
    group = ("y", "xl")
    plane = ("y", "xl", "xh")
    struct = jax.ShapeDtypeStruct
    ranks = lax.axis_size(group)
    chips = lax.axis_size(plane)
    table = rows[0]
    feats = item_feats[0]
    q_rows, e = bag_ids.shape[1], table.shape[1]
    i_rows = feats.shape[0]
    h = q_w2.shape[0]
    where = jnp.stack([lax.axis_index(group), lax.axis_index("c")]).astype(jnp.int32)

    payload, pooled, tally, units, radii = call(
        front_kernel,
        [
            struct((ranks, q_rows + i_rows + CODE_ROWS, e), BF16),
            struct((q_rows, e), BF16),
            struct((q_rows, table.shape[0]), BF16),
            struct((2, q_rows, e), F32),
            struct((2, q_rows, e), F32),
        ],
        [bag_ids[0], bag_counts, positives, table, feats, q_w1, q_w2, i_w1, i_w2],
    )
    everyone = exchange(payload, group)
    keep, send, d_x = call(
        middle_kernel,
        [struct((2 * h, e), F32), struct((2 * h, e), BF16), struct((q_rows, e), F32)],
        [where, everyone, positives, pooled, feats, units, radii, q_w1, q_w2, i_w1, i_w2],
        scalars=1,
        scratch=[
            pltpu.VMEM((ranks, 8, q_rows), F32),
            pltpu.VMEM((ranks, 8, q_rows), jnp.int32),
            pltpu.VMEM((2, q_rows, e), F32),
            pltpu.VMEM((2, 2 * h, e), F32),
        ],
    )
    swap = [(0, 1), (1, 0)]
    received = lax.ppermute(send, "c", swap)
    new_rows = call(
        rows_kernel, struct(table.shape, F32), [tally, bag_counts, d_x, table, state], flops=2**27
    )
    chip_sum = (keep + received.astype(F32)).astype(BF16).reshape(chips, 2 * h // chips, e)
    mine = jnp.sum(exchange(chip_sum, plane).astype(F32), axis=0)
    mine = gather_sum(mine, "zl")
    mine = gather_sum(mine, "zh")
    copies = jnp.broadcast_to(mine.astype(BF16), (chips,) + mine.shape)
    tower = exchange(copies, plane).reshape(2 * h, e)
    other = lax.ppermute(tower, "c", swap)
    sums = call(
        finish_kernel,
        [struct((e, h), F32), struct((h, e), F32), struct((e, h), F32), struct((h, e), F32)],
        [where, tower, other],
        scalars=1,
    )
    return (new_rows[None], *sums)


def solution(mesh):
    blk, rep = mesh.devices.shape
    strided = 4 if rep % 16 == 0 else 1
    parts = (blk // 2, 2, strided, rep // (strided * 4) if rep >= 4 else 1, 2 if rep >= 4 else 1, 2)
    fine = Mesh(mesh.devices.reshape(parts), ("y", "xl", "zh", "zl", "xh", "c"))
    rep_axes = ("zh", "zl", "xh", "c")
    blk_axes = ("y", "xl")
    in_specs = (
        P(rep_axes, blk_axes, None),
        P(rep_axes, blk_axes),
        P(rep_axes, blk_axes, None),
        P(rep_axes, blk_axes),
        P(rep_axes, blk_axes, None),
        P(rep_axes, blk_axes),
        P(),
        P(),
        P(),
        P(),
    )
    out_specs = (P(rep_axes, blk_axes, None), P(), P(), P(), P())
    return jax.shard_map(
        per_device, mesh=fine, in_specs=in_specs, out_specs=out_specs, check_vma=False
    )
```

time: 607 us -> 125 us (0.21)
  waiting for transfers between devices: 529 us -> 13.5 us
  blocking collectives: 24.6 us -> 66.1 us
  starting transfers between devices: 0.08 us -> 21.8 us
  matrix products: 21.7 us -> 0 us
  between operations: 14.9 us -> 0.78 us
  Pallas kernels: 0 us -> 13.7 us
    psum x1 -> x0, waiting for transfers between devices: 479 us -> none  [per_device(): sums = lax.psum((gq1, gq2, gi1, gi2), ('blk', 'rep'))]
    all_to_all x0 -> x4, blocking collectives: none -> 66.1 us  [exchange(): return lax.all_to_all(values, axes, 0, 0, tiled=True)]
    reduce_scatter x1 -> x0, waiting for transfers between devices: 49.6 us -> none  [per_device(): d_keys = lax.psum_scatter(key_terms, 'blk', scatter_dimension=0, tiled=True)]
    all_gather x1 -> x0, blocking collectives: 24.6 us -> none  [per_device(): all_keys = lax.all_gather(keys, 'blk', axis=0, tiled=True)]
    dot_general x28 -> x0, matrix products: 21.7 us -> none  [the longest x9 7.47 us: contract_lead(): lax.dot_general(left, right, (((0,), (0,)), ((), ())), precision=precisio...]
    ppermute x0 -> x2, starting transfers between devices: none -> 15.7 us  [the longest x1 8.45 us: per_device(): other = lax.ppermute(tower, 'c', swap)]
    pallas_call x0 -> x4, Pallas kernels: none -> 13.7 us  [call(): pl.pallas_call(kernel, out_shape=out_shape, in_specs=[SMEM] * scalars + [...]
    all_to_all x0 -> x1, waiting for transfers between devices: none -> 11.7 us  [exchange(): return lax.all_to_all(values, axes, 0, 0, tiled=True)]
  transfers between devices with their start and end apart: 2 -> 3, of which waited for: 2 -> 3; matrix products, arithmetic and copies ran while one was open for 1% -> 0% of each run, Pallas kernels for 0% -> 1%
where the time goes in v1:
time: 125 us; the launch traced here: 124 us
  blocking collectives  66.1 us (53%)
  starting transfers between devices  21.8 us (17%)
  Pallas kernels  13.7 us (11%)
  waiting for transfers between devices  13.5 us (11%)
  local copies, waits for them, and re-layouts  7.88 us (6%)
    all_to_all x4, blocking collectives, exchange(): return lax.all_to_all(values, axes, 0, 0, tiled=True)  66.1 us
    pallas_call x4, Pallas kernels, call(): pl.pallas_call(kernel, out_shape=out_shape, in_specs=[SMEM] * scalars + [...  13.7 us
    all_to_all x1, waiting for transfers between devices, exchange(): return lax.all_to_all(values, axes, 0, 0, tiled=True)  11.7 us
    ppermute x1, starting transfers between devices, per_device(): other = lax.ppermute(tower, 'c', swap)  8.45 us
    unnamed x35, local copies, waits for them, and re-layouts  7.75 us
    ppermute x1, starting transfers between devices, per_device(): received = lax.ppermute(send, 'c', swap)  7.27 us
    all_to_all x1, starting transfers between devices, exchange(): return lax.all_to_all(values, axes, 0, 0, tiled=True)  6.09 us
  transfers between devices with their start and end apart: 3, of which 3 were waited for; matrix products, arithmetic and copies ran while one was open for 0% of the time, Pallas kernels for 1%

profile of v1, /device:TPU:1, one launch (start us, length us, event | category | flops | bytes accessed | tf_op | source)
XLA Modules:
  0.0 124.1 jit_solution(7713594528710565084)
XLA Ops:
  0.6 0.8 copy.16
  1.4 0.0 copy-start
  1.5 0.9 copy-done
  2.4 0.0 copy-start.2
  2.4 0.9 copy-done.2
  3.4 0.0 copy-start.4
  3.4 0.9 copy-done.4
  4.3 0.0 copy-start.6
  4.3 0.9 copy-done.6
  5.3 0.0 copy-start.8
  5.3 0.9 copy-done.8
  6.2 0.0 copy-start.10
  6.2 0.8 copy-done.10
  7.0 0.0 copy-start.12
  7.0 0.7 copy-done.12
  7.7 0.0 copy-start.14
  7.7 0.7 copy-done.14
  8.4 2.8 %shard_map.137 = (bf16[8,528,128]{2,1,0:T(8,128)(2,1)}, bf16[256,128]{1,0:T(8,128)(2,1)S(1)}, bf16[256,256]{1,0:T(8,128)(2,1)S(1)}, f32[2,256,128]{2,1,0:T(8,128)S(1)}, f32[2,256,128]{2,1,0:T(8,128)S(1)}) custom-call(s32[256,16]{1,0:T(8,128)S(1)} %bitcast.10, s32[1,256]{1,0:T(1,128)S(1)} %copy-done.14, s32[1,256]{1,0:T(1,128)S(1)} %copy-done.12, ...), custom_call_target="tpu_custom_call" | custom-call | bytes 4194304 | tf_op jit(solution)/shard_map/pallas_call | solution.py:203
  11.2 0.0 copy-start.1
  11.2 0.0 copy-start.3
  11.2 0.0 copy-start.11
  11.2 0.0 copy-start.13
  11.2 6.1 %all-to-all-start = ((bf16[8,528,128]{2,1,0:T(8,128)(2,1)}), bf16[8,528,128]{2,1,0:T(8,128)(2,1)S(1)}, u32[]{:S(2)}, u32[]{:S(2)}) async-start(bf16[8,528,128]{2,1,0:T(8,128)(2,1)} %get-tuple-element.18), calls=%async_computation | async-start | bytes 2162688 | tf_op jit(solution)/shard_map/all_to_all | solution.py:215
  17.3 0.1 pad_add_fusion.where_ref
  17.4 11.7 %all-to-all-done.all_ref = bf16[8,528,128]{2,1,0:T(8,128)(2,1)S(1)} async-done(((bf16[8,528,128]{2,1,0:T(8,128)(2,1)}), bf16[8,528,128]{2,1,0:T(8,128)(2,1)S(1)}, u32[]{:S(2)}, u32[]{:S(2)}) %all-to-all-start) | async-done | bytes 1081376 | tf_op jit(solution)/shard_map/all_to_all | solution.py:215
  29.0 0.0 copy-done.1
  29.0 0.0 copy-done.3
  29.0 0.0 copy-done.5
  29.0 0.0 copy-done.7
  29.0 0.0 copy-done.11
  29.1 0.0 copy-done.13
  29.1 7.7 %shard_map.138 = (f32[2048,128]{1,0:T(8,128)S(1)}, bf16[2048,128]{1,0:T(8,128)(2,1)S(1)}, f32[256,128]{1,0:T(8,128)S(1)}) custom-call(s32[2]{0:T(128)S(1)} %pad_add_fusion.where_ref, bf16[8,528,128]{2,1,0:T(8,128)(2,1)S(1)} %all-to-all-done.all_ref, s32[1,256]{1,0:T(1,128)S(1)} %copy-done.13, bf16[256,128]{1,0:T(8,128)(2,1)S(1)} %get-tuple-element.19.pooled_ref, ...), custom_call_target="tpu_custom_call" | custom-call | bytes 4194304 | tf_op jit(solution)/shard_map/pallas_call | solution.py:203
  36.8 7.3 %collective-permute-start = (bf16[2048,128]{1,0:T(8,128)(2,1)S(1)}, bf16[2048,128]{1,0:T(8,128)(2,1)S(1)}, u32[]{:S(2)}, u32[]{:S(2)}) collective-permute-start(bf16[2048,128]{1,0:T(8,128)(2,1)S(1)} %get-tuple-element.24), channel_id=1, source_target_pairs={{0,1},{1,0},{2,3},{3,2},{4,5},{5,4},{6,7},{7,6},{8,9},{9,8},{10,11... | collective-permute-start | bytes 1572872 | tf_op jit(solution)/shard_map/ppermute | solution.py:261
  44.1 1.5 %collective-permute-done = bf16[2048,128]{1,0:T(8,128)(2,1)S(1)} collective-permute-done((bf16[2048,128]{1,0:T(8,128)(2,1)S(1)}, bf16[2048,128]{1,0:T(8,128)(2,1)S(1)}, u32[]{:S(2)}, u32[]{:S(2)}) %collective-permute-start) | collective-permute-done | bytes 524320 | tf_op jit(solution)/shard_map/ppermute | solution.py:261
  45.6 0.1 add_convert_fusion
  45.7 13.3 %all_to_all.25 = bf16[16,128,128]{2,1,0:T(8,128)(2,1)S(1)} all-to-all(bf16[16,128,128]{2,1,0:T(8,128)(2,1)S(1)} %bitcast.15), channel_id=1, replica_groups=mesh['y'=4,'xl'=2,'zh'=4,'zl'=4,'xh'=2,'c'=2] {'y','xl','xh'}, dimensions={0} | all-to-all | bytes 1048576 | tf_op jit(solution)/shard_map/all_to_all | solution.py:215
  58.9 0.1 convert_reduce_fusion
  59.0 11.4 %all_to_all.26 = f32[4,128,128]{2,1,0:T(8,128)S(1)} all-to-all(f32[4,128,128]{2,1,0:T(8,128)S(1)} %broadcast_in_dim.13), channel_id=1, replica_groups=mesh['y'=4,'xl'=2,'zh'=4,'zl'=4,'xh'=2,'c'=2] {'zl'}, dimensions={0} | all-to-all | bytes 524288 | tf_op jit(solution)/shard_map/all_to_all | solution.py:215
  70.5 29.1 %all_to_all.27 = f32[4,128,128]{2,1,0:T(8,128)S(1)} all-to-all(f32[4,128,128]{2,1,0:T(8,128)S(1)} %broadcast_in_dim.14), channel_id=1, replica_groups=mesh['y'=4,'xl'=2,'zh'=4,'zl'=4,'xh'=2,'c'=2] {'zh'}, dimensions={0} | all-to-all | bytes 524288 | tf_op jit(solution)/shard_map/all_to_all | solution.py:215
  99.6 0.1 broadcast_in_dim.15
  99.7 12.4 %all_to_all.28 = bf16[16,128,128]{2,1,0:T(8,128)(2,1)S(1)} all-to-all(bf16[16,128,128]{2,1,0:T(8,128)(2,1)S(1)} %broadcast_in_dim.15), channel_id=1, replica_groups=mesh['y'=4,'xl'=2,'zh'=4,'zl'=4,'xh'=2,'c'=2] {'y','xl','xh'}, dimensions={0} | all-to-all | bytes 1048576 | tf_op jit(solution)/shard_map/all_to_all | solution.py:215
  112.1 8.5 %collective-permute-start.1 = (bf16[2048,128]{1,0:T(8,128)(2,1)S(1)}, bf16[2048,128]{1,0:T(8,128)(2,1)S(1)}, u32[]{:S(2)}, u32[]{:S(2)}) collective-permute-start(bf16[2048,128]{1,0:T(8,128)(2,1)S(1)} %bitcast.8), channel_id=1, source_target_pairs={{0,1},{1,0},{2,3},{3,2},{4,5},{5,4},{6,7},{7,6},{8,9},{9,8},{10,11... | collective-permute-start | bytes 1572872 | tf_op jit(solution)/shard_map/ppermute | solution.py:271
  120.6 0.0 copy-done.9
  120.6 0.0 copy-done.15
  120.6 0.0 copy-done.16
  120.6 1.1 shard_map.139
  121.7 0.3 collective-permute-done.1.other_ref
  122.1 2.0 %shard_map.140 = (f32[128,1024]{1,0:T(8,128)}, f32[1024,128]{1,0:T(8,128)}, f32[128,1024]{1,0:T(8,128)}, f32[1024,128]{1,0:T(8,128)}) custom-call(s32[2]{0:T(128)S(1)} %pad_add_fusion.where_ref, bf16[2048,128]{1,0:T(8,128)(2,1)S(1)} %bitcast.9, bf16[2048,128]{1,0:T(8,128)(2,1)S(1)} %collective-permute-done.1.other_ref), custom_call_target="tpu_custom_call" | custom-call | bytes 4194304 | tf_op jit(solution)/shard_map/pallas_call | solution.py:203
  (9 shorter events, 0.1 us)
Async XLA Ops:
  1.4 1.0 copy-start
  2.4 0.9 copy-start.2
  3.4 0.9 copy-start.4
  4.3 0.9 copy-start.6
  5.3 0.9 copy-start.8
  6.2 0.8 copy-start.10
  7.0 0.7 copy-start.12
  7.7 0.7 copy-start.14
  11.2 17.9 %copy-start.1 = (bf16[128,1024]{1,0:T(8,128)(2,1)S(1)}, bf16[128,1024]{1,0:T(8,128)(2,1)}, u32[]{:S(2)}) copy-start(bf16[128,1024]{1,0:T(8,128)(2,1)} %qw1_ref.3) | copy-start | bytes 786436
  11.2 17.9 %copy-start.3 = (bf16[1024,128]{1,0:T(8,128)(2,1)S(1)}, bf16[1024,128]{1,0:T(8,128)(2,1)}, u32[]{:S(2)}) copy-start(bf16[1024,128]{1,0:T(8,128)(2,1)} %qw2_ref.3) | copy-start | bytes 786436
  11.2 17.9 %copy-start.5 = (bf16[128,1024]{1,0:T(8,128)(2,1)S(1)}, bf16[128,1024]{1,0:T(8,128)(2,1)}, u32[]{:S(2)}) copy-start(bf16[128,1024]{1,0:T(8,128)(2,1)} %iw1_ref.3) | copy-start | bytes 786436
  11.2 17.9 %copy-start.7 = (bf16[1024,128]{1,0:T(8,128)(2,1)S(1)}, bf16[1024,128]{1,0:T(8,128)(2,1)}, u32[]{:S(2)}) copy-start(bf16[1024,128]{1,0:T(8,128)(2,1)} %iw2_ref.3) | copy-start | bytes 786436
  11.2 17.9 %copy-start.11 = (bf16[1,256,128]{2,1,0:T(8,128)(2,1)S(1)}, bf16[1,256,128]{2,1,0:T(8,128)(2,1)}, u32[]{:S(2)}) copy-start(bf16[1,256,128]{2,1,0:T(8,128)(2,1)} %param.14) | copy-start | bytes 196612
  11.2 17.9 %copy-start.13 = (s32[1,256]{1,0:T(1,128)S(1)}, s32[1,256]{1,0:T(1,128)}, u32[]{:S(2)}) copy-start(s32[1,256]{1,0:T(1,128)} %pos_ref.3) | copy-start | bytes 3076
  11.2 17.8 %all-to-all-start = ((bf16[8,528,128]{2,1,0:T(8,128)(2,1)}), bf16[8,528,128]{2,1,0:T(8,128)(2,1)S(1)}, u32[]{:S(2)}, u32[]{:S(2)}) async-start(bf16[8,528,128]{2,1,0:T(8,128)(2,1)} %get-tuple-element.18), calls=%async_computation | async-start | bytes 2162688 | tf_op jit(solution)/shard_map/all_to_all | solution.py:215
  36.8 8.8 %collective-permute-start = (bf16[2048,128]{1,0:T(8,128)(2,1)S(1)}, bf16[2048,128]{1,0:T(8,128)(2,1)S(1)}, u32[]{:S(2)}, u32[]{:S(2)}) collective-permute-start(bf16[2048,128]{1,0:T(8,128)(2,1)S(1)} %get-tuple-element.24), channel_id=1, source_target_pairs={{0,1},{1,0},{2,3},{3,2},{4,5},{5,4},{6,7},{7,6},{8,9},{9,8},{10,11... | collective-permute-start | bytes 1572872 | tf_op jit(solution)/shard_map/ppermute | solution.py:261
  99.6 21.0 %copy-start.9 = (f32[1,256,128]{2,1,0:T(8,128)S(1)}, f32[1,256,128]{2,1,0:T(8,128)}, u32[]{:S(2)}) copy-start(f32[1,256,128]{2,1,0:T(8,128)} %param.10) | copy-start | bytes 393220
  99.6 21.0 %copy-start.15 = (s32[1,256]{1,0:T(1,128)S(1)}, s32[1,256]{1,0:T(1,128)}, u32[]{:S(2)}) copy-start(s32[1,256]{1,0:T(1,128)} %counts_ref.3) | copy-start | bytes 3076
  99.6 21.0 %copy-start.16 = (f32[1,256]{1,0:T(1,128)S(1)}, f32[1,256]{1,0:T(1,128)}, u32[]{:S(2)}) copy-start(f32[1,256]{1,0:T(1,128)} %state_ref.1) | copy-start | bytes 3076
  112.1 10.0 %collective-permute-start.1 = (bf16[2048,128]{1,0:T(8,128)(2,1)S(1)}, bf16[2048,128]{1,0:T(8,128)(2,1)S(1)}, u32[]{:S(2)}, u32[]{:S(2)}) collective-permute-start(bf16[2048,128]{1,0:T(8,128)(2,1)S(1)} %bitcast.8), channel_id=1, source_target_pairs={{0,1},{1,0},{2,3},{3,2},{4,5},{5,4},{6,7},{7,6},{8,9},{9,8},{10,11... | collective-permute-start | bytes 1572872 | tf_op jit(solution)/shard_map/ppermute | solution.py:271

commit v2 on v1

--- a/solution.py
+++ b/solution.py
@@ -43,36 +43,52 @@
 
 
 def front_kernel(
-    ids_ref, counts_ref, pos_ref, table_ref, feats_ref, qw1_ref, qw2_ref, iw1_ref, iw2_ref,
+    ids_hbm, counts_hbm, pos_hbm, table_hbm, feats_hbm, qw1_hbm, qw2_hbm, iw1_hbm, iw2_hbm,
     payload_ref, pooled_ref, tally_ref, units_ref, radii_ref,
+    ids_ref, counts_ref, pos_ref, table_ref, feats_ref, qw1_ref, qw2_ref, iw1_ref, iw2_ref, arrived,
 ):
-    q_rows, members = ids_ref.shape
+    sources = (ids_hbm, counts_hbm, table_hbm, qw1_hbm, feats_hbm, iw1_hbm, qw2_hbm, iw2_hbm, pos_hbm)
+    targets = (ids_ref, counts_ref, table_ref, qw1_ref, feats_ref, iw1_ref, qw2_ref, iw2_ref, pos_ref)
+    copies = [
+        pltpu.make_async_copy(source, target, arrived.at[i])
+        for i, (source, target) in enumerate(zip(sources, targets))
+    ]
+    for copy in copies:
+        copy.start()
+
+    members, q_rows = ids_ref.shape
     table_rows = table_ref.shape[0]
-    counts = column_of(counts_ref[...].astype(F32))
-    member = lax.broadcasted_iota(jnp.int32, (q_rows, members), 1).astype(F32)
-    ids = jnp.where(member < counts[:, :members], ids_ref[...], -1)
-    columns = lax.broadcasted_iota(jnp.int32, (q_rows, table_rows), 1)
-    tally = jnp.zeros((q_rows, table_rows), F32)
+    copies[0].wait()
+    copies[1].wait()
+    counts = counts_ref[...]
+    rows = lax.broadcasted_iota(jnp.int32, (table_rows, q_rows), 0)
+    tally = jnp.zeros((table_rows, q_rows), F32)
     for m in range(members):
-        tally = tally + jnp.where(ids[:, m : m + 1] == columns, 1.0, 0.0)
+        live = jnp.where(counts > m, ids_ref[m : m + 1], -1)
+        tally = tally + jnp.where(live == rows, 1.0, 0.0)
     tally = tally.astype(BF16)
     tally_ref[...] = tally
-    product = jnp.dot(tally, three_pieces(table_ref[...]), preferred_element_type=F32)
-    pooled = (add_pieces(product) / counts).astype(BF16)
+    copies[2].wait()
+    product = contract_lead(tally, three_pieces(table_ref[...]))
+    pooled = (add_pieces(product) / column_of(counts.astype(F32))).astype(BF16)
     pooled_ref[...] = pooled
 
-    def tower(inputs, first_ref, second_ref, slot):
-        pre = jnp.dot(inputs, first_ref[...], preferred_element_type=F32)
+    def tower(inputs, first, second, slot):
+        copies[first].wait()
+        pre = jnp.dot(inputs, targets[first][...], preferred_element_type=F32)
         hidden = (pre * jax.nn.sigmoid(pre)).astype(BF16)
-        outer = jnp.dot(hidden, second_ref[...], preferred_element_type=F32)
+        copies[second].wait()
+        outer = jnp.dot(hidden, targets[second][...], preferred_element_type=F32)
         radius = jnp.sqrt(jnp.sum(outer * outer, axis=1, keepdims=True) + NORM_EPS)
         unit = outer / radius
         units_ref[slot] = unit
         radii_ref[slot] = jnp.broadcast_to(radius, unit.shape)
         return unit.astype(BF16)
 
-    keys = tower(feats_ref[...], iw1_ref, iw2_ref, 1)
-    queries = tower(pooled, qw1_ref, qw2_ref, 0)
+    queries = tower(pooled, 3, 6, 0)
+    copies[4].wait()
+    keys = tower(feats_ref[...], 5, 7, 1)
+    copies[8].wait()
     pos = pos_ref[...]
     digits = jnp.concatenate([pos // LANES, pos % LANES], axis=0).astype(F32)
     spread = jnp.concatenate(
@@ -169,45 +185,59 @@
 def rows_kernel(tally_ref, counts_ref, d_x_ref, table_ref, state_ref, new_ref):
     counts = column_of(counts_ref[...].astype(F32))
     pieces = three_pieces(d_x_ref[...] / counts)
-    row_grads = add_pieces(contract_lead(tally_ref[...], pieces))
+    row_grads = add_pieces(jnp.dot(tally_ref[...], pieces, preferred_element_type=F32))
     mean = jnp.mean(row_grads * row_grads, axis=1, keepdims=True)
     acc = column_of(state_ref[...]) + mean
     new_ref[...] = table_ref[...] - LEARNING_RATE * row_grads / jnp.sqrt(acc)
 
 
-def finish_kernel(where_ref, mine_ref, other_ref, q1_ref, q2_ref, i1_ref, i2_ref):
+def finish_kernel(mine, where_ref, source_ref, *refs):
+    q1_ref, q2_ref, i1_ref, i2_ref, first_ref, second_ref, sent = refs[-7:]
     core = where_ref[1]
-    h = q2_ref.shape[0]
-
-    def write(source_ref, first_ref, second_ref):
+    e, h = first_ref.shape
+
+    def copies(first_hbm, second_hbm):
+        return [
+            pltpu.make_async_copy(first_ref, first_hbm, sent.at[0]),
+            pltpu.make_async_copy(second_ref, second_hbm, sent.at[1]),
+        ]
+
+    def write(first_hbm, second_hbm):
+        first, second = copies(first_hbm, second_hbm)
+        second_ref[...] = source_ref[h:].astype(F32)
+        second.start()
         for i in range(h // LANES):
             first_ref[:, i * LANES : (i + 1) * LANES] = source_ref[i * LANES : (i + 1) * LANES].astype(F32)
-        second_ref[...] = source_ref[h:].astype(F32)
-
-    @pl.when(core == 0)
+        first.start()
+        second.wait()
+        first.wait()
+
+    query_tower = (core == 0) if mine else (core != 0)
+
+    @pl.when(query_tower)
     def _():
-        write(mine_ref, q1_ref, q2_ref)
-        write(other_ref, i1_ref, i2_ref)
-
-    @pl.when(core != 0)
+        write(q1_ref, q2_ref)
+
+    @pl.when(jnp.logical_not(query_tower))
     def _():
-        write(other_ref, q1_ref, q2_ref)
-        write(mine_ref, i1_ref, i2_ref)
+        write(i1_ref, i2_ref)
 
 
 VMEM = pl.BlockSpec(memory_space=pltpu.VMEM)
 SMEM = pl.BlockSpec(memory_space=pltpu.SMEM)
-
-
-def call(kernel, out_shape, operands, scalars=0, scratch=(), flops=0, limit=32):
+HBM = pl.BlockSpec(memory_space=pltpu.HBM)
+
+
+def call(kernel, out_shape, operands, in_specs=None, out_specs=None, scratch=(), flops=0, limit=32, aliases=None):
     return pl.pallas_call(
         kernel,
         out_shape=out_shape,
-        in_specs=[SMEM] * scalars + [VMEM] * (len(operands) - scalars),
-        out_specs=jax.tree.map(lambda _: VMEM, out_shape),
+        in_specs=in_specs or [VMEM] * len(operands),
+        out_specs=out_specs or jax.tree.map(lambda _: VMEM, out_shape),
         scratch_shapes=list(scratch),
+        input_output_aliases=aliases or {},
         compiler_params=pltpu.CompilerParams(vmem_limit_bytes=limit * 2**20),
-        cost_estimate=pl.CostEstimate(flops=flops, bytes_accessed=4 * 2**20, transcendentals=0),
+        cost_estimate=pl.CostEstimate(flops=flops, bytes_accessed=2**20, transcendentals=0),
     )(*operands)
 
 
@@ -215,17 +245,12 @@
     return lax.all_to_all(values, axes, 0, 0, tiled=True)
 
 
-def gather_sum(values, axis):
-    copies = jnp.broadcast_to(values, (lax.axis_size(axis),) + values.shape)
-    return jnp.sum(exchange(copies, axis), axis=0)
-
-
 def per_device(rows, state, bag_ids, bag_counts, item_feats, positives, q_w1, q_w2, i_w1, i_w2):
     group = ("y", "xl")
-    plane = ("y", "xl", "xh")
+    block = ("y", "xl", "zp", "xh")
     struct = jax.ShapeDtypeStruct
     ranks = lax.axis_size(group)
-    chips = lax.axis_size(plane)
+    spread = lax.axis_size(block)
     table = rows[0]
     feats = item_feats[0]
     q_rows, e = bag_ids.shape[1], table.shape[1]
@@ -233,23 +258,28 @@
     h = q_w2.shape[0]
     where = jnp.stack([lax.axis_index(group), lax.axis_index("c")]).astype(jnp.int32)
 
+    ids = bag_ids[0].T
+    arguments = [ids, bag_counts, positives, table, feats, q_w1, q_w2, i_w1, i_w2]
     payload, pooled, tally, units, radii = call(
         front_kernel,
         [
             struct((ranks, q_rows + i_rows + CODE_ROWS, e), BF16),
             struct((q_rows, e), BF16),
-            struct((q_rows, table.shape[0]), BF16),
+            struct((table.shape[0], q_rows), BF16),
             struct((2, q_rows, e), F32),
             struct((2, q_rows, e), F32),
         ],
-        [bag_ids[0], bag_counts, positives, table, feats, q_w1, q_w2, i_w1, i_w2],
+        arguments,
+        in_specs=[HBM] * len(arguments),
+        scratch=[pltpu.VMEM(a.shape, a.dtype) for a in arguments]
+        + [pltpu.SemaphoreType.DMA((len(arguments),))],
     )
     everyone = exchange(payload, group)
     keep, send, d_x = call(
         middle_kernel,
         [struct((2 * h, e), F32), struct((2 * h, e), BF16), struct((q_rows, e), F32)],
         [where, everyone, positives, pooled, feats, units, radii, q_w1, q_w2, i_w1, i_w2],
-        scalars=1,
+        in_specs=[SMEM] + [VMEM] * 10,
         scratch=[
             pltpu.VMEM((ranks, 8, q_rows), F32),
             pltpu.VMEM((ranks, 8, q_rows), jnp.int32),
@@ -260,30 +290,44 @@
     swap = [(0, 1), (1, 0)]
     received = lax.ppermute(send, "c", swap)
     new_rows = call(
-        rows_kernel, struct(table.shape, F32), [tally, bag_counts, d_x, table, state], flops=2**27
-    )
-    chip_sum = (keep + received.astype(F32)).astype(BF16).reshape(chips, 2 * h // chips, e)
-    mine = jnp.sum(exchange(chip_sum, plane).astype(F32), axis=0)
-    mine = gather_sum(mine, "zl")
-    mine = gather_sum(mine, "zh")
-    copies = jnp.broadcast_to(mine.astype(BF16), (chips,) + mine.shape)
-    tower = exchange(copies, plane).reshape(2 * h, e)
+        rows_kernel, struct(table.shape, F32), [tally, bag_counts, d_x, table, state], flops=2**30
+    )
+    chip_sum = (keep + received.astype(F32)).astype(BF16).reshape(spread, 2 * h // spread, e)
+    chip_sum, new_rows = lax.optimization_barrier((chip_sum, new_rows))
+    mine = jnp.sum(exchange(chip_sum, block).astype(F32), axis=0).astype(BF16)
+    copies = jnp.broadcast_to(mine, (lax.axis_size("zh"),) + mine.shape)
+    mine = jnp.sum(exchange(copies, "zh").astype(F32), axis=0).astype(BF16)
+    copies = jnp.broadcast_to(mine, (spread,) + mine.shape)
+    tower = exchange(copies, block).reshape(2 * h, e)
     other = lax.ppermute(tower, "c", swap)
+    shapes = [struct((e, h), F32), struct((h, e), F32), struct((e, h), F32), struct((h, e), F32)]
+    buffers = [pltpu.VMEM((e, h), F32), pltpu.VMEM((h, e), F32), pltpu.SemaphoreType.DMA((2,))]
+    own = call(
+        functools.partial(finish_kernel, True),
+        shapes,
+        [where, tower],
+        in_specs=[SMEM, VMEM],
+        out_specs=[HBM] * 4,
+        scratch=buffers,
+        flops=2**30,
+    )
     sums = call(
-        finish_kernel,
-        [struct((e, h), F32), struct((h, e), F32), struct((e, h), F32), struct((h, e), F32)],
-        [where, tower, other],
-        scalars=1,
+        functools.partial(finish_kernel, False),
+        shapes,
+        [where, other, *own],
+        in_specs=[SMEM, VMEM] + [HBM] * 4,
+        out_specs=[HBM] * 4,
+        scratch=buffers,
+        aliases={2: 0, 3: 1, 4: 2, 5: 3},
     )
     return (new_rows[None], *sums)
 
 
 def solution(mesh):
     blk, rep = mesh.devices.shape
-    strided = 4 if rep % 16 == 0 else 1
-    parts = (blk // 2, 2, strided, rep // (strided * 4) if rep >= 4 else 1, 2 if rep >= 4 else 1, 2)
-    fine = Mesh(mesh.devices.reshape(parts), ("y", "xl", "zh", "zl", "xh", "c"))
-    rep_axes = ("zh", "zl", "xh", "c")
+    parts = (blk // 2, 2, max(rep // 8, 1), 2 if rep >= 8 else 1, 2 if rep >= 4 else 1, 2)
+    fine = Mesh(mesh.devices.reshape(parts), ("y", "xl", "zh", "zp", "xh", "c"))
+    rep_axes = ("zh", "zp", "xh", "c")
     blk_axes = ("y", "xl")
     in_specs = (
         P(rep_axes, blk_axes, None),

time: 125 us -> 114 us (0.912)
  blocking collectives: 66.1 us -> 57.6 us
  starting transfers between devices: 21.8 us -> 19.6 us
  Pallas kernels: 13.7 us -> 15.6 us
  waiting for transfers between devices: 13.5 us -> 12 us
    all_to_all x4 -> x3, blocking collectives: 66.1 us -> 57.6 us  [exchange(): return lax.all_to_all(values, axes, 0, 0, tiled=True)]
    ppermute x1, starting transfers between devices: 8.45 us -> 6.21 us  [per_device(): other = lax.ppermute(tower, 'c', swap)]
    pallas_call x4 -> x5, Pallas kernels: 13.7 us -> 15.6 us  [call(): pl.pallas_call(kernel, out_shape=out_shape, in_specs=in_specs or [VMEM] *...]
    unnamed x35 -> x36, local copies, waits for them, and re-layouts: 7.75 us -> 7.67 us
  transfers between devices with their start and end apart: 3 -> 3, of which waited for: 3 -> 2; matrix products, arithmetic and copies ran while one was open for 0% -> 0% of each run, Pallas kernels for 1% -> 2%
where the time goes in v2:
time: 114 us
  blocking collectives  57.6 us (51%)
  starting transfers between devices  19.6 us (17%)
  Pallas kernels  15.6 us (14%)
  waiting for transfers between devices  12 us (11%)
  local copies, waits for them, and re-layouts  7.8 us (7%)
    all_to_all x3, blocking collectives, exchange(): return lax.all_to_all(values, axes, 0, 0, tiled=True)  57.6 us
    pallas_call x5, Pallas kernels, call(): pl.pallas_call(kernel, out_shape=out_shape, in_specs=in_specs or [VMEM] *...  15.6 us
    all_to_all x1, waiting for transfers between devices, exchange(): return lax.all_to_all(values, axes, 0, 0, tiled=True)  11.6 us
    unnamed x36, local copies, waits for them, and re-layouts  7.67 us
    ppermute x1, starting transfers between devices, per_device(): received = lax.ppermute(send, 'c', swap)  7.28 us
    ppermute x1, starting transfers between devices, per_device(): other = lax.ppermute(tower, 'c', swap)  6.21 us
    all_to_all x1, starting transfers between devices, exchange(): return lax.all_to_all(values, axes, 0, 0, tiled=True)  6.07 us
  transfers between devices with their start and end apart: 3, of which 2 were waited for; matrix products, arithmetic and copies ran while one was open for 0% of the time, Pallas kernels for 2%

profile of v2, /device:TPU:1, one launch (start us, length us, event | category | flops | bytes accessed | tf_op | source)
XLA Modules:
  0.0 113.7 jit_solution(7895053586435859828)
XLA Ops:
  0.6 0.0 copy-start
  0.6 0.9 copy-done
  1.6 0.0 copy-start.2
  1.6 0.9 copy-done.2
  2.5 0.9 copy-done.4
  3.5 0.0 copy-start.6
  3.5 0.9 copy-done.6
  4.4 0.8 copy-done.8
  5.3 0.9 copy-done.10
  6.2 0.7 copy-done.12
  6.9 0.7 copy-done.13
  7.6 0.7 copy-done.15
  8.3 3.6 %shard_map.137 = (bf16[8,528,128]{2,1,0:T(8,128)(2,1)}, bf16[256,128]{1,0:T(8,128)(2,1)S(1)}, bf16[256,256]{1,0:T(8,128)(2,1)S(1)}, f32[2,256,128]{2,1,0:T(8,128)S(1)}, f32[2,256,128]{2,1,0:T(8,128)S(1)}) custom-call(s32[16,256]{1,0:T(8,128)S(1)} %bitcast.16, s32[1,256]{1,0:T(1,128)S(1)} %copy-done.15, s32[1,256]{1,0:T(1,128)S(1)} %copy-done.13, ...), custom_call_target="tpu_custom_call" | custom-call | bytes 1048576 | tf_op jit(solution)/shard_map/pallas_call | solution.py:232
  11.9 0.0 copy-start.1
  11.9 0.0 copy-start.3
  11.9 0.0 copy-start.5
  11.9 0.0 copy-start.7
  11.9 0.0 copy-start.9
  11.9 0.0 copy-start.14
  11.9 6.1 %all-to-all-start = ((bf16[8,528,128]{2,1,0:T(8,128)(2,1)}), bf16[8,528,128]{2,1,0:T(8,128)(2,1)S(1)}, u32[]{:S(2)}, u32[]{:S(2)}) async-start(bf16[8,528,128]{2,1,0:T(8,128)(2,1)} %get-tuple-element.23), calls=%async_computation | async-start | bytes 2162688 | tf_op jit(solution)/shard_map/all_to_all | solution.py:245
  18.0 0.1 pad_add_fusion.where_ref
  18.1 11.6 %all-to-all-done.all_ref = bf16[8,528,128]{2,1,0:T(8,128)(2,1)S(1)} async-done(((bf16[8,528,128]{2,1,0:T(8,128)(2,1)}), bf16[8,528,128]{2,1,0:T(8,128)(2,1)S(1)}, u32[]{:S(2)}, u32[]{:S(2)}) %all-to-all-start) | async-done | bytes 1081376 | tf_op jit(solution)/shard_map/all_to_all | solution.py:245
  29.7 0.0 copy-done.1
  29.7 0.0 copy-done.3
  29.7 0.0 copy-done.5
  29.7 0.0 copy-done.7
  29.8 0.0 copy-done.9
  29.8 0.0 copy-done.14
  29.8 0.0 copy-start.11
  29.8 0.0 copy-start.16
  29.8 0.0 copy-start.17
  29.8 7.7 %shard_map.138 = (f32[2048,128]{1,0:T(8,128)S(1)}, bf16[2048,128]{1,0:T(8,128)(2,1)S(1)}, f32[256,128]{1,0:T(8,128)S(1)}) custom-call(s32[2]{0:T(128)S(1)} %pad_add_fusion.where_ref, bf16[8,528,128]{2,1,0:T(8,128)(2,1)S(1)} %all-to-all-done.all_ref, s32[1,256]{1,0:T(1,128)S(1)} %copy-done.14, bf16[256,128]{1,0:T(8,128)(2,1)S(1)} %get-tuple-element.24.pooled_ref, ...), custom_call_target="tpu_custom_call" | custom-call | bytes 1048576 | tf_op jit(solution)/shard_map/pallas_call | solution.py:232
  37.5 7.3 %collective-permute-start = (bf16[2048,128]{1,0:T(8,128)(2,1)S(1)}, bf16[2048,128]{1,0:T(8,128)(2,1)S(1)}, u32[]{:S(2)}, u32[]{:S(2)}) collective-permute-start(bf16[2048,128]{1,0:T(8,128)(2,1)S(1)} %get-tuple-element.28), channel_id=1, source_target_pairs={{0,1},{1,0},{2,3},{3,2},{4,5},{5,4},{6,7},{7,6},{8,9},{9,8},{10,11... | collective-permute-start | bytes 1572872 | tf_op jit(solution)/shard_map/ppermute | solution.py:291
  44.8 0.0 copy-done.11
  44.8 0.0 copy-done.16
  44.8 0.0 copy-done.17
  44.8 1.1 shard_map.139
  46.0 0.4 collective-permute-done
  46.3 0.1 add_convert_fusion
  46.4 16.4 %all_to_all.20 = bf16[32,64,128]{2,1,0:T(8,128)(2,1)S(1)} all-to-all(bf16[32,64,128]{2,1,0:T(8,128)(2,1)S(1)} %bitcast.17), channel_id=1, replica_groups=mesh['y'=4,'xl'=2,'zh'=8,'zp'=2,'xh'=2,'c'=2] {'y','xl','zp','xh'}, dimensions={0} | all-to-all | bytes 1048576 | tf_op jit(solution)/shard_map/all_to_all | solution.py:245
  62.8 0.1 reduce_sum.24
  62.9 27.6 %all_to_all.21 = bf16[8,64,128]{2,1,0:T(8,128)(2,1)S(1)} all-to-all(bf16[8,64,128]{2,1,0:T(8,128)(2,1)S(1)} %broadcast_in_dim.10), channel_id=1, replica_groups=mesh['y'=4,'xl'=2,'zh'=8,'zp'=2,'xh'=2,'c'=2] {'zh'}, dimensions={0} | all-to-all | bytes 262144 | tf_op jit(solution)/shard_map/all_to_all | solution.py:245
  90.5 0.1 broadcast_in_dim.11
  90.6 13.7 %all_to_all.22 = bf16[32,64,128]{2,1,0:T(8,128)(2,1)S(1)} all-to-all(bf16[32,64,128]{2,1,0:T(8,128)(2,1)S(1)} %broadcast_in_dim.11), channel_id=1, replica_groups=mesh['y'=4,'xl'=2,'zh'=8,'zp'=2,'xh'=2,'c'=2] {'y','xl','zp','xh'}, dimensions={0} | all-to-all | bytes 1048576 | tf_op jit(solution)/shard_map/all_to_all | solution.py:245
  104.3 6.2 %collective-permute-start.1 = (bf16[2048,128]{1,0:T(8,128)(2,1)S(1)}, bf16[2048,128]{1,0:T(8,128)(2,1)S(1)}, u32[]{:S(2)}, u32[]{:S(2)}) collective-permute-start(bf16[2048,128]{1,0:T(8,128)(2,1)S(1)} %bitcast.10), channel_id=1, source_target_pairs={{0,1},{1,0},{2,3},{3,2},{4,5},{5,4},{6,7},{7,6},{8,9},{9,8},{10,11... | collective-permute-start | bytes 1572872 | tf_op jit(solution)/shard_map/ppermute | solution.py:302
  110.5 1.6 %shard_map.140 = (f32[128,1024]{1,0:T(8,128)}, f32[1024,128]{1,0:T(8,128)}, f32[128,1024]{1,0:T(8,128)}, f32[1024,128]{1,0:T(8,128)}) custom-call(s32[2]{0:T(128)S(1)} %pad_add_fusion.where_ref, bf16[2048,128]{1,0:T(8,128)(2,1)S(1)} %bitcast.11), custom_call_target="tpu_custom_call" | custom-call | flops 1073741824 | bytes 1048576 | tf_op jit(solution)/shard_map/pallas_call | solution.py:232
  112.1 0.0 collective-permute-done.1.source_ref
  112.1 1.6 %shard_map.141 = (f32[128,1024]{1,0:T(8,128)}, f32[1024,128]{1,0:T(8,128)}, f32[128,1024]{1,0:T(8,128)}, f32[1024,128]{1,0:T(8,128)}) custom-call(s32[2]{0:T(128)S(1)} %pad_add_fusion.where_ref, bf16[2048,128]{1,0:T(8,128)(2,1)S(1)} %collective-permute-done.1.source_ref, ...), custom_call_target="tpu_custom_call", output_to_operand_aliasing={{0}: (2, {}), {1}: (3, {}), {2}: (4, {}), {3}: (5, {})} | custom-call | bytes 1048576 | tf_op jit(solution)/shard_map/pallas_call | solution.py:232
  (8 shorter events, 0.1 us)
Async XLA Ops:
  0.6 1.0 copy-start
  1.6 0.9 copy-start.2
  2.5 0.9 copy-start.4
  3.5 0.9 copy-start.6
  4.4 0.8 copy-start.8
  5.3 0.9 copy-start.10
  6.2 0.7 copy-start.12
  6.9 0.7 copy-start.13
  7.6 0.7 copy-start.15
  11.9 17.9 %copy-start.1 = (bf16[128,1024]{1,0:T(8,128)(2,1)S(1)}, bf16[128,1024]{1,0:T(8,128)(2,1)}, u32[]{:S(2)}) copy-start(bf16[128,1024]{1,0:T(8,128)(2,1)} %qw1_ref.1) | copy-start | bytes 786436
  11.9 17.9 %copy-start.3 = (bf16[1024,128]{1,0:T(8,128)(2,1)S(1)}, bf16[1024,128]{1,0:T(8,128)(2,1)}, u32[]{:S(2)}) copy-start(bf16[1024,128]{1,0:T(8,128)(2,1)} %qw2_ref.1) | copy-start | bytes 786436
  11.9 17.8 %copy-start.5 = (bf16[128,1024]{1,0:T(8,128)(2,1)S(1)}, bf16[128,1024]{1,0:T(8,128)(2,1)}, u32[]{:S(2)}) copy-start(bf16[128,1024]{1,0:T(8,128)(2,1)} %iw1_ref.1) | copy-start | bytes 786436
  11.9 17.8 %copy-start.7 = (bf16[1024,128]{1,0:T(8,128)(2,1)S(1)}, bf16[1024,128]{1,0:T(8,128)(2,1)}, u32[]{:S(2)}) copy-start(bf16[1024,128]{1,0:T(8,128)(2,1)} %iw2_ref.1) | copy-start | bytes 786436
  11.9 17.8 %copy-start.9 = (bf16[1,256,128]{2,1,0:T(8,128)(2,1)S(1)}, bf16[1,256,128]{2,1,0:T(8,128)(2,1)}, u32[]{:S(2)}) copy-start(bf16[1,256,128]{2,1,0:T(8,128)(2,1)} %param.14) | copy-start | bytes 196612
  11.9 17.8 %copy-start.14 = (s32[1,256]{1,0:T(1,128)S(1)}, s32[1,256]{1,0:T(1,128)}, u32[]{:S(2)}) copy-start(s32[1,256]{1,0:T(1,128)} %pos_ref.1) | copy-start | bytes 3076
  11.9 17.8 %all-to-all-start = ((bf16[8,528,128]{2,1,0:T(8,128)(2,1)}), bf16[8,528,128]{2,1,0:T(8,128)(2,1)S(1)}, u32[]{:S(2)}, u32[]{:S(2)}) async-start(bf16[8,528,128]{2,1,0:T(8,128)(2,1)} %get-tuple-element.23), calls=%async_computation | async-start | bytes 2162688 | tf_op jit(solution)/shard_map/all_to_all | solution.py:245
  29.8 15.0 %copy-start.11 = (f32[1,256,128]{2,1,0:T(8,128)S(1)}, f32[1,256,128]{2,1,0:T(8,128)}, u32[]{:S(2)}) copy-start(f32[1,256,128]{2,1,0:T(8,128)} %param.10) | copy-start | bytes 393220
  29.8 15.0 %copy-start.16 = (s32[1,256]{1,0:T(1,128)S(1)}, s32[1,256]{1,0:T(1,128)}, u32[]{:S(2)}) copy-start(s32[1,256]{1,0:T(1,128)} %counts_ref.1) | copy-start | bytes 3076
  29.8 15.0 %copy-start.17 = (f32[1,256]{1,0:T(1,128)S(1)}, f32[1,256]{1,0:T(1,128)}, u32[]{:S(2)}) copy-start(f32[1,256]{1,0:T(1,128)} %state_ref.1) | copy-start | bytes 3076
  37.5 8.8 %collective-permute-start = (bf16[2048,128]{1,0:T(8,128)(2,1)S(1)}, bf16[2048,128]{1,0:T(8,128)(2,1)S(1)}, u32[]{:S(2)}, u32[]{:S(2)}) collective-permute-start(bf16[2048,128]{1,0:T(8,128)(2,1)S(1)} %get-tuple-element.28), channel_id=1, source_target_pairs={{0,1},{1,0},{2,3},{3,2},{4,5},{5,4},{6,7},{7,6},{8,9},{9,8},{10,11... | collective-permute-start | bytes 1572872 | tf_op jit(solution)/shard_map/ppermute | solution.py:291
  104.3 7.8 %collective-permute-start.1 = (bf16[2048,128]{1,0:T(8,128)(2,1)S(1)}, bf16[2048,128]{1,0:T(8,128)(2,1)S(1)}, u32[]{:S(2)}, u32[]{:S(2)}) collective-permute-start(bf16[2048,128]{1,0:T(8,128)(2,1)S(1)} %bitcast.10), channel_id=1, source_target_pairs={{0,1},{1,0},{2,3},{3,2},{4,5},{5,4},{6,7},{7,6},{8,9},{9,8},{10,11... | collective-permute-start | bytes 1572872 | tf_op jit(solution)/shard_map/ppermute | solution.py:302

commit v3 on v2

--- a/solution.py
+++ b/solution.py
@@ -8,6 +8,7 @@
 from jax.sharding import Mesh, PartitionSpec as P
 
 LOGIT_SCALE = 20.0
+EXP_SCALE = 28.853900817779268
 LEARNING_RATE = 0.5
 NORM_EPS = 1e-06
 
@@ -117,10 +118,12 @@
 
     def add_group(s, carry):
         queries = all_ref[s, :q_rows]
-        partial = jnp.zeros((8, q_rows), F32)
-        for t in range(ranks):
-            scores = LOGIT_SCALE * contract_last(all_ref[t, q_rows : q_rows + i_rows], queries)
-            partial = partial + jnp.sum(jnp.exp(scores).reshape(i_rows // 8, 8, q_rows), axis=0)
+
+        def add_items(t, partial):
+            scores = EXP_SCALE * contract_last(all_ref[t, q_rows : q_rows + i_rows], queries)
+            return partial + jnp.sum(jnp.exp2(scores).reshape(i_rows // 8, 8, q_rows), axis=0)
+
+        partial = lax.fori_loop(0, ranks, add_items, jnp.zeros((8, q_rows), F32), unroll=True)
         totals_ref[s] = jnp.broadcast_to(jnp.sum(partial, axis=0, keepdims=True), (8, q_rows))
         digits = all_ref[s, q_rows + i_rows :].astype(F32)
         chunks = q_rows // LANES
@@ -131,52 +134,58 @@
         codes_ref[s] = jnp.broadcast_to(code.astype(jnp.int32), (8, q_rows))
         return carry
 
-    lax.fori_loop(0, ranks, add_group, 0)
+    lax.fori_loop(0, ranks, add_group, 0, unroll=True)
 
     own_keys = all_ref[blk, q_rows : q_rows + i_rows]
-    item = blk * i_rows + lax.broadcasted_iota(jnp.int32, (i_rows, q_rows), 0)
+
+    def add_queries(s, d_keys):
+        queries = all_ref[s, :q_rows]
+        shares = jnp.exp2(EXP_SCALE * contract_last(own_keys, queries)) * (norm_c / totals_ref[s, :1])
+        item = blk * i_rows + lax.broadcasted_iota(jnp.int32, (i_rows, q_rows), 0)
+        weights = (shares - jnp.where(codes_ref[s, :1] == item, norm_c, 0.0)).astype(BF16)
+        return d_keys + jnp.dot(weights, queries, preferred_element_type=F32)
+
+
+    own_queries = all_ref[blk, :q_rows]
+    inverse = column_of(norm_c / totals_ref[blk, :1])
+    inverse = jnp.concatenate([inverse] * (i_rows // LANES), axis=1)
+    target = jnp.concatenate([column_of(pos_ref[...])] * (i_rows // LANES), axis=1)
+    target = target - lax.broadcasted_iota(jnp.int32, (q_rows, i_rows), 1)
+
+    def add_keys(t, d_queries):
+        keys = all_ref[t, q_rows : q_rows + i_rows]
+        shares = jnp.exp2(EXP_SCALE * contract_last(own_queries, keys)) * inverse
+        weights = (shares - jnp.where(target == t * i_rows, norm_c, 0.0)).astype(BF16)
+        return d_queries + jnp.dot(weights, keys, preferred_element_type=F32)
+
     d_keys = jnp.zeros((i_rows, LANES), F32)
-    for s in range(ranks):
-        queries = all_ref[s, :q_rows]
-        shares = jnp.exp(LOGIT_SCALE * contract_last(own_keys, queries)) * (1.0 / totals_ref[s, :1])
-        hits = jnp.where(codes_ref[s, :1] == item, 1.0, 0.0)
-        weights = ((shares - hits) * norm_c).astype(BF16)
-        d_keys = d_keys + jnp.dot(weights, queries, preferred_element_type=F32)
+    d_queries = jnp.zeros((q_rows, LANES), F32)
+    for r in range(ranks):
+        d_keys = add_queries(r, d_keys)
+        d_queries = add_keys(r, d_queries)
     d_units_ref[1] = LOGIT_SCALE * d_keys
-
-    own_queries = all_ref[blk, :q_rows]
-    total = column_of(totals_ref[blk, :1])
-    inverse = jnp.concatenate([1.0 / total] * (i_rows // LANES), axis=1)
-    target = jnp.concatenate([column_of(pos_ref[...])] * (i_rows // LANES), axis=1)
-    place = lax.broadcasted_iota(jnp.int32, (q_rows, i_rows), 1)
-    d_queries = jnp.zeros((q_rows, LANES), F32)
-    for t in range(ranks):
-        keys = all_ref[t, q_rows : q_rows + i_rows]
-        shares = jnp.exp(LOGIT_SCALE * contract_last(own_queries, keys)) * inverse
-        hits = jnp.where(target == place + t * i_rows, 1.0, 0.0)
-        weights = ((shares - hits) * norm_c).astype(BF16)
-        d_queries = d_queries + jnp.dot(weights, keys, preferred_element_type=F32)
     d_units_ref[0] = LOGIT_SCALE * d_queries
 
-    def tower_back(inputs, first_ref, second_ref, slot):
+    def tower_back(inputs_ref, first_ref, second_ref, slot):
         unit = units_ref[slot]
         d_unit = d_units_ref[slot]
         along = jnp.sum(unit * d_unit, axis=1, keepdims=True)
         d_outer = ((d_unit - unit * along) / radii_ref[slot]).astype(BF16)
+        inputs = inputs_ref[...]
+        h = second_ref.shape[0]
         pre = jnp.dot(inputs, first_ref[...], preferred_element_type=F32)
         sigma = jax.nn.sigmoid(pre)
         hidden = (pre * sigma).astype(BF16)
-        h = hidden.shape[1]
         grads_ref[slot, h:] = contract_lead(hidden, d_outer)
         d_hidden = contract_last(d_outer, second_ref[...])
         d_pre = (d_hidden * sigma * (1.0 + pre * (1.0 - sigma))).astype(BF16)
         first_grad = contract_lead(inputs, d_pre)
-        for i in range(h // LANES):
-            grads_ref[slot, i * LANES : (i + 1) * LANES] = first_grad[:, i * LANES : (i + 1) * LANES]
+        for j in range(h // LANES):
+            grads_ref[slot, j * LANES : (j + 1) * LANES] = first_grad[:, j * LANES : (j + 1) * LANES]
         return d_pre
 
-    tower_back(feats_ref[...], iw1_ref, iw2_ref, 1)
-    d_pre = tower_back(pooled_ref[...], qw1_ref, qw2_ref, 0)
+    tower_back(feats_ref, iw1_ref, iw2_ref, 1)
+    d_pre = tower_back(pooled_ref, qw1_ref, qw2_ref, 0)
     d_x_ref[...] = contract_last(d_pre, qw1_ref[...])
     keep_ref[...] = grads_ref[core]
     send_ref[...] = grads_ref[1 - core].astype(BF16)
@@ -273,6 +282,7 @@
         in_specs=[HBM] * len(arguments),
         scratch=[pltpu.VMEM(a.shape, a.dtype) for a in arguments]
         + [pltpu.SemaphoreType.DMA((len(arguments),))],
+        limit=60,
     )
     everyone = exchange(payload, group)
     keep, send, d_x = call(

time: 114 us -> 105 us (0.921)
  local copies, waits for them, and re-layouts: 7.8 us -> 0.21 us
    unnamed x36 -> x26, local copies, waits for them, and re-layouts: 7.67 us -> 0.08 us
  transfers between devices with their start and end apart: 3 -> 3, of which waited for: 2 -> 2; matrix products, arithmetic and copies ran while one was open for 0% -> 0% of each run, Pallas kernels for 2% -> 3%
where the time goes in v3:
time: 105 us
  blocking collectives  57.6 us (55%)
  starting transfers between devices  19.6 us (19%)
  Pallas kernels  14.5 us (14%)
  waiting for transfers between devices  12 us (11%)
    all_to_all x3, blocking collectives, exchange(): return lax.all_to_all(values, axes, 0, 0, tiled=True)  57.6 us
    pallas_call x5, Pallas kernels, call(): pl.pallas_call(kernel, out_shape=out_shape, in_specs=in_specs or [VMEM] *...  14.5 us
    all_to_all x1, waiting for transfers between devices, exchange(): return lax.all_to_all(values, axes, 0, 0, tiled=True)  11.7 us
    ppermute x1, starting transfers between devices, per_device(): received = lax.ppermute(send, 'c', swap)  7.26 us
    ppermute x1, starting transfers between devices, per_device(): other = lax.ppermute(tower, 'c', swap)  6.21 us
    all_to_all x1, starting transfers between devices, exchange(): return lax.all_to_all(values, axes, 0, 0, tiled=True)  6.09 us
  transfers between devices with their start and end apart: 3, of which 2 were waited for; matrix products, arithmetic and copies ran while one was open for 0% of the time, Pallas kernels for 3%

profile of v3, /device:TPU:1, one launch (start us, length us, event | category | flops | bytes accessed | tf_op | source)
XLA Modules:
  0.0 105.0 jit_solution(1059542349203222539)
XLA Ops:
  0.6 4.1 %shard_map.137 = (bf16[8,528,128]{2,1,0:T(8,128)(2,1)}, bf16[256,128]{1,0:T(8,128)(2,1)}, bf16[256,256]{1,0:T(8,128)(2,1)}, f32[2,256,128]{2,1,0:T(8,128)}, f32[2,256,128]{2,1,0:T(8,128)}) custom-call(s32[16,256]{1,0:T(8,128)} %bitcast.17, s32[1,256]{1,0:T(1,128)} %counts_ref.1, s32[1,256]{1,0:T(1,128)} %pos_ref.1, f32[256,128]{1,0:T(8,128)} %bitcast.14, ...), custom_call_target="tpu_custom_call" | custom-call | bytes 1048576 | tf_op jit(solution)/shard_map/pallas_call | solution.py:241
  4.8 0.0 copy-start
  4.8 0.0 copy-start.1
  4.8 0.0 copy-start.2
  4.8 0.0 copy-start.3
  4.8 0.0 copy-start.4
  4.8 0.0 copy-start.5
  4.9 0.0 copy-start.6
  4.9 0.0 copy-start.8
  4.9 0.0 copy-start.9
  4.9 6.1 %all-to-all-start = ((bf16[8,528,128]{2,1,0:T(8,128)(2,1)}), bf16[8,528,128]{2,1,0:T(8,128)(2,1)S(1)}, u32[]{:S(2)}, u32[]{:S(2)}) async-start(bf16[8,528,128]{2,1,0:T(8,128)(2,1)} %get-tuple-element.23), calls=%async_computation | async-start | bytes 2162688 | tf_op jit(solution)/shard_map/all_to_all | solution.py:254
  11.0 0.1 pad_add_fusion.where_ref
  11.1 11.7 %all-to-all-done.all_ref = bf16[8,528,128]{2,1,0:T(8,128)(2,1)S(1)} async-done(((bf16[8,528,128]{2,1,0:T(8,128)(2,1)}), bf16[8,528,128]{2,1,0:T(8,128)(2,1)S(1)}, u32[]{:S(2)}, u32[]{:S(2)}) %all-to-all-start) | async-done | bytes 1081376 | tf_op jit(solution)/shard_map/all_to_all | solution.py:254
  22.7 0.0 copy-done
  22.7 0.0 copy-done.1
  22.7 0.0 copy-done.2
  22.7 0.0 copy-done.3
  22.7 0.0 copy-done.4
  22.7 0.0 copy-done.5
  22.8 0.0 copy-done.6
  22.8 0.0 copy-done.8
  22.8 0.0 copy-done.9
  22.8 0.0 copy-start.7
  22.8 0.0 copy-start.10
  22.8 0.0 copy-start.11
  22.8 0.0 copy-start.12
  22.8 6.1 %shard_map.138 = (f32[2048,128]{1,0:T(8,128)S(1)}, bf16[2048,128]{1,0:T(8,128)(2,1)S(1)}, f32[256,128]{1,0:T(8,128)S(1)}) custom-call(s32[2]{0:T(128)S(1)} %pad_add_fusion.where_ref, bf16[8,528,128]{2,1,0:T(8,128)(2,1)S(1)} %all-to-all-done.all_ref, s32[1,256]{1,0:T(1,128)S(1)} %copy-done.9, bf16[256,128]{1,0:T(8,128)(2,1)S(1)} %copy-done.8, ...), custom_call_target="tpu_custom_call" | custom-call | bytes 1048576 | tf_op jit(solution)/shard_map/pallas_call | solution.py:241
  28.9 7.3 %collective-permute-start = (bf16[2048,128]{1,0:T(8,128)(2,1)S(1)}, bf16[2048,128]{1,0:T(8,128)(2,1)S(1)}, u32[]{:S(2)}, u32[]{:S(2)}) collective-permute-start(bf16[2048,128]{1,0:T(8,128)(2,1)S(1)} %get-tuple-element.28), channel_id=1, source_target_pairs={{0,1},{1,0},{2,3},{3,2},{4,5},{5,4},{6,7},{7,6},{8,9},{9,8},{10,11... | collective-permute-start | bytes 1572872 | tf_op jit(solution)/shard_map/ppermute | solution.py:301
  36.2 0.0 copy-done.7
  36.2 0.0 copy-done.10
  36.2 0.0 copy-done.11
  36.2 0.0 copy-done.12
  36.2 1.1 %shard_map.139 = f32[256,128]{1,0:T(8,128)} custom-call(bf16[256,256]{1,0:T(8,128)(2,1)S(1)} %copy-done.11, s32[1,256]{1,0:T(1,128)S(1)} %copy-done.10, f32[256,128]{1,0:T(8,128)S(1)} %get-tuple-element.30.d_x_ref, f32[256,128]{1,0:T(8,128)S(1)} %bitcast.15, f32[1,256]{1,0:T(1,128)S(1)} %copy-done.12), custom_call_target="tpu_custom_call" | custom-call | flops 1073741824 | bytes 1048576 | tf_op jit(solution)/shard_map/pallas_call | solution.py:241
  37.4 0.3 collective-permute-done
  37.7 0.1 add_convert_fusion
  37.8 16.4 %all_to_all.20 = bf16[32,64,128]{2,1,0:T(8,128)(2,1)S(1)} all-to-all(bf16[32,64,128]{2,1,0:T(8,128)(2,1)S(1)} %bitcast.16), channel_id=1, replica_groups=mesh['y'=4,'xl'=2,'zh'=8,'zp'=2,'xh'=2,'c'=2] {'y','xl','zp','xh'}, dimensions={0} | all-to-all | bytes 1048576 | tf_op jit(solution)/shard_map/all_to_all | solution.py:254
  54.2 0.1 reduce_sum.24
  54.3 27.6 %all_to_all.21 = bf16[8,64,128]{2,1,0:T(8,128)(2,1)S(1)} all-to-all(bf16[8,64,128]{2,1,0:T(8,128)(2,1)S(1)} %broadcast_in_dim.10), channel_id=1, replica_groups=mesh['y'=4,'xl'=2,'zh'=8,'zp'=2,'xh'=2,'c'=2] {'zh'}, dimensions={0} | all-to-all | bytes 262144 | tf_op jit(solution)/shard_map/all_to_all | solution.py:254
  81.9 0.1 broadcast_in_dim.11
  82.0 13.7 %all_to_all.22 = bf16[32,64,128]{2,1,0:T(8,128)(2,1)S(1)} all-to-all(bf16[32,64,128]{2,1,0:T(8,128)(2,1)S(1)} %broadcast_in_dim.11), channel_id=1, replica_groups=mesh['y'=4,'xl'=2,'zh'=8,'zp'=2,'xh'=2,'c'=2] {'y','xl','zp','xh'}, dimensions={0} | all-to-all | bytes 1048576 | tf_op jit(solution)/shard_map/all_to_all | solution.py:254
  95.7 6.2 %collective-permute-start.1 = (bf16[2048,128]{1,0:T(8,128)(2,1)S(1)}, bf16[2048,128]{1,0:T(8,128)(2,1)S(1)}, u32[]{:S(2)}, u32[]{:S(2)}) collective-permute-start(bf16[2048,128]{1,0:T(8,128)(2,1)S(1)} %bitcast.10), channel_id=1, source_target_pairs={{0,1},{1,0},{2,3},{3,2},{4,5},{5,4},{6,7},{7,6},{8,9},{9,8},{10,11... | collective-permute-start | bytes 1572872 | tf_op jit(solution)/shard_map/ppermute | solution.py:312
  101.9 1.6 %shard_map.140 = (f32[128,1024]{1,0:T(8,128)}, f32[1024,128]{1,0:T(8,128)}, f32[128,1024]{1,0:T(8,128)}, f32[1024,128]{1,0:T(8,128)}) custom-call(s32[2]{0:T(128)S(1)} %pad_add_fusion.where_ref, bf16[2048,128]{1,0:T(8,128)(2,1)S(1)} %bitcast.11), custom_call_target="tpu_custom_call" | custom-call | flops 1073741824 | bytes 1048576 | tf_op jit(solution)/shard_map/pallas_call | solution.py:241
  103.5 0.0 collective-permute-done.1.source_ref
  103.5 1.6 %shard_map.141 = (f32[128,1024]{1,0:T(8,128)}, f32[1024,128]{1,0:T(8,128)}, f32[128,1024]{1,0:T(8,128)}, f32[1024,128]{1,0:T(8,128)}) custom-call(s32[2]{0:T(128)S(1)} %pad_add_fusion.where_ref, bf16[2048,128]{1,0:T(8,128)(2,1)S(1)} %collective-permute-done.1.source_ref, ...), custom_call_target="tpu_custom_call", output_to_operand_aliasing={{0}: (2, {}), {1}: (3, {}), {2}: (4, {}), {3}: (5, {})} | custom-call | bytes 1048576 | tf_op jit(solution)/shard_map/pallas_call | solution.py:241
  (2 shorter events, 0.0 us)
Async XLA Ops:
  4.8 17.9 %copy-start = (bf16[128,1024]{1,0:T(8,128)(2,1)S(1)}, bf16[128,1024]{1,0:T(8,128)(2,1)}, u32[]{:S(2)}) copy-start(bf16[128,1024]{1,0:T(8,128)(2,1)} %qw1_ref.1) | copy-start | bytes 786436
  4.8 17.9 %copy-start.1 = (bf16[1024,128]{1,0:T(8,128)(2,1)S(1)}, bf16[1024,128]{1,0:T(8,128)(2,1)}, u32[]{:S(2)}) copy-start(bf16[1024,128]{1,0:T(8,128)(2,1)} %qw2_ref.1) | copy-start | bytes 786436
  4.8 17.9 %copy-start.2 = (bf16[128,1024]{1,0:T(8,128)(2,1)S(1)}, bf16[128,1024]{1,0:T(8,128)(2,1)}, u32[]{:S(2)}) copy-start(bf16[128,1024]{1,0:T(8,128)(2,1)} %iw1_ref.1) | copy-start | bytes 786436
  4.8 17.9 %copy-start.3 = (bf16[1024,128]{1,0:T(8,128)(2,1)S(1)}, bf16[1024,128]{1,0:T(8,128)(2,1)}, u32[]{:S(2)}) copy-start(bf16[1024,128]{1,0:T(8,128)(2,1)} %iw2_ref.1) | copy-start | bytes 786436
  4.8 17.9 %copy-start.4 = (bf16[1,256,128]{2,1,0:T(8,128)(2,1)S(1)}, bf16[1,256,128]{2,1,0:T(8,128)(2,1)}, u32[]{:S(2)}) copy-start(bf16[1,256,128]{2,1,0:T(8,128)(2,1)} %param.14) | copy-start | bytes 196612
  4.8 17.9 %copy-start.5 = (f32[2,256,128]{2,1,0:T(8,128)S(1)}, f32[2,256,128]{2,1,0:T(8,128)}, u32[]{:S(2)}) copy-start(f32[2,256,128]{2,1,0:T(8,128)} %get-tuple-element.25.units_ref) | copy-start | bytes 786436
  4.9 17.9 %copy-start.6 = (f32[2,256,128]{2,1,0:T(8,128)S(1)}, f32[2,256,128]{2,1,0:T(8,128)}, u32[]{:S(2)}) copy-start(f32[2,256,128]{2,1,0:T(8,128)} %get-tuple-element.26.radii_ref) | copy-start | bytes 786436
  4.9 17.9 %copy-start.8 = (bf16[256,128]{1,0:T(8,128)(2,1)S(1)}, bf16[256,128]{1,0:T(8,128)(2,1)}, u32[]{:S(2)}) copy-start(bf16[256,128]{1,0:T(8,128)(2,1)} %get-tuple-element.24.pooled_ref) | copy-start | bytes 196612
  4.9 17.9 %copy-start.9 = (s32[1,256]{1,0:T(1,128)S(1)}, s32[1,256]{1,0:T(1,128)}, u32[]{:S(2)}) copy-start(s32[1,256]{1,0:T(1,128)} %pos_ref.1) | copy-start | bytes 3076
  4.9 17.8 %all-to-all-start = ((bf16[8,528,128]{2,1,0:T(8,128)(2,1)}), bf16[8,528,128]{2,1,0:T(8,128)(2,1)S(1)}, u32[]{:S(2)}, u32[]{:S(2)}) async-start(bf16[8,528,128]{2,1,0:T(8,128)(2,1)} %get-tuple-element.23), calls=%async_computation | async-start | bytes 2162688 | tf_op jit(solution)/shard_map/all_to_all | solution.py:254
  22.8 13.4 %copy-start.7 = (f32[1,256,128]{2,1,0:T(8,128)S(1)}, f32[1,256,128]{2,1,0:T(8,128)}, u32[]{:S(2)}) copy-start(f32[1,256,128]{2,1,0:T(8,128)} %param.10) | copy-start | bytes 393220
  22.8 13.4 %copy-start.10 = (s32[1,256]{1,0:T(1,128)S(1)}, s32[1,256]{1,0:T(1,128)}, u32[]{:S(2)}) copy-start(s32[1,256]{1,0:T(1,128)} %counts_ref.1) | copy-start | bytes 3076
  22.8 13.4 %copy-start.11 = (bf16[256,256]{1,0:T(8,128)(2,1)S(1)}, bf16[256,256]{1,0:T(8,128)(2,1)}, u32[]{:S(2)}) copy-start(bf16[256,256]{1,0:T(8,128)(2,1)} %get-tuple-element.29.tally_ref) | copy-start | bytes 393220
  22.8 13.4 %copy-start.12 = (f32[1,256]{1,0:T(1,128)S(1)}, f32[1,256]{1,0:T(1,128)}, u32[]{:S(2)}) copy-start(f32[1,256]{1,0:T(1,128)} %state_ref.1) | copy-start | bytes 3076
  28.9 8.8 %collective-permute-start = (bf16[2048,128]{1,0:T(8,128)(2,1)S(1)}, bf16[2048,128]{1,0:T(8,128)(2,1)S(1)}, u32[]{:S(2)}, u32[]{:S(2)}) collective-permute-start(bf16[2048,128]{1,0:T(8,128)(2,1)S(1)} %get-tuple-element.28), channel_id=1, source_target_pairs={{0,1},{1,0},{2,3},{3,2},{4,5},{5,4},{6,7},{7,6},{8,9},{9,8},{10,11... | collective-permute-start | bytes 1572872 | tf_op jit(solution)/shard_map/ppermute | solution.py:301
  95.7 7.8 %collective-permute-start.1 = (bf16[2048,128]{1,0:T(8,128)(2,1)S(1)}, bf16[2048,128]{1,0:T(8,128)(2,1)S(1)}, u32[]{:S(2)}, u32[]{:S(2)}) collective-permute-start(bf16[2048,128]{1,0:T(8,128)(2,1)S(1)} %bitcast.10), channel_id=1, source_target_pairs={{0,1},{1,0},{2,3},{3,2},{4,5},{5,4},{6,7},{7,6},{8,9},{9,8},{10,11... | collective-permute-start | bytes 1572872 | tf_op jit(solution)/shard_map/ppermute | solution.py:312

commit v4 on v3

--- a/solution.py
+++ b/solution.py
@@ -1,5 +1,3 @@
-import functools
-
 import jax
 import jax.numpy as jnp
 from jax import lax
@@ -43,9 +41,13 @@
     return (product[:, 2 * LANES :] + product[:, LANES : 2 * LANES]) + product[:, :LANES]
 
 
+def radius_of(outer):
+    return jnp.sqrt(jnp.sum(outer * outer, axis=1, keepdims=True) + NORM_EPS)
+
+
 def front_kernel(
     ids_hbm, counts_hbm, pos_hbm, table_hbm, feats_hbm, qw1_hbm, qw2_hbm, iw1_hbm, iw2_hbm,
-    payload_ref, pooled_ref, tally_ref, units_ref, radii_ref,
+    payload_ref, pooled_ref, tally_ref, outers_ref,
     ids_ref, counts_ref, pos_ref, table_ref, feats_ref, qw1_ref, qw2_ref, iw1_ref, iw2_ref, arrived,
 ):
     sources = (ids_hbm, counts_hbm, table_hbm, qw1_hbm, feats_hbm, iw1_hbm, qw2_hbm, iw2_hbm, pos_hbm)
@@ -80,11 +82,8 @@
         hidden = (pre * jax.nn.sigmoid(pre)).astype(BF16)
         copies[second].wait()
         outer = jnp.dot(hidden, targets[second][...], preferred_element_type=F32)
-        radius = jnp.sqrt(jnp.sum(outer * outer, axis=1, keepdims=True) + NORM_EPS)
-        unit = outer / radius
-        units_ref[slot] = unit
-        radii_ref[slot] = jnp.broadcast_to(radius, unit.shape)
-        return unit.astype(BF16)
+        outers_ref[slot] = outer
+        return (outer / radius_of(outer)).astype(BF16)
 
     queries = tower(pooled, 3, 6, 0)
     copies[4].wait()
@@ -103,15 +102,50 @@
         payload_ref[copy, 2 * q_rows :] = spread
 
 
+def prepare_kernel(
+    where_ref, pooled_ref, feats_ref, other_ref, qw1_ref, qw2_ref, iw1_ref, iw2_ref,
+    slope_ref, hidden_ref, inputs_ref, second_ref,
+    both_ref, first_ref,
+):
+    core = where_ref[1]
+    rows = other_ref.shape[0]
+
+    @pl.when(core == 0)
+    def _():
+        both_ref[:rows] = pooled_ref[...]
+        first_ref[...] = qw1_ref[...]
+        second_ref[...] = qw2_ref[...]
+
+    @pl.when(core != 0)
+    def _():
+        both_ref[:rows] = feats_ref[...]
+        first_ref[...] = iw1_ref[...]
+        second_ref[...] = iw2_ref[...]
+
+    both_ref[rows:] = other_ref[...]
+    both = both_ref[...]
+    inputs_ref[...] = jnp.transpose(both)
+    pre = jnp.dot(both, first_ref[...], preferred_element_type=F32)
+    sigma = jax.nn.sigmoid(pre)
+    hidden_ref[...] = jnp.transpose((pre * sigma).astype(BF16))
+    slope_ref[...] = sigma * (1.0 + pre * (1.0 - sigma))
+
+
+def outer_grad(d_unit, outer):
+    radius = radius_of(outer)
+    unit = outer / radius
+    along = jnp.sum(unit * d_unit, axis=1, keepdims=True)
+    return ((d_unit - unit * along) / radius).astype(BF16)
+
+
 def middle_kernel(
-    where_ref, all_ref, pos_ref, pooled_ref, feats_ref, units_ref, radii_ref,
-    qw1_ref, qw2_ref, iw1_ref, iw2_ref,
-    keep_ref, send_ref, d_x_ref,
-    totals_ref, codes_ref, d_units_ref, grads_ref,
+    where_ref, all_ref, pos_ref, outers_ref,
+    d_query_outer_ref, keep_ref, send_ref,
+    totals_ref, codes_ref,
 ):
     ranks = all_ref.shape[0]
-    q_rows = pooled_ref.shape[0]
-    i_rows = feats_ref.shape[0]
+    q_rows = outers_ref.shape[1]
+    i_rows = outers_ref.shape[1]
     blk = where_ref[0]
     core = where_ref[1]
     norm_c = 1.0 / (q_rows * ranks)
@@ -163,73 +197,76 @@
     for r in range(ranks):
         d_keys = add_queries(r, d_keys)
         d_queries = add_keys(r, d_queries)
-    d_units_ref[1] = LOGIT_SCALE * d_keys
-    d_units_ref[0] = LOGIT_SCALE * d_queries
-
-    def tower_back(inputs_ref, first_ref, second_ref, slot):
-        unit = units_ref[slot]
-        d_unit = d_units_ref[slot]
-        along = jnp.sum(unit * d_unit, axis=1, keepdims=True)
-        d_outer = ((d_unit - unit * along) / radii_ref[slot]).astype(BF16)
-        inputs = inputs_ref[...]
-        h = second_ref.shape[0]
-        pre = jnp.dot(inputs, first_ref[...], preferred_element_type=F32)
-        sigma = jax.nn.sigmoid(pre)
-        hidden = (pre * sigma).astype(BF16)
-        grads_ref[slot, h:] = contract_lead(hidden, d_outer)
-        d_hidden = contract_last(d_outer, second_ref[...])
-        d_pre = (d_hidden * sigma * (1.0 + pre * (1.0 - sigma))).astype(BF16)
-        first_grad = contract_lead(inputs, d_pre)
-        for j in range(h // LANES):
-            grads_ref[slot, j * LANES : (j + 1) * LANES] = first_grad[:, j * LANES : (j + 1) * LANES]
-        return d_pre
-
-    tower_back(feats_ref, iw1_ref, iw2_ref, 1)
-    d_pre = tower_back(pooled_ref, qw1_ref, qw2_ref, 0)
-    d_x_ref[...] = contract_last(d_pre, qw1_ref[...])
-    keep_ref[...] = grads_ref[core]
-    send_ref[...] = grads_ref[1 - core].astype(BF16)
-
-
-def rows_kernel(tally_ref, counts_ref, d_x_ref, table_ref, state_ref, new_ref):
+
+    d_key_outer = outer_grad(LOGIT_SCALE * d_keys, outers_ref[1])
+    d_query_outer = outer_grad(LOGIT_SCALE * d_queries, outers_ref[0])
+    d_query_outer_ref[...] = d_query_outer
+
+    @pl.when(core == 0)
+    def _():
+        keep_ref[...] = d_query_outer
+        send_ref[...] = d_key_outer
+
+    @pl.when(core != 0)
+    def _():
+        keep_ref[...] = d_key_outer
+        send_ref[...] = d_query_outer
+
+
+def back_kernel(keep_ref, received_ref, slope_ref, hidden_ref, inputs_ref, second_ref, grads_ref):
+    h = second_ref.shape[0]
+    d_outer = jnp.concatenate([keep_ref[...], received_ref[...]], axis=0)
+    grads_ref[h:] = jnp.dot(hidden_ref[...], d_outer, preferred_element_type=F32).astype(BF16)
+    d_pre = (contract_last(d_outer, second_ref[...]) * slope_ref[...]).astype(BF16)
+    first_grad = jnp.dot(inputs_ref[...], d_pre, preferred_element_type=F32).astype(BF16)
+    for j in range(h // LANES):
+        grads_ref[j * LANES : (j + 1) * LANES] = first_grad[:, j * LANES : (j + 1) * LANES]
+
+
+def rows_kernel(
+    tally_ref, counts_ref, pooled_ref, d_outer_ref, qw1_ref, qw2_ref, table_ref, state_ref, new_ref
+):
+    pre = jnp.dot(pooled_ref[...], qw1_ref[...], preferred_element_type=F32)
+    sigma = jax.nn.sigmoid(pre)
+    d_hidden = contract_last(d_outer_ref[...], qw2_ref[...])
+    d_pre = (d_hidden * (sigma * (1.0 + pre * (1.0 - sigma)))).astype(BF16)
+    d_x = contract_last(d_pre, qw1_ref[...])
     counts = column_of(counts_ref[...].astype(F32))
-    pieces = three_pieces(d_x_ref[...] / counts)
+    pieces = three_pieces(d_x / counts)
     row_grads = add_pieces(jnp.dot(tally_ref[...], pieces, preferred_element_type=F32))
     mean = jnp.mean(row_grads * row_grads, axis=1, keepdims=True)
     acc = column_of(state_ref[...]) + mean
     new_ref[...] = table_ref[...] - LEARNING_RATE * row_grads / jnp.sqrt(acc)
 
 
-def finish_kernel(mine, where_ref, source_ref, *refs):
-    q1_ref, q2_ref, i1_ref, i2_ref, first_ref, second_ref, sent = refs[-7:]
+def finish_kernel(
+    where_ref, mine_ref, other_ref, q1_ref, q2_ref, i1_ref, i2_ref, first_ref, second_ref, sent
+):
     core = where_ref[1]
-    e, h = first_ref.shape
-
-    def copies(first_hbm, second_hbm):
-        return [
-            pltpu.make_async_copy(first_ref, first_hbm, sent.at[0]),
-            pltpu.make_async_copy(second_ref, second_hbm, sent.at[1]),
-        ]
-
-    def write(first_hbm, second_hbm):
-        first, second = copies(first_hbm, second_hbm)
-        second_ref[...] = source_ref[h:].astype(F32)
-        second.start()
-        for i in range(h // LANES):
-            first_ref[:, i * LANES : (i + 1) * LANES] = source_ref[i * LANES : (i + 1) * LANES].astype(F32)
-        first.start()
-        second.wait()
-        first.wait()
-
-    query_tower = (core == 0) if mine else (core != 0)
-
-    @pl.when(query_tower)
-    def _():
-        write(q1_ref, q2_ref)
-
-    @pl.when(jnp.logical_not(query_tower))
-    def _():
-        write(i1_ref, i2_ref)
+    h = second_ref.shape[1]
+
+    def write(query_source, item_source):
+        copies = []
+        for slot, (source_ref, first_hbm, second_hbm) in enumerate(
+            ((query_source, q1_ref, q2_ref), (item_source, i1_ref, i2_ref))
+        ):
+            second_ref[slot] = source_ref[h:].astype(F32)
+            copies.append(pltpu.make_async_copy(second_ref.at[slot], second_hbm, sent.at[slot, 0]))
+            copies[-1].start()
+            for j in range(0, h, LANES):
+                first_ref[slot, :, j : j + LANES] = source_ref[j : j + LANES].astype(F32)
+            copies.append(pltpu.make_async_copy(first_ref.at[slot], first_hbm, sent.at[slot, 1]))
+            copies[-1].start()
+        for copy in copies:
+            copy.wait()
+
+    @pl.when(core == 0)
+    def _():
+        write(mine_ref, other_ref)
+
+    @pl.when(core != 0)
+    def _():
+        write(other_ref, mine_ref)
 
 
 VMEM = pl.BlockSpec(memory_space=pltpu.VMEM)
@@ -237,14 +274,13 @@
 HBM = pl.BlockSpec(memory_space=pltpu.HBM)
 
 
-def call(kernel, out_shape, operands, in_specs=None, out_specs=None, scratch=(), flops=0, limit=32, aliases=None):
+def call(kernel, out_shape, operands, in_specs=None, out_specs=None, scratch=(), flops=0, limit=32):
     return pl.pallas_call(
         kernel,
         out_shape=out_shape,
         in_specs=in_specs or [VMEM] * len(operands),
         out_specs=out_specs or jax.tree.map(lambda _: VMEM, out_shape),
         scratch_shapes=list(scratch),
-        input_output_aliases=aliases or {},
         compiler_params=pltpu.CompilerParams(vmem_limit_bytes=limit * 2**20),
         cost_estimate=pl.CostEstimate(flops=flops, bytes_accessed=2**20, transcendentals=0),
     )(*operands)
@@ -269,13 +305,12 @@
 
     ids = bag_ids[0].T
     arguments = [ids, bag_counts, positives, table, feats, q_w1, q_w2, i_w1, i_w2]
-    payload, pooled, tally, units, radii = call(
+    payload, pooled, tally, outers = call(
         front_kernel,
         [
             struct((ranks, q_rows + i_rows + CODE_ROWS, e), BF16),
             struct((q_rows, e), BF16),
             struct((table.shape[0], q_rows), BF16),
-            struct((2, q_rows, e), F32),
             struct((2, q_rows, e), F32),
         ],
         arguments,
@@ -285,50 +320,54 @@
         limit=60,
     )
     everyone = exchange(payload, group)
-    keep, send, d_x = call(
+    swap = [(0, 1), (1, 0)]
+    other_inputs = lax.ppermute(jnp.where(where[1] == 0, feats, pooled), "c", swap)
+    prepared = call(
+        prepare_kernel,
+        [
+            struct((2 * q_rows, h), F32),
+            struct((h, 2 * q_rows), BF16),
+            struct((e, 2 * q_rows), BF16),
+            struct((h, e), BF16),
+        ],
+        [where, pooled, feats, other_inputs, q_w1, q_w2, i_w1, i_w2],
+        in_specs=[SMEM] + [VMEM] * 7,
+        scratch=[pltpu.VMEM((2 * q_rows, e), BF16), pltpu.VMEM((e, h), BF16)],
+        flops=2**28,
+    )
+    d_query_outer, keep, send = call(
         middle_kernel,
-        [struct((2 * h, e), F32), struct((2 * h, e), BF16), struct((q_rows, e), F32)],
-        [where, everyone, positives, pooled, feats, units, radii, q_w1, q_w2, i_w1, i_w2],
-        in_specs=[SMEM] + [VMEM] * 10,
-        scratch=[
-            pltpu.VMEM((ranks, 8, q_rows), F32),
-            pltpu.VMEM((ranks, 8, q_rows), jnp.int32),
-            pltpu.VMEM((2, q_rows, e), F32),
-            pltpu.VMEM((2, 2 * h, e), F32),
-        ],
-    )
-    swap = [(0, 1), (1, 0)]
+        [struct((q_rows, e), BF16)] * 3,
+        [where, everyone, positives, outers],
+        in_specs=[SMEM] + [VMEM] * 3,
+        scratch=[pltpu.VMEM((ranks, 8, q_rows), F32), pltpu.VMEM((ranks, 8, q_rows), jnp.int32)],
+    )
     received = lax.ppermute(send, "c", swap)
+    grads = call(back_kernel, struct((2 * h, e), BF16), [keep, received, *prepared])
     new_rows = call(
-        rows_kernel, struct(table.shape, F32), [tally, bag_counts, d_x, table, state], flops=2**30
-    )
-    chip_sum = (keep + received.astype(F32)).astype(BF16).reshape(spread, 2 * h // spread, e)
-    chip_sum, new_rows = lax.optimization_barrier((chip_sum, new_rows))
+        rows_kernel,
+        struct(table.shape, F32),
+        [tally, bag_counts, pooled, d_query_outer, q_w1, q_w2, table, state],
+        flops=2**30,
+    )
+    chip_sum = grads.reshape(spread, 2 * h // spread, e)
     mine = jnp.sum(exchange(chip_sum, block).astype(F32), axis=0).astype(BF16)
     copies = jnp.broadcast_to(mine, (lax.axis_size("zh"),) + mine.shape)
     mine = jnp.sum(exchange(copies, "zh").astype(F32), axis=0).astype(BF16)
     copies = jnp.broadcast_to(mine, (spread,) + mine.shape)
     tower = exchange(copies, block).reshape(2 * h, e)
     other = lax.ppermute(tower, "c", swap)
-    shapes = [struct((e, h), F32), struct((h, e), F32), struct((e, h), F32), struct((h, e), F32)]
-    buffers = [pltpu.VMEM((e, h), F32), pltpu.VMEM((h, e), F32), pltpu.SemaphoreType.DMA((2,))]
-    own = call(
-        functools.partial(finish_kernel, True),
-        shapes,
-        [where, tower],
-        in_specs=[SMEM, VMEM],
+    sums = call(
+        finish_kernel,
+        [struct((e, h), F32), struct((h, e), F32), struct((e, h), F32), struct((h, e), F32)],
+        [where, tower, other],
+        in_specs=[SMEM, VMEM, VMEM],
         out_specs=[HBM] * 4,
-        scratch=buffers,
-        flops=2**30,
-    )
-    sums = call(
-        functools.partial(finish_kernel, False),
-        shapes,
-        [where, other, *own],
-        in_specs=[SMEM, VMEM] + [HBM] * 4,
-        out_specs=[HBM] * 4,
-        scratch=buffers,
-        aliases={2: 0, 3: 1, 4: 2, 5: 3},
+        scratch=[
+            pltpu.VMEM((2, e, h), F32),
+            pltpu.VMEM((2, h, e), F32),
+            pltpu.SemaphoreType.DMA((2, 2)),
+        ],
     )
     return (new_rows[None], *sums)
 

time: 105 us -> 105 us (level)
  waiting for transfers between devices: 12 us -> 5.03 us
  starting transfers between devices: 19.6 us -> 26 us
    all_to_all x1, waiting for transfers between devices: 11.7 us -> 5.02 us  [exchange(): return lax.all_to_all(values, axes, 0, 0, tiled=True)]
    ppermute x0 -> x1, starting transfers between devices: none -> 6.54 us  [per_device(): lax.ppermute(jnp.where(where[1] == 0, feats, pooled), 'c', swap)]
    pallas_call x5 -> x6, Pallas kernels: 14.5 us -> 14.5 us  [call(): pl.pallas_call(kernel, out_shape=out_shape, in_specs=in_specs or [VMEM] *...]
  transfers between devices with their start and end apart: 3 -> 4, of which waited for: 2 -> 1; matrix products, arithmetic and copies ran while one was open for 0% -> 0% of each run, Pallas kernels for 3% -> 7%
where the time goes in v4:
time: 105 us
  blocking collectives  57.9 us (55%)
  starting transfers between devices  26 us (25%)
  Pallas kernels  14.5 us (14%)
  waiting for transfers between devices  5.03 us (5%)
    all_to_all x3, blocking collectives, exchange(): return lax.all_to_all(values, axes, 0, 0, tiled=True)  57.9 us
    pallas_call x6, Pallas kernels, call(): pl.pallas_call(kernel, out_shape=out_shape, in_specs=in_specs or [VMEM] *...  14.5 us
    ppermute x1, starting transfers between devices, per_device(): received = lax.ppermute(send, 'c', swap)  7.25 us
    ppermute x1, starting transfers between devices, per_device(): lax.ppermute(jnp.where(where[1] == 0, feats, pooled), 'c', swap)  6.54 us
    all_to_all x1, starting transfers between devices, exchange(): return lax.all_to_all(values, axes, 0, 0, tiled=True)  6.09 us
    ppermute x1, starting transfers between devices, per_device(): other = lax.ppermute(tower, 'c', swap)  6.07 us
    all_to_all x1, waiting for transfers between devices, exchange(): return lax.all_to_all(values, axes, 0, 0, tiled=True)  5.02 us
  transfers between devices with their start and end apart: 4, of which 1 were waited for; matrix products, arithmetic and copies ran while one was open for 0% of the time, Pallas kernels for 7%

profile of v4, /device:TPU:1, one launch (start us, length us, event | category | flops | bytes accessed | tf_op | source)
XLA Modules:
  0.0 104.7 jit_solution(6173521273736837080)
XLA Ops:
  0.6 4.1 %shard_map.137 = (bf16[8,528,128]{2,1,0:T(8,128)(2,1)}, bf16[256,128]{1,0:T(8,128)(2,1)}, bf16[256,256]{1,0:T(8,128)(2,1)}, f32[2,256,128]{2,1,0:T(8,128)}) custom-call(s32[16,256]{1,0:T(8,128)} %bitcast.18, s32[1,256]{1,0:T(1,128)} %counts_ref.1, s32[1,256]{1,0:T(1,128)} %pos_ref.1, f32[256,128]{1,0:T(8,128)} %bitcast.16, bf16[256,128]{1,0:T(8,128)(2,1)} %bitcast.14, ...), custom_call_target="tpu_custom_call" | custom-call | bytes 1048576 | tf_op jit(solution)/shard_map/pallas_call | solution.py:278
  4.7 0.0 copy-start.4
  4.7 0.0 copy-start.5
  4.7 0.0 copy-start.6
  4.7 0.0 copy-start.8
  4.7 6.1 %all-to-all-start = ((bf16[8,528,128]{2,1,0:T(8,128)(2,1)}), bf16[8,528,128]{2,1,0:T(8,128)(2,1)S(1)}, u32[]{:S(2)}, u32[]{:S(2)}) async-start(bf16[8,528,128]{2,1,0:T(8,128)(2,1)} %get-tuple-element.22), calls=%async_computation | async-start | bytes 2162688 | tf_op jit(solution)/shard_map/all_to_all | solution.py:290
  10.8 0.0 copy-start
  10.8 0.0 copy-start.1
  10.8 0.0 copy-start.2
  10.9 0.0 copy-start.3
  10.9 0.0 copy-done.4
  10.9 0.0 copy-done.5
  10.9 6.5 %collective-permute-start.1 = (bf16[256,128]{1,0:T(8,128)(2,1)S(1)}, bf16[256,128]{1,0:T(8,128)(2,1)S(1)}, u32[]{:S(2)}, u32[]{:S(2)}) collective-permute-start(bf16[256,128]{1,0:T(8,128)(2,1)S(1)} %broadcast_select_fusion), channel_id=1, source_target_pairs={{0,1},{1,0},{2,3},{3,2},{4,5},{5,4},{6,7},{7,6},{8,9},{9,8},{10,11... | collective-permute-start | bytes 196616 | tf_op jit(solution)/shard_map/ppermute | solution.py:324
  17.5 0.1 pad_add_fusion.where_ref
  17.6 5.0 %all-to-all-done.all_ref = bf16[8,528,128]{2,1,0:T(8,128)(2,1)S(1)} async-done(((bf16[8,528,128]{2,1,0:T(8,128)(2,1)}), bf16[8,528,128]{2,1,0:T(8,128)(2,1)S(1)}, u32[]{:S(2)}, u32[]{:S(2)}) %all-to-all-start) | async-done | bytes 1081376 | tf_op jit(solution)/shard_map/all_to_all | solution.py:290
  22.6 0.0 copy-done.6
  22.6 0.0 copy-done.8
  22.6 4.5 %shard_map.138 = (bf16[256,128]{1,0:T(8,128)(2,1)S(1)}, bf16[256,128]{1,0:T(8,128)(2,1)S(1)}, bf16[256,128]{1,0:T(8,128)(2,1)S(1)}) custom-call(s32[2]{0:T(128)S(1)} %pad_add_fusion.where_ref, bf16[8,528,128]{2,1,0:T(8,128)(2,1)S(1)} %all-to-all-done.all_ref, s32[1,256]{1,0:T(1,128)S(1)} %copy-done.8, f32[2,256,128]{2,1,0:T(8,128)S(1)} %copy-done.6), custom_call_target="tpu_custom_call" | custom-call | bytes 1048576 | tf_op jit(solution)/shard_map/pallas_call | solution.py:278
  27.1 7.3 %collective-permute-start = (bf16[256,128]{1,0:T(8,128)(2,1)S(1)}, bf16[256,128]{1,0:T(8,128)(2,1)S(1)}, u32[]{:S(2)}, u32[]{:S(2)}) collective-permute-start(bf16[256,128]{1,0:T(8,128)(2,1)S(1)} %get-tuple-element.26), channel_id=1, source_target_pairs={{0,1},{1,0},{2,3},{3,2},{4,5},{5,4},{6,7},{7,6},{8,9},{9,8},{10,11... | collective-permute-start | bytes 196616 | tf_op jit(solution)/shard_map/ppermute | solution.py:345
  34.3 0.0 collective-permute-done.1.other_ref
  34.3 0.0 copy-done
  34.3 0.0 copy-done.1
  34.3 0.0 copy-done.2
  34.4 0.0 copy-done.3
  34.4 1.4 %shard_map.140 = (f32[512,1024]{1,0:T(8,128)S(1)}, bf16[1024,512]{1,0:T(8,128)(2,1)S(1)}, bf16[128,512]{1,0:T(8,128)(2,1)S(1)}, bf16[1024,128]{1,0:T(8,128)(2,1)S(1)}) custom-call(s32[2]{0:T(128)S(1)} %pad_add_fusion.where_ref, bf16[256,128]{1,0:T(8,128)(2,1)S(1)} %copy-done.5, bf16[256,128]{1,0:T(8,128)(2,1)S(1)} %bitcast.15, ...), custom_call_target="tpu_custom_call" | custom-call | flops 268435456 | bytes 1048576 | tf_op jit(solution)/shard_map/pallas_call | solution.py:278
  35.8 0.0 collective-permute-done.received_ref
  35.8 0.9 shard_map.141
  36.7 16.8 %all_to_all.20 = bf16[32,64,128]{2,1,0:T(8,128)(2,1)S(1)} all-to-all(bf16[32,64,128]{2,1,0:T(8,128)(2,1)S(1)} %bitcast.13), channel_id=1, replica_groups=mesh['y'=4,'xl'=2,'zh'=8,'zp'=2,'xh'=2,'c'=2] {'y','xl','zp','xh'}, dimensions={0} | all-to-all | bytes 1048576 | tf_op jit(solution)/shard_map/all_to_all | solution.py:290
  53.5 0.1 reduce_sum.24
  53.6 0.0 copy-start.7
  53.6 0.0 copy-start.9
  53.6 0.0 copy-start.10
  53.6 0.0 copy-start.11
  53.6 27.3 %all_to_all.21 = bf16[8,64,128]{2,1,0:T(8,128)(2,1)S(1)} all-to-all(bf16[8,64,128]{2,1,0:T(8,128)(2,1)S(1)} %broadcast_in_dim.10), channel_id=1, replica_groups=mesh['y'=4,'xl'=2,'zh'=8,'zp'=2,'xh'=2,'c'=2] {'zh'}, dimensions={0} | all-to-all | bytes 262144 | tf_op jit(solution)/shard_map/all_to_all | solution.py:290
  81.0 0.1 broadcast_in_dim.11
  81.1 13.9 %all_to_all.22 = bf16[32,64,128]{2,1,0:T(8,128)(2,1)S(1)} all-to-all(bf16[32,64,128]{2,1,0:T(8,128)(2,1)S(1)} %broadcast_in_dim.11), channel_id=1, replica_groups=mesh['y'=4,'xl'=2,'zh'=8,'zp'=2,'xh'=2,'c'=2] {'y','xl','zp','xh'}, dimensions={0} | all-to-all | bytes 1048576 | tf_op jit(solution)/shard_map/all_to_all | solution.py:290
  94.9 6.1 %collective-permute-start.2 = (bf16[2048,128]{1,0:T(8,128)(2,1)S(1)}, bf16[2048,128]{1,0:T(8,128)(2,1)S(1)}, u32[]{:S(2)}, u32[]{:S(2)}) collective-permute-start(bf16[2048,128]{1,0:T(8,128)(2,1)S(1)} %bitcast.11), channel_id=1, source_target_pairs={{0,1},{1,0},{2,3},{3,2},{4,5},{5,4},{6,7},{7,6},{8,9},{9,8},{10,11... | collective-permute-start | bytes 1572872 | tf_op jit(solution)/shard_map/ppermute | solution.py:359
  101.0 0.0 copy-done.7
  101.0 0.0 copy-done.9
  101.0 0.0 copy-done.10
  101.0 0.0 copy-done.11
  101.0 1.8 %shard_map.139 = f32[256,128]{1,0:T(8,128)} custom-call(bf16[256,256]{1,0:T(8,128)(2,1)S(1)} %copy-done.10, s32[1,256]{1,0:T(1,128)S(1)} %copy-done.9, bf16[256,128]{1,0:T(8,128)(2,1)S(1)} %copy-done.5, bf16[256,128]{1,0:T(8,128)(2,1)S(1)} %get-tuple-element.24.d_outer_ref, bf16[128,1024]{1,0:T(8,128)(2,1)S(1)} %copy-done.2, ...), custom_call_target="tpu_custom_call" | custom-call | flops 1073741824 | bytes 1048576 | tf_op jit(solution)/shard_map/pallas_call | solution.py:278
  102.8 0.0 collective-permute-done.2.other_ref
  102.8 1.9 %shard_map.142 = (f32[128,1024]{1,0:T(8,128)}, f32[1024,128]{1,0:T(8,128)}, f32[128,1024]{1,0:T(8,128)}, f32[1024,128]{1,0:T(8,128)}) custom-call(s32[2]{0:T(128)S(1)} %pad_add_fusion.where_ref, bf16[2048,128]{1,0:T(8,128)(2,1)S(1)} %bitcast.12, bf16[2048,128]{1,0:T(8,128)(2,1)S(1)} %collective-permute-done.2.other_ref), custom_call_target="tpu_custom_call" | custom-call | bytes 1048576 | tf_op jit(solution)/shard_map/pallas_call | solution.py:278
  (3 shorter events, 0.1 us)
Async XLA Ops:
  4.7 6.2 %copy-start.4 = (bf16[1,256,128]{2,1,0:T(8,128)(2,1)S(1)}, bf16[1,256,128]{2,1,0:T(8,128)(2,1)}, u32[]{:S(2)}) copy-start(bf16[1,256,128]{2,1,0:T(8,128)(2,1)} %param.14) | copy-start | bytes 196612
  4.7 6.2 %copy-start.5 = (bf16[256,128]{1,0:T(8,128)(2,1)S(1)}, bf16[256,128]{1,0:T(8,128)(2,1)}, u32[]{:S(2)}) copy-start(bf16[256,128]{1,0:T(8,128)(2,1)} %get-tuple-element.21.pooled_ref) | copy-start | bytes 196612
  4.7 17.9 %copy-start.6 = (f32[2,256,128]{2,1,0:T(8,128)S(1)}, f32[2,256,128]{2,1,0:T(8,128)}, u32[]{:S(2)}) copy-start(f32[2,256,128]{2,1,0:T(8,128)} %get-tuple-element.23.outers_ref) | copy-start | bytes 786436
  4.7 17.8 %copy-start.8 = (s32[1,256]{1,0:T(1,128)S(1)}, s32[1,256]{1,0:T(1,128)}, u32[]{:S(2)}) copy-start(s32[1,256]{1,0:T(1,128)} %pos_ref.1) | copy-start | bytes 3076
  4.7 17.8 %all-to-all-start = ((bf16[8,528,128]{2,1,0:T(8,128)(2,1)}), bf16[8,528,128]{2,1,0:T(8,128)(2,1)S(1)}, u32[]{:S(2)}, u32[]{:S(2)}) async-start(bf16[8,528,128]{2,1,0:T(8,128)(2,1)} %get-tuple-element.22), calls=%async_computation | async-start | bytes 2162688 | tf_op jit(solution)/shard_map/all_to_all | solution.py:290
  10.8 23.5 %copy-start = (bf16[128,1024]{1,0:T(8,128)(2,1)S(1)}, bf16[128,1024]{1,0:T(8,128)(2,1)}, u32[]{:S(2)}) copy-start(bf16[128,1024]{1,0:T(8,128)(2,1)} %iw1_ref.1) | copy-start | bytes 786436
  10.8 23.5 %copy-start.1 = (bf16[1024,128]{1,0:T(8,128)(2,1)S(1)}, bf16[1024,128]{1,0:T(8,128)(2,1)}, u32[]{:S(2)}) copy-start(bf16[1024,128]{1,0:T(8,128)(2,1)} %iw2_ref.1) | copy-start | bytes 786436
  10.8 23.5 %copy-start.2 = (bf16[128,1024]{1,0:T(8,128)(2,1)S(1)}, bf16[128,1024]{1,0:T(8,128)(2,1)}, u32[]{:S(2)}) copy-start(bf16[128,1024]{1,0:T(8,128)(2,1)} %qw1_ref.3) | copy-start | bytes 786436
  10.9 23.5 %copy-start.3 = (bf16[1024,128]{1,0:T(8,128)(2,1)S(1)}, bf16[1024,128]{1,0:T(8,128)(2,1)}, u32[]{:S(2)}) copy-start(bf16[1024,128]{1,0:T(8,128)(2,1)} %qw2_ref.3) | copy-start | bytes 786436
  10.9 23.4 %collective-permute-start.1 = (bf16[256,128]{1,0:T(8,128)(2,1)S(1)}, bf16[256,128]{1,0:T(8,128)(2,1)S(1)}, u32[]{:S(2)}, u32[]{:S(2)}) collective-permute-start(bf16[256,128]{1,0:T(8,128)(2,1)S(1)} %broadcast_select_fusion), channel_id=1, source_target_pairs={{0,1},{1,0},{2,3},{3,2},{4,5},{5,4},{6,7},{7,6},{8,9},{9,8},{10,11... | collective-permute-start | bytes 196616 | tf_op jit(solution)/shard_map/ppermute | solution.py:324
  27.1 8.7 %collective-permute-start = (bf16[256,128]{1,0:T(8,128)(2,1)S(1)}, bf16[256,128]{1,0:T(8,128)(2,1)S(1)}, u32[]{:S(2)}, u32[]{:S(2)}) collective-permute-start(bf16[256,128]{1,0:T(8,128)(2,1)S(1)} %get-tuple-element.26), channel_id=1, source_target_pairs={{0,1},{1,0},{2,3},{3,2},{4,5},{5,4},{6,7},{7,6},{8,9},{9,8},{10,11... | collective-permute-start | bytes 196616 | tf_op jit(solution)/shard_map/ppermute | solution.py:345
  53.6 47.4 %copy-start.7 = (f32[1,256,128]{2,1,0:T(8,128)S(1)}, f32[1,256,128]{2,1,0:T(8,128)}, u32[]{:S(2)}) copy-start(f32[1,256,128]{2,1,0:T(8,128)} %param.10) | copy-start | bytes 393220
  53.6 47.4 %copy-start.9 = (s32[1,256]{1,0:T(1,128)S(1)}, s32[1,256]{1,0:T(1,128)}, u32[]{:S(2)}) copy-start(s32[1,256]{1,0:T(1,128)} %counts_ref.1) | copy-start | bytes 3076
  53.6 47.4 %copy-start.10 = (bf16[256,256]{1,0:T(8,128)(2,1)S(1)}, bf16[256,256]{1,0:T(8,128)(2,1)}, u32[]{:S(2)}) copy-start(bf16[256,256]{1,0:T(8,128)(2,1)} %get-tuple-element.20.tally_ref) | copy-start | bytes 393220
  53.6 47.4 %copy-start.11 = (f32[1,256]{1,0:T(1,128)S(1)}, f32[1,256]{1,0:T(1,128)}, u32[]{:S(2)}) copy-start(f32[1,256]{1,0:T(1,128)} %state_ref.1) | copy-start | bytes 3076
  94.9 7.9 %collective-permute-start.2 = (bf16[2048,128]{1,0:T(8,128)(2,1)S(1)}, bf16[2048,128]{1,0:T(8,128)(2,1)S(1)}, u32[]{:S(2)}, u32[]{:S(2)}) collective-permute-start(bf16[2048,128]{1,0:T(8,128)(2,1)S(1)} %bitcast.11), channel_id=1, source_target_pairs={{0,1},{1,0},{2,3},{3,2},{4,5},{5,4},{6,7},{7,6},{8,9},{9,8},{10,11... | collective-permute-start | bytes 1572872 | tf_op jit(solution)/shard_map/ppermute | solution.py:359

commit v5 on v4

--- a/solution.py
+++ b/solution.py
@@ -102,33 +102,34 @@
         payload_ref[copy, 2 * q_rows :] = spread
 
 
+def backward(inputs, hidden_t, slope, d_outer, second):
+    d_pre = (contract_last(d_outer, second) * slope).astype(BF16)
+    return contract_lead(inputs, d_pre), jnp.dot(hidden_t, d_outer, preferred_element_type=F32)
+
+
+def forward(inputs, first):
+    pre = jnp.dot(inputs, first, preferred_element_type=F32)
+    sigma = jax.nn.sigmoid(pre)
+    return jnp.transpose((pre * sigma).astype(BF16)), sigma * (1.0 + pre * (1.0 - sigma))
+
+
 def prepare_kernel(
-    where_ref, pooled_ref, feats_ref, other_ref, qw1_ref, qw2_ref, iw1_ref, iw2_ref,
-    slope_ref, hidden_ref, inputs_ref, second_ref,
-    both_ref, first_ref,
+    where_ref, keep_ref, qw1_ref, qw2_ref, iw1_ref, iw2_ref,
+    hidden_ref, slope_ref, first_ref, second_ref,
 ):
     core = where_ref[1]
-    rows = other_ref.shape[0]
 
     @pl.when(core == 0)
     def _():
-        both_ref[:rows] = pooled_ref[...]
         first_ref[...] = qw1_ref[...]
         second_ref[...] = qw2_ref[...]
 
     @pl.when(core != 0)
     def _():
-        both_ref[:rows] = feats_ref[...]
         first_ref[...] = iw1_ref[...]
         second_ref[...] = iw2_ref[...]
 
-    both_ref[rows:] = other_ref[...]
-    both = both_ref[...]
-    inputs_ref[...] = jnp.transpose(both)
-    pre = jnp.dot(both, first_ref[...], preferred_element_type=F32)
-    sigma = jax.nn.sigmoid(pre)
-    hidden_ref[...] = jnp.transpose((pre * sigma).astype(BF16))
-    slope_ref[...] = sigma * (1.0 + pre * (1.0 - sigma))
+    hidden_ref[...], slope_ref[...] = forward(keep_ref[keep_ref.shape[0] // 2 :], first_ref[...])
 
 
 def outer_grad(d_unit, outer):
@@ -139,7 +140,7 @@
 
 
 def middle_kernel(
-    where_ref, all_ref, pos_ref, outers_ref,
+    where_ref, all_ref, pos_ref, outers_ref, pooled_ref, feats_ref,
     d_query_outer_ref, keep_ref, send_ref,
     totals_ref, codes_ref,
 ):
@@ -202,23 +203,30 @@
     d_query_outer = outer_grad(LOGIT_SCALE * d_queries, outers_ref[0])
     d_query_outer_ref[...] = d_query_outer
 
+    def split(query_ref, key_ref):
+        query_ref[:q_rows] = d_query_outer
+        query_ref[q_rows:] = pooled_ref[...]
+        key_ref[:i_rows] = d_key_outer
+        key_ref[i_rows:] = feats_ref[...]
+
     @pl.when(core == 0)
     def _():
-        keep_ref[...] = d_query_outer
-        send_ref[...] = d_key_outer
+        split(keep_ref, send_ref)
 
     @pl.when(core != 0)
     def _():
-        keep_ref[...] = d_key_outer
-        send_ref[...] = d_query_outer
-
-
-def back_kernel(keep_ref, received_ref, slope_ref, hidden_ref, inputs_ref, second_ref, grads_ref):
+        split(send_ref, keep_ref)
+
+
+def back_kernel(keep_ref, received_ref, hidden_ref, slope_ref, first_ref, second_ref, grads_ref):
     h = second_ref.shape[0]
-    d_outer = jnp.concatenate([keep_ref[...], received_ref[...]], axis=0)
-    grads_ref[h:] = jnp.dot(hidden_ref[...], d_outer, preferred_element_type=F32).astype(BF16)
-    d_pre = (contract_last(d_outer, second_ref[...]) * slope_ref[...]).astype(BF16)
-    first_grad = jnp.dot(inputs_ref[...], d_pre, preferred_element_type=F32).astype(BF16)
+    rows = keep_ref.shape[0] // 2
+    second = second_ref[...]
+    hidden_t, slope = forward(received_ref[rows:], first_ref[...])
+    first_mine, second_mine = backward(keep_ref[rows:], hidden_ref[...], slope_ref[...], keep_ref[:rows], second)
+    first_other, second_other = backward(received_ref[rows:], hidden_t, slope, received_ref[:rows], second)
+    grads_ref[h:] = (second_mine + second_other).astype(BF16)
+    first_grad = (first_mine + first_other).astype(BF16)
     for j in range(h // LANES):
         grads_ref[j * LANES : (j + 1) * LANES] = first_grad[:, j * LANES : (j + 1) * LANES]
 
@@ -305,6 +313,7 @@
 
     ids = bag_ids[0].T
     arguments = [ids, bag_counts, positives, table, feats, q_w1, q_w2, i_w1, i_w2]
+    arguments = [pltpu.with_memory_space_constraint(a, pltpu.HBM) for a in arguments]
     payload, pooled, tally, outers = call(
         front_kernel,
         [
@@ -317,32 +326,25 @@
         in_specs=[HBM] * len(arguments),
         scratch=[pltpu.VMEM(a.shape, a.dtype) for a in arguments]
         + [pltpu.SemaphoreType.DMA((len(arguments),))],
-        limit=60,
-    )
+    )
+    payload, where = lax.optimization_barrier((payload, where))
     everyone = exchange(payload, group)
+    d_query_outer, keep, send = call(
+        middle_kernel,
+        [struct((q_rows, e), BF16), struct((2 * q_rows, e), BF16), struct((2 * q_rows, e), BF16)],
+        [where, everyone, positives, outers, pooled, feats],
+        in_specs=[SMEM] + [VMEM] * 5,
+        scratch=[pltpu.VMEM((ranks, 8, q_rows), F32), pltpu.VMEM((ranks, 8, q_rows), jnp.int32)],
+    )
     swap = [(0, 1), (1, 0)]
-    other_inputs = lax.ppermute(jnp.where(where[1] == 0, feats, pooled), "c", swap)
+    received = lax.ppermute(send, "c", swap)
     prepared = call(
         prepare_kernel,
-        [
-            struct((2 * q_rows, h), F32),
-            struct((h, 2 * q_rows), BF16),
-            struct((e, 2 * q_rows), BF16),
-            struct((h, e), BF16),
-        ],
-        [where, pooled, feats, other_inputs, q_w1, q_w2, i_w1, i_w2],
-        in_specs=[SMEM] + [VMEM] * 7,
-        scratch=[pltpu.VMEM((2 * q_rows, e), BF16), pltpu.VMEM((e, h), BF16)],
+        [struct((h, q_rows), BF16), struct((q_rows, h), F32), struct((e, h), BF16), struct((h, e), BF16)],
+        [where, keep, q_w1, q_w2, i_w1, i_w2],
+        in_specs=[SMEM] + [VMEM] * 5,
         flops=2**28,
     )
-    d_query_outer, keep, send = call(
-        middle_kernel,
-        [struct((q_rows, e), BF16)] * 3,
-        [where, everyone, positives, outers],
-        in_specs=[SMEM] + [VMEM] * 3,
-        scratch=[pltpu.VMEM((ranks, 8, q_rows), F32), pltpu.VMEM((ranks, 8, q_rows), jnp.int32)],
-    )
-    received = lax.ppermute(send, "c", swap)
     grads = call(back_kernel, struct((2 * h, e), BF16), [keep, received, *prepared])
     new_rows = call(
         rows_kernel,

time: 105 us -> 104 us (level)
  blocking collectives: 57.9 us -> 77.1 us
  starting transfers between devices: 26 us -> 12.3 us
  waiting for transfers between devices: 5.03 us -> 0.01 us
    all_to_all x3 -> x4, blocking collectives: 57.9 us -> 77.1 us  [exchange(): return lax.all_to_all(values, axes, 0, 0, tiled=True)]
    ppermute x1 -> x0, starting transfers between devices: 6.54 us -> none  [per_device(): lax.ppermute(jnp.where(where[1] == 0, feats, pooled), 'c', swap)]
    all_to_all x1 -> x0, starting transfers between devices: 6.09 us -> none  [exchange(): return lax.all_to_all(values, axes, 0, 0, tiled=True)]
    all_to_all x1 -> x0, waiting for transfers between devices: 5.02 us -> none  [exchange(): return lax.all_to_all(values, axes, 0, 0, tiled=True)]
  transfers between devices with their start and end apart: 4 -> 2, of which waited for: 1 -> 0; matrix products, arithmetic and copies ran while one was open for 0% -> 0% of each run, Pallas kernels for 7% -> 3%
where the time goes in v5:
time: 104 us
  blocking collectives  77.1 us (74%)
  Pallas kernels  13.5 us (13%)
  starting transfers between devices  12.3 us (12%)
    all_to_all x4, blocking collectives, exchange(): return lax.all_to_all(values, axes, 0, 0, tiled=True)  77.1 us
    pallas_call x6, Pallas kernels, call(): pl.pallas_call(kernel, out_shape=out_shape, in_specs=in_specs or [VMEM] *...  13.5 us
    ppermute x1, starting transfers between devices, per_device(): received = lax.ppermute(send, 'c', swap)  6.5 us
    ppermute x1, starting transfers between devices, per_device(): other = lax.ppermute(tower, 'c', swap)  5.82 us
  transfers between devices with their start and end apart: 2, of which 0 were waited for; matrix products, arithmetic and copies ran while one was open for 0% of the time, Pallas kernels for 3%

profile of v5, /device:TPU:1, one launch (start us, length us, event | category | flops | bytes accessed | tf_op | source)
XLA Modules:
  0.0 104.1 jit_solution(2083207896069139216)
XLA Ops:
  0.6 0.1 pad_add_fusion.where_ref
  0.7 3.0 %shard_map.137 = (bf16[8,528,128]{2,1,0:T(8,128)(2,1)S(1)}, bf16[256,128]{1,0:T(8,128)(2,1)S(1)}, bf16[256,256]{1,0:T(8,128)(2,1)S(1)}, f32[2,256,128]{2,1,0:T(8,128)S(1)}) custom-call(s32[16,256]{1,0:T(8,128)} %bitcast.17, s32[1,256]{1,0:T(1,128)} %counts_ref.1, s32[1,256]{1,0:T(1,128)} %pos_ref.1, f32[256,128]{1,0:T(8,128)} %bitcast.15, ...), custom_call_target="tpu_custom_call" | custom-call | bytes 1048576 | tf_op jit(solution)/shard_map/pallas_call | solution.py:286
  3.7 0.0 copy-start.4
  3.7 0.0 copy-start.6
  3.7 18.5 %all_to_all.20.all_ref = bf16[8,528,128]{2,1,0:T(8,128)(2,1)S(1)} all-to-all(bf16[8,528,128]{2,1,0:T(8,128)(2,1)S(1)} %get-tuple-element.26), channel_id=1, replica_groups=mesh['y'=4,'xl'=2,'zh'=8,'zp'=2,'xh'=2,'c'=2] {'y','xl'}, dimensions={0} | all-to-all | bytes 2162688 | tf_op jit(solution)/shard_map/all_to_all | solution.py:298
  22.2 0.0 copy-start
  22.2 0.0 copy-start.1
  22.2 0.0 copy-start.2
  22.2 0.0 copy-start.3
  22.2 0.0 copy-done.4
  22.2 0.0 copy-done.6
  22.2 4.5 %shard_map.138 = (bf16[256,128]{1,0:T(8,128)(2,1)S(1)}, bf16[512,128]{1,0:T(8,128)(2,1)S(1)}, bf16[512,128]{1,0:T(8,128)(2,1)S(1)}) custom-call(s32[2]{0:T(128)S(1)} %pad_add_fusion.where_ref, bf16[8,528,128]{2,1,0:T(8,128)(2,1)S(1)} %all_to_all.20.all_ref, s32[1,256]{1,0:T(1,128)S(1)} %copy-done.6, f32[2,256,128]{2,1,0:T(8,128)S(1)} %get-tuple-element.27.outers_ref, ...), custom_call_target="tpu_custom_call" | custom-call | bytes 1048576 | tf_op jit(solution)/shard_map/pallas_call | solution.py:286
  26.7 6.5 %collective-permute-start = (bf16[512,128]{1,0:T(8,128)(2,1)S(1)}, bf16[512,128]{1,0:T(8,128)(2,1)S(1)}, u32[]{:S(2)}, u32[]{:S(2)}) collective-permute-start(bf16[512,128]{1,0:T(8,128)(2,1)S(1)} %get-tuple-element.30), channel_id=1, source_target_pairs={{0,1},{1,0},{2,3},{3,2},{4,5},{5,4},{6,7},{7,6},{8,9},{9,8},{10,11... | collective-permute-start | bytes 393224 | tf_op jit(solution)/shard_map/ppermute | solution.py:340
  33.2 0.0 copy-done
  33.2 0.0 copy-done.1
  33.2 0.0 copy-done.2
  33.3 0.0 copy-done.3
  33.3 1.1 %shard_map.140 = (bf16[1024,256]{1,0:T(8,128)(2,1)S(1)}, f32[256,1024]{1,0:T(8,128)S(1)}, bf16[128,1024]{1,0:T(8,128)(2,1)S(1)}, bf16[1024,128]{1,0:T(8,128)(2,1)S(1)}) custom-call(s32[2]{0:T(128)S(1)} %pad_add_fusion.where_ref, bf16[512,128]{1,0:T(8,128)(2,1)S(1)} %get-tuple-element.29.keep_ref, bf16[128,1024]{1,0:T(8,128)(2,1)S(1)} %copy-done.2, ...), custom_call_target="tpu_custom_call" | custom-call | flops 268435456 | bytes 1048576 | tf_op jit(solution)/shard_map/pallas_call | solution.py:286
  34.4 0.0 collective-permute-done.received_ref
  34.4 1.3 %shard_map.141 = bf16[2048,128]{1,0:T(8,128)(2,1)S(1)} custom-call(bf16[512,128]{1,0:T(8,128)(2,1)S(1)} %get-tuple-element.29.keep_ref, bf16[512,128]{1,0:T(8,128)(2,1)S(1)} %collective-permute-done.received_ref, bf16[1024,256]{1,0:T(8,128)(2,1)S(1)} %get-tuple-element.31.hidden_ref, f32[256,1024]{1,0:T(8,128)S(1)} %get-tuple-element.32.slope_ref, ...), custom_call_target="tpu_custom_call" | custom-call | bytes 1048576 | tf_op jit(solution)/shard_map/pallas_call | solution.py:286
  35.6 17.2 %all_to_all.21 = bf16[32,64,128]{2,1,0:T(8,128)(2,1)S(1)} all-to-all(bf16[32,64,128]{2,1,0:T(8,128)(2,1)S(1)} %bitcast.12), channel_id=1, replica_groups=mesh['y'=4,'xl'=2,'zh'=8,'zp'=2,'xh'=2,'c'=2] {'y','xl','zp','xh'}, dimensions={0} | all-to-all | bytes 1048576 | tf_op jit(solution)/shard_map/all_to_all | solution.py:298
  52.8 0.1 reduce_sum.24
  52.9 0.0 copy-start.5
  52.9 0.0 copy-start.7
  52.9 0.0 copy-start.8
  53.0 27.5 %all_to_all.22 = bf16[8,64,128]{2,1,0:T(8,128)(2,1)S(1)} all-to-all(bf16[8,64,128]{2,1,0:T(8,128)(2,1)S(1)} %broadcast_in_dim.10), channel_id=1, replica_groups=mesh['y'=4,'xl'=2,'zh'=8,'zp'=2,'xh'=2,'c'=2] {'zh'}, dimensions={0} | all-to-all | bytes 262144 | tf_op jit(solution)/shard_map/all_to_all | solution.py:298
  80.5 0.1 broadcast_in_dim.11
  80.6 13.9 %all_to_all.23 = bf16[32,64,128]{2,1,0:T(8,128)(2,1)S(1)} all-to-all(bf16[32,64,128]{2,1,0:T(8,128)(2,1)S(1)} %broadcast_in_dim.11), channel_id=1, replica_groups=mesh['y'=4,'xl'=2,'zh'=8,'zp'=2,'xh'=2,'c'=2] {'y','xl','zp','xh'}, dimensions={0} | all-to-all | bytes 1048576 | tf_op jit(solution)/shard_map/all_to_all | solution.py:298
  94.5 5.8 %collective-permute-start.1 = (bf16[2048,128]{1,0:T(8,128)(2,1)S(1)}, bf16[2048,128]{1,0:T(8,128)(2,1)S(1)}, u32[]{:S(2)}, u32[]{:S(2)}) collective-permute-start(bf16[2048,128]{1,0:T(8,128)(2,1)S(1)} %bitcast.10), channel_id=1, source_target_pairs={{0,1},{1,0},{2,3},{3,2},{4,5},{5,4},{6,7},{7,6},{8,9},{9,8},{10,11... | collective-permute-start | bytes 1572872 | tf_op jit(solution)/shard_map/ppermute | solution.py:361
  100.4 0.0 copy-done.5
  100.4 0.0 copy-done.7
  100.4 0.0 copy-done.8
  100.4 1.8 %shard_map.139 = f32[256,128]{1,0:T(8,128)} custom-call(bf16[256,256]{1,0:T(8,128)(2,1)S(1)} %get-tuple-element.22.tally_ref, s32[1,256]{1,0:T(1,128)S(1)} %copy-done.7, bf16[256,128]{1,0:T(8,128)(2,1)S(1)} %get-tuple-element.23.pooled_ref, bf16[256,128]{1,0:T(8,128)(2,1)S(1)} %get-tuple-element.28.d_outer_ref, bf16[128,1024]{1,0:T(8,128)(2,1)S(1)} %copy-done.2, ...), custom_call_target="tpu_custom_call" | custom-call | flops 1073741824 | bytes 1048576 | tf_op jit(solution)/shard_map/pallas_call | solution.py:286
  102.1 0.0 collective-permute-done.1.other_ref
  102.2 1.9 %shard_map.142 = (f32[128,1024]{1,0:T(8,128)}, f32[1024,128]{1,0:T(8,128)}, f32[128,1024]{1,0:T(8,128)}, f32[1024,128]{1,0:T(8,128)}) custom-call(s32[2]{0:T(128)S(1)} %pad_add_fusion.where_ref, bf16[2048,128]{1,0:T(8,128)(2,1)S(1)} %bitcast.11, bf16[2048,128]{1,0:T(8,128)(2,1)S(1)} %collective-permute-done.1.other_ref), custom_call_target="tpu_custom_call" | custom-call | bytes 1048576 | tf_op jit(solution)/shard_map/pallas_call | solution.py:286
  (2 shorter events, 0.0 us)
Async XLA Ops:
  3.7 18.5 %copy-start.4 = (bf16[1,256,128]{2,1,0:T(8,128)(2,1)S(1)}, bf16[1,256,128]{2,1,0:T(8,128)(2,1)}, u32[]{:S(2)}) copy-start(bf16[1,256,128]{2,1,0:T(8,128)(2,1)} %param.14) | copy-start | bytes 196612
  3.7 18.5 %copy-start.6 = (s32[1,256]{1,0:T(1,128)S(1)}, s32[1,256]{1,0:T(1,128)}, u32[]{:S(2)}) copy-start(s32[1,256]{1,0:T(1,128)} %pos_ref.1) | copy-start | bytes 3076
  22.2 11.0 %copy-start = (bf16[128,1024]{1,0:T(8,128)(2,1)S(1)}, bf16[128,1024]{1,0:T(8,128)(2,1)}, u32[]{:S(2)}) copy-start(bf16[128,1024]{1,0:T(8,128)(2,1)} %iw1_ref.1) | copy-start | bytes 786436
  22.2 11.0 %copy-start.1 = (bf16[1024,128]{1,0:T(8,128)(2,1)S(1)}, bf16[1024,128]{1,0:T(8,128)(2,1)}, u32[]{:S(2)}) copy-start(bf16[1024,128]{1,0:T(8,128)(2,1)} %iw2_ref.1) | copy-start | bytes 786436
  22.2 11.0 %copy-start.2 = (bf16[128,1024]{1,0:T(8,128)(2,1)S(1)}, bf16[128,1024]{1,0:T(8,128)(2,1)}, u32[]{:S(2)}) copy-start(bf16[128,1024]{1,0:T(8,128)(2,1)} %qw1_ref.3) | copy-start | bytes 786436
  22.2 11.1 %copy-start.3 = (bf16[1024,128]{1,0:T(8,128)(2,1)S(1)}, bf16[1024,128]{1,0:T(8,128)(2,1)}, u32[]{:S(2)}) copy-start(bf16[1024,128]{1,0:T(8,128)(2,1)} %qw2_ref.3) | copy-start | bytes 786436
  26.7 7.7 %collective-permute-start = (bf16[512,128]{1,0:T(8,128)(2,1)S(1)}, bf16[512,128]{1,0:T(8,128)(2,1)S(1)}, u32[]{:S(2)}, u32[]{:S(2)}) collective-permute-start(bf16[512,128]{1,0:T(8,128)(2,1)S(1)} %get-tuple-element.30), channel_id=1, source_target_pairs={{0,1},{1,0},{2,3},{3,2},{4,5},{5,4},{6,7},{7,6},{8,9},{9,8},{10,11... | collective-permute-start | bytes 393224 | tf_op jit(solution)/shard_map/ppermute | solution.py:340
  52.9 47.5 %copy-start.5 = (f32[1,256,128]{2,1,0:T(8,128)S(1)}, f32[1,256,128]{2,1,0:T(8,128)}, u32[]{:S(2)}) copy-start(f32[1,256,128]{2,1,0:T(8,128)} %param.10) | copy-start | bytes 393220
  52.9 47.5 %copy-start.7 = (s32[1,256]{1,0:T(1,128)S(1)}, s32[1,256]{1,0:T(1,128)}, u32[]{:S(2)}) copy-start(s32[1,256]{1,0:T(1,128)} %counts_ref.1) | copy-start | bytes 3076
  52.9 47.5 %copy-start.8 = (f32[1,256]{1,0:T(1,128)S(1)}, f32[1,256]{1,0:T(1,128)}, u32[]{:S(2)}) copy-start(f32[1,256]{1,0:T(1,128)} %state_ref.1) | copy-start | bytes 3076
  94.5 7.6 %collective-permute-start.1 = (bf16[2048,128]{1,0:T(8,128)(2,1)S(1)}, bf16[2048,128]{1,0:T(8,128)(2,1)S(1)}, u32[]{:S(2)}, u32[]{:S(2)}) collective-permute-start(bf16[2048,128]{1,0:T(8,128)(2,1)S(1)} %bitcast.10), channel_id=1, source_target_pairs={{0,1},{1,0},{2,3},{3,2},{4,5},{5,4},{6,7},{7,6},{8,9},{9,8},{10,11... | collective-permute-start | bytes 1572872 | tf_op jit(solution)/shard_map/ppermute | solution.py:361

commit v6 on v5

--- a/solution.py
+++ b/solution.py
@@ -1,5 +1,8 @@
+import functools
+
 import jax
 import jax.numpy as jnp
+import numpy as np
 from jax import lax
 from jax.experimental import pallas as pl
 from jax.experimental.pallas import tpu as pltpu
@@ -140,15 +143,16 @@
 
 
 def middle_kernel(
-    where_ref, all_ref, pos_ref, outers_ref, pooled_ref, feats_ref,
+    order, where_ref, all_ref, pos_ref, outers_ref, pooled_ref, feats_ref,
     d_query_outer_ref, keep_ref, send_ref,
     totals_ref, codes_ref,
 ):
     ranks = all_ref.shape[0]
     q_rows = outers_ref.shape[1]
     i_rows = outers_ref.shape[1]
-    blk = where_ref[0]
+    slot = where_ref[0]
     core = where_ref[1]
+    item_start = where_ref[2] * i_rows
     norm_c = 1.0 / (q_rows * ranks)
 
     def add_group(s, carry):
@@ -171,18 +175,18 @@
 
     lax.fori_loop(0, ranks, add_group, 0, unroll=True)
 
-    own_keys = all_ref[blk, q_rows : q_rows + i_rows]
+    own_keys = all_ref[slot, q_rows : q_rows + i_rows]
 
     def add_queries(s, d_keys):
         queries = all_ref[s, :q_rows]
         shares = jnp.exp2(EXP_SCALE * contract_last(own_keys, queries)) * (norm_c / totals_ref[s, :1])
-        item = blk * i_rows + lax.broadcasted_iota(jnp.int32, (i_rows, q_rows), 0)
+        item = item_start + lax.broadcasted_iota(jnp.int32, (i_rows, q_rows), 0)
         weights = (shares - jnp.where(codes_ref[s, :1] == item, norm_c, 0.0)).astype(BF16)
         return d_keys + jnp.dot(weights, queries, preferred_element_type=F32)
 
 
-    own_queries = all_ref[blk, :q_rows]
-    inverse = column_of(norm_c / totals_ref[blk, :1])
+    own_queries = all_ref[slot, :q_rows]
+    inverse = column_of(norm_c / totals_ref[slot, :1])
     inverse = jnp.concatenate([inverse] * (i_rows // LANES), axis=1)
     target = jnp.concatenate([column_of(pos_ref[...])] * (i_rows // LANES), axis=1)
     target = target - lax.broadcasted_iota(jnp.int32, (q_rows, i_rows), 1)
@@ -190,7 +194,7 @@
     def add_keys(t, d_queries):
         keys = all_ref[t, q_rows : q_rows + i_rows]
         shares = jnp.exp2(EXP_SCALE * contract_last(own_queries, keys)) * inverse
-        weights = (shares - jnp.where(target == t * i_rows, norm_c, 0.0)).astype(BF16)
+        weights = (shares - jnp.where(target == order[t] * i_rows, norm_c, 0.0)).astype(BF16)
         return d_queries + jnp.dot(weights, keys, preferred_element_type=F32)
 
     d_keys = jnp.zeros((i_rows, LANES), F32)
@@ -299,8 +303,9 @@
 
 
 def per_device(rows, state, bag_ids, bag_counts, item_feats, positives, q_w1, q_w2, i_w1, i_w2):
-    group = ("y", "xl")
-    block = ("y", "xl", "zp", "xh")
+    group = ("ya", "xl", "yb")
+    block = ("zp", "xh", "xl", "ya", "yb")
+    strided = ("zb", "zc", "za")
     struct = jax.ShapeDtypeStruct
     ranks = lax.axis_size(group)
     spread = lax.axis_size(block)
@@ -309,7 +314,13 @@
     q_rows, e = bag_ids.shape[1], table.shape[1]
     i_rows = feats.shape[0]
     h = q_w2.shape[0]
-    where = jnp.stack([lax.axis_index(group), lax.axis_index("c")]).astype(jnp.int32)
+    blk_axes = ("ya", "yb", "xl")
+    where = jnp.stack(
+        [lax.axis_index(group), lax.axis_index("c"), lax.axis_index(blk_axes)]
+    ).astype(jnp.int32)
+    sizes = [lax.axis_size(axis) for axis in blk_axes]
+    numbers = np.arange(ranks).reshape(sizes).transpose([blk_axes.index(axis) for axis in group])
+    order = [int(number) for number in numbers.reshape(-1)]
 
     ids = bag_ids[0].T
     arguments = [ids, bag_counts, positives, table, feats, q_w1, q_w2, i_w1, i_w2]
@@ -330,7 +341,7 @@
     payload, where = lax.optimization_barrier((payload, where))
     everyone = exchange(payload, group)
     d_query_outer, keep, send = call(
-        middle_kernel,
+        functools.partial(middle_kernel, order),
         [struct((q_rows, e), BF16), struct((2 * q_rows, e), BF16), struct((2 * q_rows, e), BF16)],
         [where, everyone, positives, outers, pooled, feats],
         in_specs=[SMEM] + [VMEM] * 5,
@@ -354,8 +365,8 @@
     )
     chip_sum = grads.reshape(spread, 2 * h // spread, e)
     mine = jnp.sum(exchange(chip_sum, block).astype(F32), axis=0).astype(BF16)
-    copies = jnp.broadcast_to(mine, (lax.axis_size("zh"),) + mine.shape)
-    mine = jnp.sum(exchange(copies, "zh").astype(F32), axis=0).astype(BF16)
+    copies = jnp.broadcast_to(mine, (lax.axis_size(strided),) + mine.shape)
+    mine = jnp.sum(exchange(copies, strided).astype(F32), axis=0).astype(BF16)
     copies = jnp.broadcast_to(mine, (spread,) + mine.shape)
     tower = exchange(copies, block).reshape(2 * h, e)
     other = lax.ppermute(tower, "c", swap)
@@ -375,11 +386,13 @@
 
 
 def solution(mesh):
-    blk, rep = mesh.devices.shape
-    parts = (blk // 2, 2, max(rep // 8, 1), 2 if rep >= 8 else 1, 2 if rep >= 4 else 1, 2)
-    fine = Mesh(mesh.devices.reshape(parts), ("y", "xl", "zh", "zp", "xh", "c"))
-    rep_axes = ("zh", "zp", "xh", "c")
-    blk_axes = ("y", "xl")
+    blk_axes = ("ya", "yb", "xl")
+    rep_axes = ("za", "zb", "zc", "zp", "xh", "c")
+    parts = []
+    for size, axes in zip(mesh.devices.shape, (blk_axes, rep_axes)):
+        bits = size.bit_length() - 1
+        parts += [1] * (len(axes) - bits) + [2] * bits
+    fine = Mesh(mesh.devices.reshape(parts), blk_axes + rep_axes)
     in_specs = (
         P(rep_axes, blk_axes, None),
         P(rep_axes, blk_axes),

time: 104 us -> 102 us (0.981)
  blocking collectives: 77.1 us -> 74.2 us
    all_to_all x4, blocking collectives: 77.1 us -> 74.2 us  [exchange(): return lax.all_to_all(values, axes, 0, 0, tiled=True)]
where the time goes in v6:
time: 102 us
  blocking collectives  74.2 us (73%)
  Pallas kernels  13.5 us (13%)
  starting transfers between devices  12.9 us (13%)
    all_to_all x4, blocking collectives, exchange(): return lax.all_to_all(values, axes, 0, 0, tiled=True)  74.2 us
    pallas_call x6, Pallas kernels, call(): pl.pallas_call(kernel, out_shape=out_shape, in_specs=in_specs or [VMEM] *...  13.5 us
    ppermute x1, starting transfers between devices, per_device(): received = lax.ppermute(send, 'c', swap)  6.49 us
    ppermute x1, starting transfers between devices, per_device(): other = lax.ppermute(tower, 'c', swap)  6.46 us
  transfers between devices with their start and end apart: 2, of which 0 were waited for; matrix products, arithmetic and copies ran while one was open for 0% of the time, Pallas kernels for 3%

profile of v6, /device:TPU:1, one launch (start us, length us, event | category | flops | bytes accessed | tf_op | source)
XLA Modules:
  0.0 101.9 jit_solution(4992025045890983958)
XLA Ops:
  0.6 0.1 pad_add_fusion.where_ref
  0.7 3.0 %shard_map.137 = (bf16[8,528,128]{2,1,0:T(8,128)(2,1)S(1)}, bf16[256,128]{1,0:T(8,128)(2,1)S(1)}, bf16[256,256]{1,0:T(8,128)(2,1)S(1)}, f32[2,256,128]{2,1,0:T(8,128)S(1)}) custom-call(s32[16,256]{1,0:T(8,128)} %bitcast.18, s32[1,256]{1,0:T(1,128)} %counts_ref.1, s32[1,256]{1,0:T(1,128)} %pos_ref.1, f32[256,128]{1,0:T(8,128)} %bitcast.16, ...), custom_call_target="tpu_custom_call" | custom-call | bytes 1048576 | tf_op jit(solution)/shard_map/pallas_call | solution.py:290
  3.7 0.0 copy-start.4
  3.7 0.0 copy-start.6
  3.7 18.6 %all_to_all.20.all_ref = bf16[8,528,128]{2,1,0:T(8,128)(2,1)S(1)} all-to-all(bf16[8,528,128]{2,1,0:T(8,128)(2,1)S(1)} %get-tuple-element.26), channel_id=1, replica_groups=mesh['ya'=2,'yb'=2,'xl'=2,'za'=2,'zb'=2,'zc'=2,'zp'=2,'xh'=2,'c'=2] {'ya..., dimensions={0} | all-to-all | bytes 2162688 | tf_op jit(solution)/shard_map/all_to_all | solution.py:302
  22.3 0.0 copy-start
  22.3 0.0 copy-start.1
  22.3 0.0 copy-start.2
  22.3 0.0 copy-start.3
  22.3 0.0 copy-done.4
  22.4 0.0 copy-done.6
  22.4 4.5 %shard_map.138 = (bf16[256,128]{1,0:T(8,128)(2,1)S(1)}, bf16[512,128]{1,0:T(8,128)(2,1)S(1)}, bf16[512,128]{1,0:T(8,128)(2,1)S(1)}) custom-call(s32[3]{0:T(128)S(1)} %pad_add_fusion.where_ref, bf16[8,528,128]{2,1,0:T(8,128)(2,1)S(1)} %all_to_all.20.all_ref, s32[1,256]{1,0:T(1,128)S(1)} %copy-done.6, f32[2,256,128]{2,1,0:T(8,128)S(1)} %get-tuple-element.27.outers_ref, ...), custom_call_target="tpu_custom_call" | custom-call | bytes 1048576 | tf_op jit(solution)/shard_map/pallas_call | solution.py:290
  26.9 6.5 %collective-permute-start = (bf16[512,128]{1,0:T(8,128)(2,1)S(1)}, bf16[512,128]{1,0:T(8,128)(2,1)S(1)}, u32[]{:S(2)}, u32[]{:S(2)}) collective-permute-start(bf16[512,128]{1,0:T(8,128)(2,1)S(1)} %get-tuple-element.30), channel_id=1, source_target_pairs={{0,1},{1,0},{2,3},{3,2},{4,5},{5,4},{6,7},{7,6},{8,9},{9,8},{10,11... | collective-permute-start | bytes 393224 | tf_op jit(solution)/shard_map/ppermute | solution.py:351
  33.4 0.0 copy-done
  33.4 0.0 copy-done.1
  33.4 0.0 copy-done.2
  33.4 0.0 copy-done.3
  33.4 1.1 %shard_map.140 = (bf16[1024,256]{1,0:T(8,128)(2,1)S(1)}, f32[256,1024]{1,0:T(8,128)S(1)}, bf16[128,1024]{1,0:T(8,128)(2,1)S(1)}, bf16[1024,128]{1,0:T(8,128)(2,1)S(1)}) custom-call(s32[3]{0:T(128)S(1)} %pad_add_fusion.where_ref, bf16[512,128]{1,0:T(8,128)(2,1)S(1)} %get-tuple-element.29.keep_ref, bf16[128,1024]{1,0:T(8,128)(2,1)S(1)} %copy-done.2, ...), custom_call_target="tpu_custom_call" | custom-call | flops 268435456 | bytes 1048576 | tf_op jit(solution)/shard_map/pallas_call | solution.py:290
  34.5 0.0 collective-permute-done.received_ref
  34.5 1.3 %shard_map.141 = bf16[2048,128]{1,0:T(8,128)(2,1)S(1)} custom-call(bf16[512,128]{1,0:T(8,128)(2,1)S(1)} %get-tuple-element.29.keep_ref, bf16[512,128]{1,0:T(8,128)(2,1)S(1)} %collective-permute-done.received_ref, bf16[1024,256]{1,0:T(8,128)(2,1)S(1)} %get-tuple-element.31.hidden_ref, f32[256,1024]{1,0:T(8,128)S(1)} %get-tuple-element.32.slope_ref, ...), custom_call_target="tpu_custom_call" | custom-call | bytes 1048576 | tf_op jit(solution)/shard_map/pallas_call | solution.py:290
  35.8 16.2 %all_to_all.21 = bf16[32,64,128]{2,1,0:T(8,128)(2,1)S(1)} all-to-all(bf16[32,64,128]{2,1,0:T(8,128)(2,1)S(1)} %bitcast.13), channel_id=1, replica_groups=mesh['ya'=2,'yb'=2,'xl'=2,'za'=2,'zb'=2,'zc'=2,'zp'=2,'xh'=2,'c'=2] {'zp..., dimensions={0} | all-to-all | bytes 1048576 | tf_op jit(solution)/shard_map/all_to_all | solution.py:302
  52.0 0.1 reduce_sum.24
  52.0 0.0 copy-start.5
  52.1 0.0 copy-start.7
  52.1 0.0 copy-start.8
  52.1 25.5 %all_to_all.22 = bf16[8,64,128]{2,1,0:T(8,128)(2,1)S(1)} all-to-all(bf16[8,64,128]{2,1,0:T(8,128)(2,1)S(1)} %broadcast_in_dim.10), channel_id=1, replica_groups=mesh['ya'=2,'yb'=2,'xl'=2,'za'=2,'zb'=2,'zc'=2,'zp'=2,'xh'=2,'c'=2] {'zb..., dimensions={0} | all-to-all | bytes 262144 | tf_op jit(solution)/shard_map/all_to_all | solution.py:302
  77.7 0.1 broadcast_in_dim.11
  77.8 13.9 %all_to_all.23 = bf16[32,64,128]{2,1,0:T(8,128)(2,1)S(1)} all-to-all(bf16[32,64,128]{2,1,0:T(8,128)(2,1)S(1)} %broadcast_in_dim.11), channel_id=1, replica_groups=mesh['ya'=2,'yb'=2,'xl'=2,'za'=2,'zb'=2,'zc'=2,'zp'=2,'xh'=2,'c'=2] {'zp..., dimensions={0} | all-to-all | bytes 1048576 | tf_op jit(solution)/shard_map/all_to_all | solution.py:302
  91.7 6.5 %collective-permute-start.1 = (bf16[2048,128]{1,0:T(8,128)(2,1)S(1)}, bf16[2048,128]{1,0:T(8,128)(2,1)S(1)}, u32[]{:S(2)}, u32[]{:S(2)}) collective-permute-start(bf16[2048,128]{1,0:T(8,128)(2,1)S(1)} %bitcast.11), channel_id=1, source_target_pairs={{0,1},{1,0},{2,3},{3,2},{4,5},{5,4},{6,7},{7,6},{8,9},{9,8},{10,11... | collective-permute-start | bytes 1572872 | tf_op jit(solution)/shard_map/ppermute | solution.py:372
  98.1 0.0 copy-done.5
  98.2 0.0 copy-done.7
  98.2 0.0 copy-done.8
  98.2 1.8 %shard_map.139 = f32[256,128]{1,0:T(8,128)} custom-call(bf16[256,256]{1,0:T(8,128)(2,1)S(1)} %get-tuple-element.22.tally_ref, s32[1,256]{1,0:T(1,128)S(1)} %copy-done.7, bf16[256,128]{1,0:T(8,128)(2,1)S(1)} %get-tuple-element.23.pooled_ref, bf16[256,128]{1,0:T(8,128)(2,1)S(1)} %get-tuple-element.28.d_outer_ref, bf16[128,1024]{1,0:T(8,128)(2,1)S(1)} %copy-done.2, ...), custom_call_target="tpu_custom_call" | custom-call | flops 1073741824 | bytes 1048576 | tf_op jit(solution)/shard_map/pallas_call | solution.py:290
  99.9 0.0 collective-permute-done.1.other_ref
  99.9 1.9 %shard_map.142 = (f32[128,1024]{1,0:T(8,128)}, f32[1024,128]{1,0:T(8,128)}, f32[128,1024]{1,0:T(8,128)}, f32[1024,128]{1,0:T(8,128)}) custom-call(s32[3]{0:T(128)S(1)} %pad_add_fusion.where_ref, bf16[2048,128]{1,0:T(8,128)(2,1)S(1)} %bitcast.12, bf16[2048,128]{1,0:T(8,128)(2,1)S(1)} %collective-permute-done.1.other_ref), custom_call_target="tpu_custom_call" | custom-call | bytes 1048576 | tf_op jit(solution)/shard_map/pallas_call | solution.py:290
  (2 shorter events, 0.0 us)
Async XLA Ops:
  3.7 18.7 %copy-start.4 = (bf16[1,256,128]{2,1,0:T(8,128)(2,1)S(1)}, bf16[1,256,128]{2,1,0:T(8,128)(2,1)}, u32[]{:S(2)}) copy-start(bf16[1,256,128]{2,1,0:T(8,128)(2,1)} %param.14) | copy-start | bytes 196612
  3.7 18.7 %copy-start.6 = (s32[1,256]{1,0:T(1,128)S(1)}, s32[1,256]{1,0:T(1,128)}, u32[]{:S(2)}) copy-start(s32[1,256]{1,0:T(1,128)} %pos_ref.1) | copy-start | bytes 3076
  22.3 11.0 %copy-start = (bf16[128,1024]{1,0:T(8,128)(2,1)S(1)}, bf16[128,1024]{1,0:T(8,128)(2,1)}, u32[]{:S(2)}) copy-start(bf16[128,1024]{1,0:T(8,128)(2,1)} %iw1_ref.1) | copy-start | bytes 786436
  22.3 11.0 %copy-start.1 = (bf16[1024,128]{1,0:T(8,128)(2,1)S(1)}, bf16[1024,128]{1,0:T(8,128)(2,1)}, u32[]{:S(2)}) copy-start(bf16[1024,128]{1,0:T(8,128)(2,1)} %iw2_ref.1) | copy-start | bytes 786436
  22.3 11.0 %copy-start.2 = (bf16[128,1024]{1,0:T(8,128)(2,1)S(1)}, bf16[128,1024]{1,0:T(8,128)(2,1)}, u32[]{:S(2)}) copy-start(bf16[128,1024]{1,0:T(8,128)(2,1)} %qw1_ref.3) | copy-start | bytes 786436
  22.3 11.0 %copy-start.3 = (bf16[1024,128]{1,0:T(8,128)(2,1)S(1)}, bf16[1024,128]{1,0:T(8,128)(2,1)}, u32[]{:S(2)}) copy-start(bf16[1024,128]{1,0:T(8,128)(2,1)} %qw2_ref.3) | copy-start | bytes 786436
  26.9 7.6 %collective-permute-start = (bf16[512,128]{1,0:T(8,128)(2,1)S(1)}, bf16[512,128]{1,0:T(8,128)(2,1)S(1)}, u32[]{:S(2)}, u32[]{:S(2)}) collective-permute-start(bf16[512,128]{1,0:T(8,128)(2,1)S(1)} %get-tuple-element.30), channel_id=1, source_target_pairs={{0,1},{1,0},{2,3},{3,2},{4,5},{5,4},{6,7},{7,6},{8,9},{9,8},{10,11... | collective-permute-start | bytes 393224 | tf_op jit(solution)/shard_map/ppermute | solution.py:351
  52.0 46.1 %copy-start.5 = (f32[1,256,128]{2,1,0:T(8,128)S(1)}, f32[1,256,128]{2,1,0:T(8,128)}, u32[]{:S(2)}) copy-start(f32[1,256,128]{2,1,0:T(8,128)} %param.10) | copy-start | bytes 393220
  52.1 46.1 %copy-start.7 = (s32[1,256]{1,0:T(1,128)S(1)}, s32[1,256]{1,0:T(1,128)}, u32[]{:S(2)}) copy-start(s32[1,256]{1,0:T(1,128)} %counts_ref.1) | copy-start | bytes 3076
  52.1 46.1 %copy-start.8 = (f32[1,256]{1,0:T(1,128)S(1)}, f32[1,256]{1,0:T(1,128)}, u32[]{:S(2)}) copy-start(f32[1,256]{1,0:T(1,128)} %state_ref.1) | copy-start | bytes 3076
  91.7 8.3 %collective-permute-start.1 = (bf16[2048,128]{1,0:T(8,128)(2,1)S(1)}, bf16[2048,128]{1,0:T(8,128)(2,1)S(1)}, u32[]{:S(2)}, u32[]{:S(2)}) collective-permute-start(bf16[2048,128]{1,0:T(8,128)(2,1)S(1)} %bitcast.11), channel_id=1, source_target_pairs={{0,1},{1,0},{2,3},{3,2},{4,5},{5,4},{6,7},{7,6},{8,9},{9,8},{10,11... | collective-permute-start | bytes 1572872 | tf_op jit(solution)/shard_map/ppermute | solution.py:372

commit v7 on v6

--- a/solution.py
+++ b/solution.py
@@ -145,7 +145,7 @@
 def middle_kernel(
     order, where_ref, all_ref, pos_ref, outers_ref, pooled_ref, feats_ref,
     d_query_outer_ref, keep_ref, send_ref,
-    totals_ref, codes_ref,
+    totals_ref, codes_ref, by_item_ref, by_query_ref,
 ):
     ranks = all_ref.shape[0]
     q_rows = outers_ref.shape[1]
@@ -155,15 +155,23 @@
     item_start = where_ref[2] * i_rows
     norm_c = 1.0 / (q_rows * ranks)
 
-    def add_group(s, carry):
-        queries = all_ref[s, :q_rows]
-
-        def add_items(t, partial):
-            scores = EXP_SCALE * contract_last(all_ref[t, q_rows : q_rows + i_rows], queries)
-            return partial + jnp.sum(jnp.exp2(scores).reshape(i_rows // 8, 8, q_rows), axis=0)
-
-        partial = lax.fori_loop(0, ranks, add_items, jnp.zeros((8, q_rows), F32), unroll=True)
-        totals_ref[s] = jnp.broadcast_to(jnp.sum(partial, axis=0, keepdims=True), (8, q_rows))
+    own_keys = all_ref[slot, q_rows : q_rows + i_rows]
+    own_queries = all_ref[slot, :q_rows]
+
+    def powers(left, right):
+        return jnp.exp2(EXP_SCALE * contract_last(left, right))
+
+    def fold(values):
+        return jnp.sum(values.reshape(values.shape[0] // 8, 8, values.shape[1]), axis=0)
+
+    own_sums = jnp.zeros((q_rows, LANES), F32)
+    for s in range(ranks):
+        by_item_ref[s] = powers(own_keys, all_ref[s, :q_rows])
+        totals_ref[s] = fold(by_item_ref[s])
+        by_query = powers(own_queries, all_ref[s, q_rows : q_rows + i_rows])
+        by_query_ref[s] = by_query
+        for i in range(0, i_rows, LANES):
+            own_sums = own_sums + by_query[:, i : i + LANES]
         digits = all_ref[s, q_rows + i_rows :].astype(F32)
         chunks = q_rows // LANES
         code = jnp.concatenate(
@@ -171,38 +179,32 @@
             axis=1,
         )
         codes_ref[s] = jnp.broadcast_to(code.astype(jnp.int32), (8, q_rows))
-        return carry
-
-    lax.fori_loop(0, ranks, add_group, 0, unroll=True)
-
-    own_keys = all_ref[slot, q_rows : q_rows + i_rows]
-
-    def add_queries(s, d_keys):
+
+    for j in range(1, ranks):
+        s = lax.rem(slot + j, ranks)
         queries = all_ref[s, :q_rows]
-        shares = jnp.exp2(EXP_SCALE * contract_last(own_keys, queries)) * (norm_c / totals_ref[s, :1])
-        item = item_start + lax.broadcasted_iota(jnp.int32, (i_rows, q_rows), 0)
-        weights = (shares - jnp.where(codes_ref[s, :1] == item, norm_c, 0.0)).astype(BF16)
-        return d_keys + jnp.dot(weights, queries, preferred_element_type=F32)
-
-
-    own_queries = all_ref[slot, :q_rows]
-    inverse = column_of(norm_c / totals_ref[slot, :1])
-    inverse = jnp.concatenate([inverse] * (i_rows // LANES), axis=1)
+        partial = totals_ref[s]
+        for i in range(1, ranks):
+            t = lax.rem(slot + i, ranks)
+            partial = partial + fold(powers(all_ref[t, q_rows : q_rows + i_rows], queries))
+        totals_ref[s] = jnp.broadcast_to(jnp.sum(partial, axis=0, keepdims=True), (8, q_rows))
+    own_total = jnp.broadcast_to(jnp.sum(own_sums, axis=1, keepdims=True), (q_rows, LANES))
+    totals_ref[slot] = jnp.transpose(own_total)[:8]
+
+    item = item_start + lax.broadcasted_iota(jnp.int32, (i_rows, q_rows), 0)
+    inverse = jnp.concatenate([norm_c / own_total] * (i_rows // LANES), axis=1)
     target = jnp.concatenate([column_of(pos_ref[...])] * (i_rows // LANES), axis=1)
     target = target - lax.broadcasted_iota(jnp.int32, (q_rows, i_rows), 1)
-
-    def add_keys(t, d_queries):
-        keys = all_ref[t, q_rows : q_rows + i_rows]
-        shares = jnp.exp2(EXP_SCALE * contract_last(own_queries, keys)) * inverse
-        weights = (shares - jnp.where(target == order[t] * i_rows, norm_c, 0.0)).astype(BF16)
-        return d_queries + jnp.dot(weights, keys, preferred_element_type=F32)
-
     d_keys = jnp.zeros((i_rows, LANES), F32)
     d_queries = jnp.zeros((q_rows, LANES), F32)
     for r in range(ranks):
-        d_keys = add_queries(r, d_keys)
-        d_queries = add_keys(r, d_queries)
-
+        shares = by_item_ref[r] * (norm_c / totals_ref[r, :1])
+        weights = (shares - jnp.where(codes_ref[r, :1] == item, norm_c, 0.0)).astype(BF16)
+        d_keys = d_keys + jnp.dot(weights, all_ref[r, :q_rows], preferred_element_type=F32)
+        shares = by_query_ref[r] * inverse
+        weights = (shares - jnp.where(target == order[r] * i_rows, norm_c, 0.0)).astype(BF16)
+        keys = all_ref[r, q_rows : q_rows + i_rows]
+        d_queries = d_queries + jnp.dot(weights, keys, preferred_element_type=F32)
     d_key_outer = outer_grad(LOGIT_SCALE * d_keys, outers_ref[1])
     d_query_outer = outer_grad(LOGIT_SCALE * d_queries, outers_ref[0])
     d_query_outer_ref[...] = d_query_outer
@@ -303,8 +305,8 @@
 
 
 def per_device(rows, state, bag_ids, bag_counts, item_feats, positives, q_w1, q_w2, i_w1, i_w2):
-    group = ("ya", "xl", "yb")
-    block = ("zp", "xh", "xl", "ya", "yb")
+    group = ("yb", "xl", "ya")
+    block = ("zp", "ya", "yb", "xh", "xl")
     strided = ("zb", "zc", "za")
     struct = jax.ShapeDtypeStruct
     ranks = lax.axis_size(group)
@@ -345,7 +347,12 @@
         [struct((q_rows, e), BF16), struct((2 * q_rows, e), BF16), struct((2 * q_rows, e), BF16)],
         [where, everyone, positives, outers, pooled, feats],
         in_specs=[SMEM] + [VMEM] * 5,
-        scratch=[pltpu.VMEM((ranks, 8, q_rows), F32), pltpu.VMEM((ranks, 8, q_rows), jnp.int32)],
+        scratch=[
+            pltpu.VMEM((ranks, 8, q_rows), F32),
+            pltpu.VMEM((ranks, 8, q_rows), jnp.int32),
+            pltpu.VMEM((ranks, i_rows, q_rows), F32),
+            pltpu.VMEM((ranks, q_rows, i_rows), F32),
+        ],
     )
     swap = [(0, 1), (1, 0)]
     received = lax.ppermute(send, "c", swap)

time: 102 us -> 102 us (level)
  no operation moved by 1% of the time
where the time goes in v7:
time: 102 us
  blocking collectives  74.4 us (73%)
  Pallas kernels  13.1 us (13%)
  starting transfers between devices  12.9 us (13%)
    all_to_all x4, blocking collectives, exchange(): return lax.all_to_all(values, axes, 0, 0, tiled=True)  74.4 us
    pallas_call x6, Pallas kernels, call(): pl.pallas_call(kernel, out_shape=out_shape, in_specs=in_specs or [VMEM] *...  13.1 us
    ppermute x1, starting transfers between devices, per_device(): received = lax.ppermute(send, 'c', swap)  6.47 us
    ppermute x1, starting transfers between devices, per_device(): other = lax.ppermute(tower, 'c', swap)  6.4 us
  transfers between devices with their start and end apart: 2, of which 0 were waited for; matrix products, arithmetic and copies ran while one was open for 0% of the time, Pallas kernels for 3%

profile of v7, /device:TPU:1, one launch (start us, length us, event | category | flops | bytes accessed | tf_op | source)
XLA Modules:
  0.0 101.6 jit_solution(1387083959418333808)
XLA Ops:
  0.6 0.1 pad_add_fusion.where_ref
  0.7 3.0 %shard_map.137 = (bf16[8,528,128]{2,1,0:T(8,128)(2,1)S(1)}, bf16[256,128]{1,0:T(8,128)(2,1)S(1)}, bf16[256,256]{1,0:T(8,128)(2,1)S(1)}, f32[2,256,128]{2,1,0:T(8,128)S(1)}) custom-call(s32[16,256]{1,0:T(8,128)} %bitcast.18, s32[1,256]{1,0:T(1,128)} %counts_ref.1, s32[1,256]{1,0:T(1,128)} %pos_ref.1, f32[256,128]{1,0:T(8,128)} %bitcast.16, ...), custom_call_target="tpu_custom_call" | custom-call | bytes 1048576 | tf_op jit(solution)/shard_map/pallas_call | solution.py:292
  3.7 0.0 copy-start.4
  3.7 0.0 copy-start.6
  3.7 18.6 %all_to_all.20.all_ref = bf16[8,528,128]{2,1,0:T(8,128)(2,1)S(1)} all-to-all(bf16[8,528,128]{2,1,0:T(8,128)(2,1)S(1)} %get-tuple-element.26), channel_id=1, replica_groups=mesh['ya'=2,'yb'=2,'xl'=2,'za'=2,'zb'=2,'zc'=2,'zp'=2,'xh'=2,'c'=2] {'yb..., dimensions={0} | all-to-all | bytes 2162688 | tf_op jit(solution)/shard_map/all_to_all | solution.py:304
  22.3 0.0 copy-start
  22.3 0.0 copy-start.1
  22.3 0.0 copy-start.2
  22.3 0.0 copy-start.3
  22.4 0.0 copy-done.4
  22.4 0.0 copy-done.6
  22.4 4.1 %shard_map.138 = (bf16[256,128]{1,0:T(8,128)(2,1)S(1)}, bf16[512,128]{1,0:T(8,128)(2,1)S(1)}, bf16[512,128]{1,0:T(8,128)(2,1)S(1)}) custom-call(s32[3]{0:T(128)S(1)} %pad_add_fusion.where_ref, bf16[8,528,128]{2,1,0:T(8,128)(2,1)S(1)} %all_to_all.20.all_ref, s32[1,256]{1,0:T(1,128)S(1)} %copy-done.6, f32[2,256,128]{2,1,0:T(8,128)S(1)} %get-tuple-element.27.outers_ref, ...), custom_call_target="tpu_custom_call" | custom-call | bytes 1048576 | tf_op jit(solution)/shard_map/pallas_call | solution.py:292
  26.5 6.5 %collective-permute-start = (bf16[512,128]{1,0:T(8,128)(2,1)S(1)}, bf16[512,128]{1,0:T(8,128)(2,1)S(1)}, u32[]{:S(2)}, u32[]{:S(2)}) collective-permute-start(bf16[512,128]{1,0:T(8,128)(2,1)S(1)} %get-tuple-element.30), channel_id=1, source_target_pairs={{0,1},{1,0},{2,3},{3,2},{4,5},{5,4},{6,7},{7,6},{8,9},{9,8},{10,11... | collective-permute-start | bytes 393224 | tf_op jit(solution)/shard_map/ppermute | solution.py:358
  33.0 0.0 copy-done
  33.0 0.0 copy-done.1
  33.0 0.0 copy-done.2
  33.0 0.0 copy-done.3
  33.0 1.1 %shard_map.140 = (bf16[1024,256]{1,0:T(8,128)(2,1)S(1)}, f32[256,1024]{1,0:T(8,128)S(1)}, bf16[128,1024]{1,0:T(8,128)(2,1)S(1)}, bf16[1024,128]{1,0:T(8,128)(2,1)S(1)}) custom-call(s32[3]{0:T(128)S(1)} %pad_add_fusion.where_ref, bf16[512,128]{1,0:T(8,128)(2,1)S(1)} %get-tuple-element.29.keep_ref, bf16[128,1024]{1,0:T(8,128)(2,1)S(1)} %copy-done.2, ...), custom_call_target="tpu_custom_call" | custom-call | flops 268435456 | bytes 1048576 | tf_op jit(solution)/shard_map/pallas_call | solution.py:292
  34.1 0.0 collective-permute-done.received_ref
  34.1 1.3 %shard_map.141 = bf16[2048,128]{1,0:T(8,128)(2,1)S(1)} custom-call(bf16[512,128]{1,0:T(8,128)(2,1)S(1)} %get-tuple-element.29.keep_ref, bf16[512,128]{1,0:T(8,128)(2,1)S(1)} %collective-permute-done.received_ref, bf16[1024,256]{1,0:T(8,128)(2,1)S(1)} %get-tuple-element.31.hidden_ref, f32[256,1024]{1,0:T(8,128)S(1)} %get-tuple-element.32.slope_ref, ...), custom_call_target="tpu_custom_call" | custom-call | bytes 1048576 | tf_op jit(solution)/shard_map/pallas_call | solution.py:292
  35.4 16.4 %all_to_all.21 = bf16[32,64,128]{2,1,0:T(8,128)(2,1)S(1)} all-to-all(bf16[32,64,128]{2,1,0:T(8,128)(2,1)S(1)} %bitcast.13), channel_id=1, replica_groups=mesh['ya'=2,'yb'=2,'xl'=2,'za'=2,'zb'=2,'zc'=2,'zp'=2,'xh'=2,'c'=2] {'zp..., dimensions={0} | all-to-all | bytes 1048576 | tf_op jit(solution)/shard_map/all_to_all | solution.py:304
  51.7 0.1 reduce_sum.24
  51.8 0.0 copy-start.5
  51.8 0.0 copy-start.7
  51.9 0.0 copy-start.8
  51.9 25.6 %all_to_all.22 = bf16[8,64,128]{2,1,0:T(8,128)(2,1)S(1)} all-to-all(bf16[8,64,128]{2,1,0:T(8,128)(2,1)S(1)} %broadcast_in_dim.10), channel_id=1, replica_groups=mesh['ya'=2,'yb'=2,'xl'=2,'za'=2,'zb'=2,'zc'=2,'zp'=2,'xh'=2,'c'=2] {'zb..., dimensions={0} | all-to-all | bytes 262144 | tf_op jit(solution)/shard_map/all_to_all | solution.py:304
  77.6 0.1 broadcast_in_dim.11
  77.7 13.8 %all_to_all.23 = bf16[32,64,128]{2,1,0:T(8,128)(2,1)S(1)} all-to-all(bf16[32,64,128]{2,1,0:T(8,128)(2,1)S(1)} %broadcast_in_dim.11), channel_id=1, replica_groups=mesh['ya'=2,'yb'=2,'xl'=2,'za'=2,'zb'=2,'zc'=2,'zp'=2,'xh'=2,'c'=2] {'zp..., dimensions={0} | all-to-all | bytes 1048576 | tf_op jit(solution)/shard_map/all_to_all | solution.py:304
  91.5 6.4 %collective-permute-start.1 = (bf16[2048,128]{1,0:T(8,128)(2,1)S(1)}, bf16[2048,128]{1,0:T(8,128)(2,1)S(1)}, u32[]{:S(2)}, u32[]{:S(2)}) collective-permute-start(bf16[2048,128]{1,0:T(8,128)(2,1)S(1)} %bitcast.11), channel_id=1, source_target_pairs={{0,1},{1,0},{2,3},{3,2},{4,5},{5,4},{6,7},{7,6},{8,9},{9,8},{10,11... | collective-permute-start | bytes 1572872 | tf_op jit(solution)/shard_map/ppermute | solution.py:379
  97.9 0.0 copy-done.5
  97.9 0.0 copy-done.7
  97.9 0.0 copy-done.8
  97.9 1.8 %shard_map.139 = f32[256,128]{1,0:T(8,128)} custom-call(bf16[256,256]{1,0:T(8,128)(2,1)S(1)} %get-tuple-element.22.tally_ref, s32[1,256]{1,0:T(1,128)S(1)} %copy-done.7, bf16[256,128]{1,0:T(8,128)(2,1)S(1)} %get-tuple-element.23.pooled_ref, bf16[256,128]{1,0:T(8,128)(2,1)S(1)} %get-tuple-element.28.d_outer_ref, bf16[128,1024]{1,0:T(8,128)(2,1)S(1)} %copy-done.2, ...), custom_call_target="tpu_custom_call" | custom-call | flops 1073741824 | bytes 1048576 | tf_op jit(solution)/shard_map/pallas_call | solution.py:292
  99.7 0.0 collective-permute-done.1.other_ref
  99.7 1.9 %shard_map.142 = (f32[128,1024]{1,0:T(8,128)}, f32[1024,128]{1,0:T(8,128)}, f32[128,1024]{1,0:T(8,128)}, f32[1024,128]{1,0:T(8,128)}) custom-call(s32[3]{0:T(128)S(1)} %pad_add_fusion.where_ref, bf16[2048,128]{1,0:T(8,128)(2,1)S(1)} %bitcast.12, bf16[2048,128]{1,0:T(8,128)(2,1)S(1)} %collective-permute-done.1.other_ref), custom_call_target="tpu_custom_call" | custom-call | bytes 1048576 | tf_op jit(solution)/shard_map/pallas_call | solution.py:292
  (2 shorter events, 0.0 us)
Async XLA Ops:
  3.7 18.7 %copy-start.4 = (bf16[1,256,128]{2,1,0:T(8,128)(2,1)S(1)}, bf16[1,256,128]{2,1,0:T(8,128)(2,1)}, u32[]{:S(2)}) copy-start(bf16[1,256,128]{2,1,0:T(8,128)(2,1)} %param.14) | copy-start | bytes 196612
  3.7 18.7 %copy-start.6 = (s32[1,256]{1,0:T(1,128)S(1)}, s32[1,256]{1,0:T(1,128)}, u32[]{:S(2)}) copy-start(s32[1,256]{1,0:T(1,128)} %pos_ref.1) | copy-start | bytes 3076
  22.3 10.6 %copy-start = (bf16[128,1024]{1,0:T(8,128)(2,1)S(1)}, bf16[128,1024]{1,0:T(8,128)(2,1)}, u32[]{:S(2)}) copy-start(bf16[128,1024]{1,0:T(8,128)(2,1)} %iw1_ref.1) | copy-start | bytes 786436
  22.3 10.6 %copy-start.1 = (bf16[1024,128]{1,0:T(8,128)(2,1)S(1)}, bf16[1024,128]{1,0:T(8,128)(2,1)}, u32[]{:S(2)}) copy-start(bf16[1024,128]{1,0:T(8,128)(2,1)} %iw2_ref.1) | copy-start | bytes 786436
  22.3 10.6 %copy-start.2 = (bf16[128,1024]{1,0:T(8,128)(2,1)S(1)}, bf16[128,1024]{1,0:T(8,128)(2,1)}, u32[]{:S(2)}) copy-start(bf16[128,1024]{1,0:T(8,128)(2,1)} %qw1_ref.3) | copy-start | bytes 786436
  22.3 10.7 %copy-start.3 = (bf16[1024,128]{1,0:T(8,128)(2,1)S(1)}, bf16[1024,128]{1,0:T(8,128)(2,1)}, u32[]{:S(2)}) copy-start(bf16[1024,128]{1,0:T(8,128)(2,1)} %qw2_ref.3) | copy-start | bytes 786436
  26.5 7.6 %collective-permute-start = (bf16[512,128]{1,0:T(8,128)(2,1)S(1)}, bf16[512,128]{1,0:T(8,128)(2,1)S(1)}, u32[]{:S(2)}, u32[]{:S(2)}) collective-permute-start(bf16[512,128]{1,0:T(8,128)(2,1)S(1)} %get-tuple-element.30), channel_id=1, source_target_pairs={{0,1},{1,0},{2,3},{3,2},{4,5},{5,4},{6,7},{7,6},{8,9},{9,8},{10,11... | collective-permute-start | bytes 393224 | tf_op jit(solution)/shard_map/ppermute | solution.py:358
  51.8 46.0 %copy-start.5 = (f32[1,256,128]{2,1,0:T(8,128)S(1)}, f32[1,256,128]{2,1,0:T(8,128)}, u32[]{:S(2)}) copy-start(f32[1,256,128]{2,1,0:T(8,128)} %param.10) | copy-start | bytes 393220
  51.8 46.0 %copy-start.7 = (s32[1,256]{1,0:T(1,128)S(1)}, s32[1,256]{1,0:T(1,128)}, u32[]{:S(2)}) copy-start(s32[1,256]{1,0:T(1,128)} %counts_ref.1) | copy-start | bytes 3076
  51.9 46.0 %copy-start.8 = (f32[1,256]{1,0:T(1,128)S(1)}, f32[1,256]{1,0:T(1,128)}, u32[]{:S(2)}) copy-start(f32[1,256]{1,0:T(1,128)} %state_ref.1) | copy-start | bytes 3076
  91.5 8.2 %collective-permute-start.1 = (bf16[2048,128]{1,0:T(8,128)(2,1)S(1)}, bf16[2048,128]{1,0:T(8,128)(2,1)S(1)}, u32[]{:S(2)}, u32[]{:S(2)}) collective-permute-start(bf16[2048,128]{1,0:T(8,128)(2,1)S(1)} %bitcast.11), channel_id=1, source_target_pairs={{0,1},{1,0},{2,3},{3,2},{4,5},{5,4},{6,7},{7,6},{8,9},{9,8},{10,11... | collective-permute-start | bytes 1572872 | tf_op jit(solution)/shard_map/ppermute | solution.py:379

commit v8 on v7

--- a/solution.py
+++ b/solution.py
@@ -62,6 +62,13 @@
     for copy in copies:
         copy.start()
 
+    def tower(inputs, first, second, slot):
+        pre = jnp.dot(inputs, targets[first][...], preferred_element_type=F32)
+        hidden = (pre * jax.nn.sigmoid(pre)).astype(BF16)
+        outer = jnp.dot(hidden, targets[second][...], preferred_element_type=F32)
+        outers_ref[slot] = outer
+        return (outer / radius_of(outer)).astype(BF16)
+
     members, q_rows = ids_ref.shape
     table_rows = table_ref.shape[0]
     copies[0].wait()
@@ -74,24 +81,14 @@
         tally = tally + jnp.where(live == rows, 1.0, 0.0)
     tally = tally.astype(BF16)
     tally_ref[...] = tally
-    copies[2].wait()
+    for copy in copies[2:]:
+        copy.wait()
+    keys = tower(feats_ref[...], 5, 7, 1)
     product = contract_lead(tally, three_pieces(table_ref[...]))
     pooled = (add_pieces(product) / column_of(counts.astype(F32))).astype(BF16)
     pooled_ref[...] = pooled
 
-    def tower(inputs, first, second, slot):
-        copies[first].wait()
-        pre = jnp.dot(inputs, targets[first][...], preferred_element_type=F32)
-        hidden = (pre * jax.nn.sigmoid(pre)).astype(BF16)
-        copies[second].wait()
-        outer = jnp.dot(hidden, targets[second][...], preferred_element_type=F32)
-        outers_ref[slot] = outer
-        return (outer / radius_of(outer)).astype(BF16)
-
     queries = tower(pooled, 3, 6, 0)
-    copies[4].wait()
-    keys = tower(feats_ref[...], 5, 7, 1)
-    copies[8].wait()
     pos = pos_ref[...]
     digits = jnp.concatenate([pos // LANES, pos % LANES], axis=0).astype(F32)
     spread = jnp.concatenate(

time: 102 us -> 101 us (level)
  no operation moved by 1% of the time
where the time goes in v8:
time: 101 us
  blocking collectives  74.4 us (74%)
  starting transfers between devices  12.9 us (13%)
  Pallas kernels  12.5 us (12%)
    all_to_all x4, blocking collectives, exchange(): return lax.all_to_all(values, axes, 0, 0, tiled=True)  74.4 us
    pallas_call x6, Pallas kernels, call(): pl.pallas_call(kernel, out_shape=out_shape, in_specs=in_specs or [VMEM] *...  12.5 us
    ppermute x1, starting transfers between devices, per_device(): received = lax.ppermute(send, 'c', swap)  6.47 us
    ppermute x1, starting transfers between devices, per_device(): other = lax.ppermute(tower, 'c', swap)  6.42 us
  transfers between devices with their start and end apart: 2, of which 0 were waited for; matrix products, arithmetic and copies ran while one was open for 0% of the time, Pallas kernels for 3%

profile of v8, /device:TPU:1, one launch (start us, length us, event | category | flops | bytes accessed | tf_op | source)
XLA Modules:
  0.0 101.0 jit_solution(4302968969417784299)
XLA Ops:
  0.6 0.1 pad_add_fusion.where_ref
  0.7 2.4 %shard_map.137 = (bf16[8,528,128]{2,1,0:T(8,128)(2,1)S(1)}, bf16[256,128]{1,0:T(8,128)(2,1)S(1)}, bf16[256,256]{1,0:T(8,128)(2,1)S(1)}, f32[2,256,128]{2,1,0:T(8,128)S(1)}) custom-call(s32[16,256]{1,0:T(8,128)} %bitcast.18, s32[1,256]{1,0:T(1,128)} %counts_ref.1, s32[1,256]{1,0:T(1,128)} %pos_ref.1, f32[256,128]{1,0:T(8,128)} %bitcast.16, ...), custom_call_target="tpu_custom_call" | custom-call | bytes 1048576 | tf_op jit(solution)/shard_map/pallas_call | solution.py:289
  3.1 0.0 copy-start.4
  3.1 0.0 copy-start.6
  3.1 18.6 %all_to_all.20.all_ref = bf16[8,528,128]{2,1,0:T(8,128)(2,1)S(1)} all-to-all(bf16[8,528,128]{2,1,0:T(8,128)(2,1)S(1)} %get-tuple-element.26), channel_id=1, replica_groups=mesh['ya'=2,'yb'=2,'xl'=2,'za'=2,'zb'=2,'zc'=2,'zp'=2,'xh'=2,'c'=2] {'yb..., dimensions={0} | all-to-all | bytes 2162688 | tf_op jit(solution)/shard_map/all_to_all | solution.py:301
  21.7 0.0 copy-start
  21.7 0.0 copy-start.1
  21.7 0.0 copy-start.2
  21.7 0.0 copy-start.3
  21.7 0.0 copy-done.4
  21.7 0.0 copy-done.6
  21.7 4.1 %shard_map.138 = (bf16[256,128]{1,0:T(8,128)(2,1)S(1)}, bf16[512,128]{1,0:T(8,128)(2,1)S(1)}, bf16[512,128]{1,0:T(8,128)(2,1)S(1)}) custom-call(s32[3]{0:T(128)S(1)} %pad_add_fusion.where_ref, bf16[8,528,128]{2,1,0:T(8,128)(2,1)S(1)} %all_to_all.20.all_ref, s32[1,256]{1,0:T(1,128)S(1)} %copy-done.6, f32[2,256,128]{2,1,0:T(8,128)S(1)} %get-tuple-element.27.outers_ref, ...), custom_call_target="tpu_custom_call" | custom-call | bytes 1048576 | tf_op jit(solution)/shard_map/pallas_call | solution.py:289
  25.9 6.5 %collective-permute-start = (bf16[512,128]{1,0:T(8,128)(2,1)S(1)}, bf16[512,128]{1,0:T(8,128)(2,1)S(1)}, u32[]{:S(2)}, u32[]{:S(2)}) collective-permute-start(bf16[512,128]{1,0:T(8,128)(2,1)S(1)} %get-tuple-element.30), channel_id=1, source_target_pairs={{0,1},{1,0},{2,3},{3,2},{4,5},{5,4},{6,7},{7,6},{8,9},{9,8},{10,11... | collective-permute-start | bytes 393224 | tf_op jit(solution)/shard_map/ppermute | solution.py:355
  32.3 0.0 copy-done
  32.4 0.0 copy-done.1
  32.4 0.0 copy-done.2
  32.4 0.0 copy-done.3
  32.4 1.1 %shard_map.140 = (bf16[1024,256]{1,0:T(8,128)(2,1)S(1)}, f32[256,1024]{1,0:T(8,128)S(1)}, bf16[128,1024]{1,0:T(8,128)(2,1)S(1)}, bf16[1024,128]{1,0:T(8,128)(2,1)S(1)}) custom-call(s32[3]{0:T(128)S(1)} %pad_add_fusion.where_ref, bf16[512,128]{1,0:T(8,128)(2,1)S(1)} %get-tuple-element.29.keep_ref, bf16[128,1024]{1,0:T(8,128)(2,1)S(1)} %copy-done.2, ...), custom_call_target="tpu_custom_call" | custom-call | flops 268435456 | bytes 1048576 | tf_op jit(solution)/shard_map/pallas_call | solution.py:289
  33.5 0.0 collective-permute-done.received_ref
  33.5 1.3 %shard_map.141 = bf16[2048,128]{1,0:T(8,128)(2,1)S(1)} custom-call(bf16[512,128]{1,0:T(8,128)(2,1)S(1)} %get-tuple-element.29.keep_ref, bf16[512,128]{1,0:T(8,128)(2,1)S(1)} %collective-permute-done.received_ref, bf16[1024,256]{1,0:T(8,128)(2,1)S(1)} %get-tuple-element.31.hidden_ref, f32[256,1024]{1,0:T(8,128)S(1)} %get-tuple-element.32.slope_ref, ...), custom_call_target="tpu_custom_call" | custom-call | bytes 1048576 | tf_op jit(solution)/shard_map/pallas_call | solution.py:289
  34.8 16.4 %all_to_all.21 = bf16[32,64,128]{2,1,0:T(8,128)(2,1)S(1)} all-to-all(bf16[32,64,128]{2,1,0:T(8,128)(2,1)S(1)} %bitcast.13), channel_id=1, replica_groups=mesh['ya'=2,'yb'=2,'xl'=2,'za'=2,'zb'=2,'zc'=2,'zp'=2,'xh'=2,'c'=2] {'zp..., dimensions={0} | all-to-all | bytes 1048576 | tf_op jit(solution)/shard_map/all_to_all | solution.py:301
  51.1 0.1 reduce_sum.24
  51.2 0.0 copy-start.5
  51.2 0.0 copy-start.7
  51.2 0.0 copy-start.8
  51.3 25.6 %all_to_all.22 = bf16[8,64,128]{2,1,0:T(8,128)(2,1)S(1)} all-to-all(bf16[8,64,128]{2,1,0:T(8,128)(2,1)S(1)} %broadcast_in_dim.10), channel_id=1, replica_groups=mesh['ya'=2,'yb'=2,'xl'=2,'za'=2,'zb'=2,'zc'=2,'zp'=2,'xh'=2,'c'=2] {'zb..., dimensions={0} | all-to-all | bytes 262144 | tf_op jit(solution)/shard_map/all_to_all | solution.py:301
  76.9 0.1 broadcast_in_dim.11
  77.1 13.8 %all_to_all.23 = bf16[32,64,128]{2,1,0:T(8,128)(2,1)S(1)} all-to-all(bf16[32,64,128]{2,1,0:T(8,128)(2,1)S(1)} %broadcast_in_dim.11), channel_id=1, replica_groups=mesh['ya'=2,'yb'=2,'xl'=2,'za'=2,'zb'=2,'zc'=2,'zp'=2,'xh'=2,'c'=2] {'zp..., dimensions={0} | all-to-all | bytes 1048576 | tf_op jit(solution)/shard_map/all_to_all | solution.py:301
  90.8 6.4 %collective-permute-start.1 = (bf16[2048,128]{1,0:T(8,128)(2,1)S(1)}, bf16[2048,128]{1,0:T(8,128)(2,1)S(1)}, u32[]{:S(2)}, u32[]{:S(2)}) collective-permute-start(bf16[2048,128]{1,0:T(8,128)(2,1)S(1)} %bitcast.11), channel_id=1, source_target_pairs={{0,1},{1,0},{2,3},{3,2},{4,5},{5,4},{6,7},{7,6},{8,9},{9,8},{10,11... | collective-permute-start | bytes 1572872 | tf_op jit(solution)/shard_map/ppermute | solution.py:376
  97.3 0.0 copy-done.5
  97.3 0.0 copy-done.7
  97.3 0.0 copy-done.8
  97.3 1.8 %shard_map.139 = f32[256,128]{1,0:T(8,128)} custom-call(bf16[256,256]{1,0:T(8,128)(2,1)S(1)} %get-tuple-element.22.tally_ref, s32[1,256]{1,0:T(1,128)S(1)} %copy-done.7, bf16[256,128]{1,0:T(8,128)(2,1)S(1)} %get-tuple-element.23.pooled_ref, bf16[256,128]{1,0:T(8,128)(2,1)S(1)} %get-tuple-element.28.d_outer_ref, bf16[128,1024]{1,0:T(8,128)(2,1)S(1)} %copy-done.2, ...), custom_call_target="tpu_custom_call" | custom-call | flops 1073741824 | bytes 1048576 | tf_op jit(solution)/shard_map/pallas_call | solution.py:289
  99.1 0.0 collective-permute-done.1.other_ref
  99.1 1.9 %shard_map.142 = (f32[128,1024]{1,0:T(8,128)}, f32[1024,128]{1,0:T(8,128)}, f32[128,1024]{1,0:T(8,128)}, f32[1024,128]{1,0:T(8,128)}) custom-call(s32[3]{0:T(128)S(1)} %pad_add_fusion.where_ref, bf16[2048,128]{1,0:T(8,128)(2,1)S(1)} %bitcast.12, bf16[2048,128]{1,0:T(8,128)(2,1)S(1)} %collective-permute-done.1.other_ref), custom_call_target="tpu_custom_call" | custom-call | bytes 1048576 | tf_op jit(solution)/shard_map/pallas_call | solution.py:289
  (2 shorter events, 0.0 us)
Async XLA Ops:
  3.1 18.6 %copy-start.4 = (bf16[1,256,128]{2,1,0:T(8,128)(2,1)S(1)}, bf16[1,256,128]{2,1,0:T(8,128)(2,1)}, u32[]{:S(2)}) copy-start(bf16[1,256,128]{2,1,0:T(8,128)(2,1)} %param.14) | copy-start | bytes 196612
  3.1 18.6 %copy-start.6 = (s32[1,256]{1,0:T(1,128)S(1)}, s32[1,256]{1,0:T(1,128)}, u32[]{:S(2)}) copy-start(s32[1,256]{1,0:T(1,128)} %pos_ref.1) | copy-start | bytes 3076
  21.7 10.6 %copy-start = (bf16[128,1024]{1,0:T(8,128)(2,1)S(1)}, bf16[128,1024]{1,0:T(8,128)(2,1)}, u32[]{:S(2)}) copy-start(bf16[128,1024]{1,0:T(8,128)(2,1)} %iw1_ref.1) | copy-start | bytes 786436
  21.7 10.6 %copy-start.1 = (bf16[1024,128]{1,0:T(8,128)(2,1)S(1)}, bf16[1024,128]{1,0:T(8,128)(2,1)}, u32[]{:S(2)}) copy-start(bf16[1024,128]{1,0:T(8,128)(2,1)} %iw2_ref.1) | copy-start | bytes 786436
  21.7 10.6 %copy-start.2 = (bf16[128,1024]{1,0:T(8,128)(2,1)S(1)}, bf16[128,1024]{1,0:T(8,128)(2,1)}, u32[]{:S(2)}) copy-start(bf16[128,1024]{1,0:T(8,128)(2,1)} %qw1_ref.3) | copy-start | bytes 786436
  21.7 10.7 %copy-start.3 = (bf16[1024,128]{1,0:T(8,128)(2,1)S(1)}, bf16[1024,128]{1,0:T(8,128)(2,1)}, u32[]{:S(2)}) copy-start(bf16[1024,128]{1,0:T(8,128)(2,1)} %qw2_ref.3) | copy-start | bytes 786436
  25.9 7.6 %collective-permute-start = (bf16[512,128]{1,0:T(8,128)(2,1)S(1)}, bf16[512,128]{1,0:T(8,128)(2,1)S(1)}, u32[]{:S(2)}, u32[]{:S(2)}) collective-permute-start(bf16[512,128]{1,0:T(8,128)(2,1)S(1)} %get-tuple-element.30), channel_id=1, source_target_pairs={{0,1},{1,0},{2,3},{3,2},{4,5},{5,4},{6,7},{7,6},{8,9},{9,8},{10,11... | collective-permute-start | bytes 393224 | tf_op jit(solution)/shard_map/ppermute | solution.py:355
  51.2 46.1 %copy-start.5 = (f32[1,256,128]{2,1,0:T(8,128)S(1)}, f32[1,256,128]{2,1,0:T(8,128)}, u32[]{:S(2)}) copy-start(f32[1,256,128]{2,1,0:T(8,128)} %param.10) | copy-start | bytes 393220
  51.2 46.1 %copy-start.7 = (s32[1,256]{1,0:T(1,128)S(1)}, s32[1,256]{1,0:T(1,128)}, u32[]{:S(2)}) copy-start(s32[1,256]{1,0:T(1,128)} %counts_ref.1) | copy-start | bytes 3076
  51.2 46.1 %copy-start.8 = (f32[1,256]{1,0:T(1,128)S(1)}, f32[1,256]{1,0:T(1,128)}, u32[]{:S(2)}) copy-start(f32[1,256]{1,0:T(1,128)} %state_ref.1) | copy-start | bytes 3076
  90.8 8.2 %collective-permute-start.1 = (bf16[2048,128]{1,0:T(8,128)(2,1)S(1)}, bf16[2048,128]{1,0:T(8,128)(2,1)S(1)}, u32[]{:S(2)}, u32[]{:S(2)}) collective-permute-start(bf16[2048,128]{1,0:T(8,128)(2,1)S(1)} %bitcast.11), channel_id=1, source_target_pairs={{0,1},{1,0},{2,3},{3,2},{4,5},{5,4},{6,7},{7,6},{8,9},{9,8},{10,11... | collective-permute-start | bytes 1572872 | tf_op jit(solution)/shard_map/ppermute | solution.py:376

commit v9 on v8

--- a/solution.py
+++ b/solution.py
@@ -243,11 +243,11 @@
     d_pre = (d_hidden * (sigma * (1.0 + pre * (1.0 - sigma)))).astype(BF16)
     d_x = contract_last(d_pre, qw1_ref[...])
     counts = column_of(counts_ref[...].astype(F32))
-    pieces = three_pieces(d_x / counts)
+    pieces = three_pieces(d_x * (1.0 / counts))
     row_grads = add_pieces(jnp.dot(tally_ref[...], pieces, preferred_element_type=F32))
     mean = jnp.mean(row_grads * row_grads, axis=1, keepdims=True)
     acc = column_of(state_ref[...]) + mean
-    new_ref[...] = table_ref[...] - LEARNING_RATE * row_grads / jnp.sqrt(acc)
+    new_ref[...] = table_ref[...] - row_grads * (LEARNING_RATE * lax.rsqrt(acc))
 
 
 def finish_kernel(

time: 101 us -> 101 us (level)
  no operation moved by 1% of the time
where the time goes in v9:
time: 101 us
  blocking collectives  74.4 us (74%)
  starting transfers between devices  12.9 us (13%)
  Pallas kernels  12.5 us (12%)
    all_to_all x4, blocking collectives, exchange(): return lax.all_to_all(values, axes, 0, 0, tiled=True)  74.4 us
    pallas_call x6, Pallas kernels, call(): pl.pallas_call(kernel, out_shape=out_shape, in_specs=in_specs or [VMEM] *...  12.5 us
    ppermute x1, starting transfers between devices, per_device(): received = lax.ppermute(send, 'c', swap)  6.47 us
    ppermute x1, starting transfers between devices, per_device(): other = lax.ppermute(tower, 'c', swap)  6.42 us
  transfers between devices with their start and end apart: 2, of which 0 were waited for; matrix products, arithmetic and copies ran while one was open for 0% of the time, Pallas kernels for 3%

profile of v9, /device:TPU:1, one launch (start us, length us, event | category | flops | bytes accessed | tf_op | source)
XLA Modules:
  0.0 101.0 jit_solution(14976050273257841868)
XLA Ops:
  0.6 0.1 pad_add_fusion.where_ref
  0.7 2.4 %shard_map.137 = (bf16[8,528,128]{2,1,0:T(8,128)(2,1)S(1)}, bf16[256,128]{1,0:T(8,128)(2,1)S(1)}, bf16[256,256]{1,0:T(8,128)(2,1)S(1)}, f32[2,256,128]{2,1,0:T(8,128)S(1)}) custom-call(s32[16,256]{1,0:T(8,128)} %bitcast.18, s32[1,256]{1,0:T(1,128)} %counts_ref.1, s32[1,256]{1,0:T(1,128)} %pos_ref.1, f32[256,128]{1,0:T(8,128)} %bitcast.16, ...), custom_call_target="tpu_custom_call" | custom-call | bytes 1048576 | tf_op jit(solution)/shard_map/pallas_call | solution.py:289
  3.1 0.0 copy-start.4
  3.1 0.0 copy-start.6
  3.1 18.6 %all_to_all.20.all_ref = bf16[8,528,128]{2,1,0:T(8,128)(2,1)S(1)} all-to-all(bf16[8,528,128]{2,1,0:T(8,128)(2,1)S(1)} %get-tuple-element.26), channel_id=1, replica_groups=mesh['ya'=2,'yb'=2,'xl'=2,'za'=2,'zb'=2,'zc'=2,'zp'=2,'xh'=2,'c'=2] {'yb..., dimensions={0} | all-to-all | bytes 2162688 | tf_op jit(solution)/shard_map/all_to_all | solution.py:301
  21.7 0.0 copy-start
  21.7 0.0 copy-start.1
  21.7 0.0 copy-start.2
  21.7 0.0 copy-start.3
  21.7 0.0 copy-done.4
  21.7 0.0 copy-done.6
  21.7 4.1 %shard_map.138 = (bf16[256,128]{1,0:T(8,128)(2,1)S(1)}, bf16[512,128]{1,0:T(8,128)(2,1)S(1)}, bf16[512,128]{1,0:T(8,128)(2,1)S(1)}) custom-call(s32[3]{0:T(128)S(1)} %pad_add_fusion.where_ref, bf16[8,528,128]{2,1,0:T(8,128)(2,1)S(1)} %all_to_all.20.all_ref, s32[1,256]{1,0:T(1,128)S(1)} %copy-done.6, f32[2,256,128]{2,1,0:T(8,128)S(1)} %get-tuple-element.27.outers_ref, ...), custom_call_target="tpu_custom_call" | custom-call | bytes 1048576 | tf_op jit(solution)/shard_map/pallas_call | solution.py:289
  25.9 6.5 %collective-permute-start = (bf16[512,128]{1,0:T(8,128)(2,1)S(1)}, bf16[512,128]{1,0:T(8,128)(2,1)S(1)}, u32[]{:S(2)}, u32[]{:S(2)}) collective-permute-start(bf16[512,128]{1,0:T(8,128)(2,1)S(1)} %get-tuple-element.30), channel_id=1, source_target_pairs={{0,1},{1,0},{2,3},{3,2},{4,5},{5,4},{6,7},{7,6},{8,9},{9,8},{10,11... | collective-permute-start | bytes 393224 | tf_op jit(solution)/shard_map/ppermute | solution.py:355
  32.3 0.0 copy-done
  32.4 0.0 copy-done.1
  32.4 0.0 copy-done.2
  32.4 0.0 copy-done.3
  32.4 1.1 %shard_map.140 = (bf16[1024,256]{1,0:T(8,128)(2,1)S(1)}, f32[256,1024]{1,0:T(8,128)S(1)}, bf16[128,1024]{1,0:T(8,128)(2,1)S(1)}, bf16[1024,128]{1,0:T(8,128)(2,1)S(1)}) custom-call(s32[3]{0:T(128)S(1)} %pad_add_fusion.where_ref, bf16[512,128]{1,0:T(8,128)(2,1)S(1)} %get-tuple-element.29.keep_ref, bf16[128,1024]{1,0:T(8,128)(2,1)S(1)} %copy-done.2, ...), custom_call_target="tpu_custom_call" | custom-call | flops 268435456 | bytes 1048576 | tf_op jit(solution)/shard_map/pallas_call | solution.py:289
  33.5 0.0 collective-permute-done.received_ref
  33.5 1.3 %shard_map.141 = bf16[2048,128]{1,0:T(8,128)(2,1)S(1)} custom-call(bf16[512,128]{1,0:T(8,128)(2,1)S(1)} %get-tuple-element.29.keep_ref, bf16[512,128]{1,0:T(8,128)(2,1)S(1)} %collective-permute-done.received_ref, bf16[1024,256]{1,0:T(8,128)(2,1)S(1)} %get-tuple-element.31.hidden_ref, f32[256,1024]{1,0:T(8,128)S(1)} %get-tuple-element.32.slope_ref, ...), custom_call_target="tpu_custom_call" | custom-call | bytes 1048576 | tf_op jit(solution)/shard_map/pallas_call | solution.py:289
  34.8 16.4 %all_to_all.21 = bf16[32,64,128]{2,1,0:T(8,128)(2,1)S(1)} all-to-all(bf16[32,64,128]{2,1,0:T(8,128)(2,1)S(1)} %bitcast.13), channel_id=1, replica_groups=mesh['ya'=2,'yb'=2,'xl'=2,'za'=2,'zb'=2,'zc'=2,'zp'=2,'xh'=2,'c'=2] {'zp..., dimensions={0} | all-to-all | bytes 1048576 | tf_op jit(solution)/shard_map/all_to_all | solution.py:301
  51.1 0.1 reduce_sum.24
  51.2 0.0 copy-start.5
  51.2 0.0 copy-start.7
  51.2 0.0 copy-start.8
  51.3 25.6 %all_to_all.22 = bf16[8,64,128]{2,1,0:T(8,128)(2,1)S(1)} all-to-all(bf16[8,64,128]{2,1,0:T(8,128)(2,1)S(1)} %broadcast_in_dim.10), channel_id=1, replica_groups=mesh['ya'=2,'yb'=2,'xl'=2,'za'=2,'zb'=2,'zc'=2,'zp'=2,'xh'=2,'c'=2] {'zb..., dimensions={0} | all-to-all | bytes 262144 | tf_op jit(solution)/shard_map/all_to_all | solution.py:301
  76.9 0.1 broadcast_in_dim.11
  77.1 13.8 %all_to_all.23 = bf16[32,64,128]{2,1,0:T(8,128)(2,1)S(1)} all-to-all(bf16[32,64,128]{2,1,0:T(8,128)(2,1)S(1)} %broadcast_in_dim.11), channel_id=1, replica_groups=mesh['ya'=2,'yb'=2,'xl'=2,'za'=2,'zb'=2,'zc'=2,'zp'=2,'xh'=2,'c'=2] {'zp..., dimensions={0} | all-to-all | bytes 1048576 | tf_op jit(solution)/shard_map/all_to_all | solution.py:301
  90.8 6.4 %collective-permute-start.1 = (bf16[2048,128]{1,0:T(8,128)(2,1)S(1)}, bf16[2048,128]{1,0:T(8,128)(2,1)S(1)}, u32[]{:S(2)}, u32[]{:S(2)}) collective-permute-start(bf16[2048,128]{1,0:T(8,128)(2,1)S(1)} %bitcast.11), channel_id=1, source_target_pairs={{0,1},{1,0},{2,3},{3,2},{4,5},{5,4},{6,7},{7,6},{8,9},{9,8},{10,11... | collective-permute-start | bytes 1572872 | tf_op jit(solution)/shard_map/ppermute | solution.py:376
  97.3 0.0 copy-done.5
  97.3 0.0 copy-done.7
  97.3 0.0 copy-done.8
  97.3 1.7 %shard_map.139 = f32[256,128]{1,0:T(8,128)} custom-call(bf16[256,256]{1,0:T(8,128)(2,1)S(1)} %get-tuple-element.22.tally_ref, s32[1,256]{1,0:T(1,128)S(1)} %copy-done.7, bf16[256,128]{1,0:T(8,128)(2,1)S(1)} %get-tuple-element.23.pooled_ref, bf16[256,128]{1,0:T(8,128)(2,1)S(1)} %get-tuple-element.28.d_outer_ref, bf16[128,1024]{1,0:T(8,128)(2,1)S(1)} %copy-done.2, ...), custom_call_target="tpu_custom_call" | custom-call | flops 1073741824 | bytes 1048576 | tf_op jit(solution)/shard_map/pallas_call | solution.py:289
  99.0 0.0 collective-permute-done.1.other_ref
  99.0 1.9 %shard_map.142 = (f32[128,1024]{1,0:T(8,128)}, f32[1024,128]{1,0:T(8,128)}, f32[128,1024]{1,0:T(8,128)}, f32[1024,128]{1,0:T(8,128)}) custom-call(s32[3]{0:T(128)S(1)} %pad_add_fusion.where_ref, bf16[2048,128]{1,0:T(8,128)(2,1)S(1)} %bitcast.12, bf16[2048,128]{1,0:T(8,128)(2,1)S(1)} %collective-permute-done.1.other_ref), custom_call_target="tpu_custom_call" | custom-call | bytes 1048576 | tf_op jit(solution)/shard_map/pallas_call | solution.py:289
  (2 shorter events, 0.0 us)
Async XLA Ops:
  3.1 18.6 %copy-start.4 = (bf16[1,256,128]{2,1,0:T(8,128)(2,1)S(1)}, bf16[1,256,128]{2,1,0:T(8,128)(2,1)}, u32[]{:S(2)}) copy-start(bf16[1,256,128]{2,1,0:T(8,128)(2,1)} %param.14) | copy-start | bytes 196612
  3.1 18.6 %copy-start.6 = (s32[1,256]{1,0:T(1,128)S(1)}, s32[1,256]{1,0:T(1,128)}, u32[]{:S(2)}) copy-start(s32[1,256]{1,0:T(1,128)} %pos_ref.1) | copy-start | bytes 3076
  21.7 10.6 %copy-start = (bf16[128,1024]{1,0:T(8,128)(2,1)S(1)}, bf16[128,1024]{1,0:T(8,128)(2,1)}, u32[]{:S(2)}) copy-start(bf16[128,1024]{1,0:T(8,128)(2,1)} %iw1_ref.1) | copy-start | bytes 786436
  21.7 10.6 %copy-start.1 = (bf16[1024,128]{1,0:T(8,128)(2,1)S(1)}, bf16[1024,128]{1,0:T(8,128)(2,1)}, u32[]{:S(2)}) copy-start(bf16[1024,128]{1,0:T(8,128)(2,1)} %iw2_ref.1) | copy-start | bytes 786436
  21.7 10.6 %copy-start.2 = (bf16[128,1024]{1,0:T(8,128)(2,1)S(1)}, bf16[128,1024]{1,0:T(8,128)(2,1)}, u32[]{:S(2)}) copy-start(bf16[128,1024]{1,0:T(8,128)(2,1)} %qw1_ref.3) | copy-start | bytes 786436
  21.7 10.7 %copy-start.3 = (bf16[1024,128]{1,0:T(8,128)(2,1)S(1)}, bf16[1024,128]{1,0:T(8,128)(2,1)}, u32[]{:S(2)}) copy-start(bf16[1024,128]{1,0:T(8,128)(2,1)} %qw2_ref.3) | copy-start | bytes 786436
  25.9 7.6 %collective-permute-start = (bf16[512,128]{1,0:T(8,128)(2,1)S(1)}, bf16[512,128]{1,0:T(8,128)(2,1)S(1)}, u32[]{:S(2)}, u32[]{:S(2)}) collective-permute-start(bf16[512,128]{1,0:T(8,128)(2,1)S(1)} %get-tuple-element.30), channel_id=1, source_target_pairs={{0,1},{1,0},{2,3},{3,2},{4,5},{5,4},{6,7},{7,6},{8,9},{9,8},{10,11... | collective-permute-start | bytes 393224 | tf_op jit(solution)/shard_map/ppermute | solution.py:355
  51.2 46.1 %copy-start.5 = (f32[1,256,128]{2,1,0:T(8,128)S(1)}, f32[1,256,128]{2,1,0:T(8,128)}, u32[]{:S(2)}) copy-start(f32[1,256,128]{2,1,0:T(8,128)} %param.10) | copy-start | bytes 393220
  51.2 46.1 %copy-start.7 = (s32[1,256]{1,0:T(1,128)S(1)}, s32[1,256]{1,0:T(1,128)}, u32[]{:S(2)}) copy-start(s32[1,256]{1,0:T(1,128)} %counts_ref.1) | copy-start | bytes 3076
  51.2 46.1 %copy-start.8 = (f32[1,256]{1,0:T(1,128)S(1)}, f32[1,256]{1,0:T(1,128)}, u32[]{:S(2)}) copy-start(f32[1,256]{1,0:T(1,128)} %state_ref.1) | copy-start | bytes 3076
  90.8 8.2 %collective-permute-start.1 = (bf16[2048,128]{1,0:T(8,128)(2,1)S(1)}, bf16[2048,128]{1,0:T(8,128)(2,1)S(1)}, u32[]{:S(2)}, u32[]{:S(2)}) collective-permute-start(bf16[2048,128]{1,0:T(8,128)(2,1)S(1)} %bitcast.11), channel_id=1, source_target_pairs={{0,1},{1,0},{2,3},{3,2},{4,5},{5,4},{6,7},{7,6},{8,9},{9,8},{10,11... | collective-permute-start | bytes 1572872 | tf_op jit(solution)/shard_map/ppermute | solution.py:376
